TPU v7x, 128 devices: a whole 4x4x4 slice. The times are simulated.
128 devices in a mesh: src: 4 (over x), rcv: 32 (over z, y, core).
Axes of the slice: x: 4, y: 4, z: 4, core: 2. Of those that a mesh axis runs over, the one named last changes fastest.
Arguments:
- traces: bfloat16 [4096, 512], P('rcv'), may hold values from -6 to 6
- band_group: int32 [4096], P('rcv'), may hold values from 0 to 23
- filters: float32 [24, 32], replicated, may hold values from -1 to 1
- pair_bin: int32 [2, 512, 4096], P(None, 'src', 'rcv'), may hold values from 0 to 1023, as said below
- bin_order: int32 [1024], replicated, may hold values from 0 to 1023, each once
Outputs:
- bin_stacks: float32 [1024, 512], P(('src', 'rcv'))
Inputs may be any that keep to these rules, and one draw needn't show every extreme that they name: pair_bin[k, p, c] is the distance along the fiber between the source channel of row p at step k and channel c, in bins of 4 channel spacings, where the spacing between neighbouring channels varies by up to a half; every bin number appears; for one step, one block of 128 source rows and one block of 128 receiver channels, the bins lie within 66 consecutive values.
All inputs are finite; a program needn't handle non-finite values.
Results may differ from a plain program's by a relative error of at most 0.0037.
Values may be sent and summed in bfloat16 or wider, within the bound.
No kernel may reach another device: no remote copies, remote signals or barrier semaphores. Data moves between devices by JAX's collectives and lax.ppermute only.
A program may use at most 256 MiB of HBM per device.

v0:
```python
import jax
import jax.numpy as jnp
from jax import lax
from jax.sharding import PartitionSpec as P

LAGS = 512
LAGBLK = 128
BANDS = 24
TAPS = 32
STEPS = 2
BINS_DEV = 8


def from_root(value, axis, root):
    mine = lax.axis_index(axis) == root
    return lax.psum(jnp.where(mine, value, jnp.zeros_like(value)), axis)


def prefilter(traces, band_group, filters):
    onehot = (band_group[:, None] == jnp.arange(BANDS, dtype=jnp.int32)[None, :]).astype(
        jnp.float32
    )
    taps = jnp.dot(onehot, filters, precision=lax.Precision.HIGHEST)
    signal = traces.astype(jnp.float32)
    padded = jnp.pad(signal, ((0, 0), (TAPS - 1, 0)))
    length = signal.shape[1]
    output = jnp.zeros_like(signal)
    for step in range(TAPS):
        output = (
            output
            + taps[:, step : step + 1] * padded[:, TAPS - 1 - step : TAPS - 1 - step + length]
        )
    scale = lax.rsqrt(jnp.mean(output * output, axis=1, keepdims=True) + 1e-06)
    return (output * scale).astype(jnp.bfloat16)


def hankel_rows(window):
    rows, width = window.shape
    half = width // 2
    tiled = jnp.tile(window, (1, half))
    tiled = jnp.pad(tiled, ((0, 0), (0, half)))
    return tiled.reshape(rows, half, width + 1)[:, :, :half]


def build_hankel(receivers):
    rows, length = receivers.shape
    padded = jnp.pad(receivers, ((0, 0), (LAGS // 2, LAGS // 2)))
    blocks = padded.reshape(rows, (length + LAGS) // LAGBLK, LAGBLK)
    windows = jnp.concatenate([blocks[:, :-1], blocks[:, 1:]], axis=2)
    return lax.map(hankel_rows, jnp.transpose(windows, (1, 0, 2)))


def correlate_window(source, hankel, selector):
    rows, length = source.shape
    nblocks = length // LAGBLK
    shaped = source.reshape(rows, nblocks, LAGBLK)
    pieces = []
    for shift in range(LAGS // LAGBLK):
        corr = jnp.einsum(
            "ibu,bjum->ijm",
            shaped,
            hankel[shift : shift + nblocks],
            preferred_element_type=jnp.float32,
        )
        pieces.append(jnp.dot(selector, corr.reshape(-1, LAGBLK), precision=lax.Precision.HIGHEST))
    return jnp.concatenate(pieces, axis=1)


def shards(traces, band_group, filters, pair_bin, bin_order):
    filtered = prefilter(traces, band_group, filters)
    hankel = build_hankel(filtered)
    nbins = bin_order.shape[0]
    rows, length = filtered.shape
    group = lax.axis_index("src")
    n_groups = lax.axis_size("src")
    n_owners = lax.axis_size("rcv")
    stride = n_owners // (STEPS * n_groups)
    window = 2 * BINS_DEV * n_groups + 8
    offsets = jnp.arange(window, dtype=jnp.int32)
    partial_value = jnp.zeros((nbins, LAGS), jnp.float32)
    counts = jnp.zeros((nbins,), jnp.float32)
    for step in range(STEPS):
        owner = (step * n_groups + group) * stride
        source = from_root(filtered, "rcv", owner)
        flat_bins = pair_bin[step].reshape(-1)
        base = jnp.minimum(jnp.min(flat_bins), nbins - window)
        selector = (flat_bins[None, :] - base == offsets[:, None]).astype(jnp.float32)
        local = correlate_window(source, hankel, selector)
        current = lax.dynamic_slice_in_dim(partial_value, base, window, 0)
        partial_value = lax.dynamic_update_slice_in_dim(partial_value, current + local, base, 0)
        current_counts = lax.dynamic_slice_in_dim(counts, base, window, 0)
        counts = lax.dynamic_update_slice_in_dim(
            counts, current_counts + jnp.sum(selector, axis=1), base, 0
        )
    reorder = (bin_order[:, None] == jnp.arange(nbins, dtype=jnp.int32)[None, :]).astype(
        jnp.float32
    )
    ordered = jnp.dot(reorder, partial_value, precision=lax.Precision.HIGHEST)
    ordered_counts = jnp.dot(reorder, counts[:, None], precision=lax.Precision.HIGHEST)[:, 0]
    sums, totals = (
        lax.psum_scatter(ordered, ("src", "rcv"), scatter_dimension=0, tiled=True),
        lax.psum_scatter(ordered_counts, ("src", "rcv"), scatter_dimension=0, tiled=True),
    )
    return sums / jnp.sqrt(length * totals)[:, None]


def solution(mesh):
    in_specs = (P("rcv", None), P("rcv"), P(), P(None, "src", "rcv"), P())
    out_specs = P(("src", "rcv"), None)
    return jax.shard_map(shards, mesh=mesh, in_specs=in_specs, out_specs=out_specs, check_vma=False)
```

profile of v0, /device:TPU:0, one launch (start us, length us, event | category | flops | bytes accessed | tf_op | source)
XLA Modules:
  0.0 1106.9 jit_solution(6226053008563414995)
XLA Ops:
  12.0 255.5 %while.12 = (s32[]{:T(128)}, bf16[7,128,128,128]{3,2,0,1:T(8,128)(2,1)}, bf16[7,128,256]{1,2,0:T(8,128)(2,1)S(1)}, s32[]{:T(128)}, bf16[]{:T(256)}) while((s32[]{:T(128)}, bf16[7,128,128,128]{3,2,0,1:T(8,128)(2,1)}, bf16[7,128,256]{1,2,0:T(8,128)(2,1)S(1)}, s32[]{:T(128)}, bf16[]{:T(256)}) %tuple.62), condition=%wide.region_4.5_spmd, body=%wide.region_3.4_spmd.sunk | while | flops 2 | bytes 67404352 | solution.py:50
  18.2 12.9 %reshape.109 = bf16[128,128,257]{0,2,1:T(8,128)(2,1)} reshape(bf16[128,32896]{0,1:T(8,128)(2,1)} %pad.47) | data formatting | bytes 16842752 | tf_op jit(solution)/shard_map/while/body/eval_jaxpr/reshape | solution.py:42
  31.1 4.8 slice_bitcast_fusion.34
  35.9 6.8 copy.67
  42.8 5.8 constant_dynamic-update-slice_fusion.2
  54.7 12.9 %reshape.109 = bf16[128,128,257]{0,2,1:T(8,128)(2,1)} reshape(bf16[128,32896]{0,1:T(8,128)(2,1)} %pad.47) | data formatting | bytes 16842752 | tf_op jit(solution)/shard_map/while/body/eval_jaxpr/reshape | solution.py:42
  67.7 4.8 slice_bitcast_fusion.34
  72.5 6.8 copy.67
  79.3 5.8 constant_dynamic-update-slice_fusion.2
  91.3 13.0 %reshape.109 = bf16[128,128,257]{0,2,1:T(8,128)(2,1)} reshape(bf16[128,32896]{0,1:T(8,128)(2,1)} %pad.47) | data formatting | bytes 16842752 | tf_op jit(solution)/shard_map/while/body/eval_jaxpr/reshape | solution.py:42
  104.2 4.8 slice_bitcast_fusion.34
  109.0 6.8 copy.67
  115.8 5.7 constant_dynamic-update-slice_fusion.2
  127.7 12.9 %reshape.109 = bf16[128,128,257]{0,2,1:T(8,128)(2,1)} reshape(bf16[128,32896]{0,1:T(8,128)(2,1)} %pad.47) | data formatting | bytes 16842752 | tf_op jit(solution)/shard_map/while/body/eval_jaxpr/reshape | solution.py:42
  140.6 4.8 slice_bitcast_fusion.34
  145.4 6.8 copy.67
  152.2 5.8 constant_dynamic-update-slice_fusion.2
  164.2 12.9 %reshape.109 = bf16[128,128,257]{0,2,1:T(8,128)(2,1)} reshape(bf16[128,32896]{0,1:T(8,128)(2,1)} %pad.47) | data formatting | bytes 16842752 | tf_op jit(solution)/shard_map/while/body/eval_jaxpr/reshape | solution.py:42
  177.1 4.8 slice_bitcast_fusion.34
  181.9 6.8 copy.67
  188.7 5.8 constant_dynamic-update-slice_fusion.2
  200.7 12.9 %reshape.109 = bf16[128,128,257]{0,2,1:T(8,128)(2,1)} reshape(bf16[128,32896]{0,1:T(8,128)(2,1)} %pad.47) | data formatting | bytes 16842752 | tf_op jit(solution)/shard_map/while/body/eval_jaxpr/reshape | solution.py:42
  213.6 4.8 slice_bitcast_fusion.34
  218.4 6.8 copy.67
  225.2 5.8 constant_dynamic-update-slice_fusion.2
  237.2 12.9 %reshape.109 = bf16[128,128,257]{0,2,1:T(8,128)(2,1)} reshape(bf16[128,32896]{0,1:T(8,128)(2,1)} %pad.47) | data formatting | bytes 16842752 | tf_op jit(solution)/shard_map/while/body/eval_jaxpr/reshape | solution.py:42
  250.1 4.8 slice_bitcast_fusion.34
  254.9 6.8 copy.67
  261.7 5.8 constant_dynamic-update-slice_fusion.2
  269.7 8.4 fusion.38
  278.1 11.5 %fusion.32 = f32[128,128,128]{2,0,1:T(8,128)} fusion(bf16[7,128,128,128]{3,2,0,1:T(8,128)(2,1)} %get-tuple-element.46, bf16[128,4,128]{2,0,1:T(8,128)(2,1)S(1)} %copy-done.4), kind=kOutput, calls=%fused_computation.36 | convolution fusion | flops 2147483648 | bytes 25296896 | tf_op jit(solution)/shard_map/ibu,bjum->ijm/dot_general | solution.py:59
  289.7 11.5 %fusion.26 = f32[128,128,128]{2,0,1:T(8,128)} fusion(bf16[7,128,128,128]{3,2,0,1:T(8,128)(2,1)} %get-tuple-element.46, bf16[128,4,128]{2,0,1:T(8,128)(2,1)S(1)} %copy-done.4), kind=kOutput, calls=%fused_computation.34 | convolution fusion | flops 2147483648 | bytes 25296896 | tf_op jit(solution)/shard_map/ibu,bjum->ijm/dot_general | solution.py:59
  301.2 11.6 %fusion.44 = f32[128,128,128]{2,0,1:T(8,128)} fusion(bf16[7,128,128,128]{3,2,0,1:T(8,128)(2,1)} %get-tuple-element.46, bf16[128,4,128]{2,0,1:T(8,128)(2,1)S(1)} %copy-done.4), kind=kOutput, calls=%fused_computation.40 | convolution fusion | flops 2147483648 | bytes 25296896 | tf_op jit(solution)/shard_map/ibu,bjum->ijm/dot_general | solution.py:59
  312.8 11.5 %fusion.47 = f32[128,128,128]{2,0,1:T(8,128)} fusion(bf16[7,128,128,128]{3,2,0,1:T(8,128)(2,1)} %get-tuple-element.46, bf16[128,4,128]{2,0,1:T(8,128)(2,1)S(1)} %copy-done.3), kind=kOutput, calls=%fused_computation.41 | convolution fusion | flops 2147483648 | bytes 25296896 | tf_op jit(solution)/shard_map/ibu,bjum->ijm/dot_general | solution.py:59
  324.3 11.6 %fusion.41 = f32[128,128,128]{2,0,1:T(8,128)} fusion(bf16[7,128,128,128]{3,2,0,1:T(8,128)(2,1)} %get-tuple-element.46, bf16[128,4,128]{2,0,1:T(8,128)(2,1)S(1)} %copy-done.3), kind=kOutput, calls=%fused_computation.39 | convolution fusion | flops 2147483648 | bytes 25296896 | tf_op jit(solution)/shard_map/ibu,bjum->ijm/dot_general | solution.py:59
  335.9 12.1 %fusion.35 = f32[128,128,128]{2,0,1:T(8,128)} fusion(bf16[7,128,128,128]{3,2,0,1:T(8,128)(2,1)} %get-tuple-element.46, bf16[128,4,128]{2,0,1:T(8,128)(2,1)S(1)} %copy-done.3), kind=kOutput, calls=%fused_computation.37 | convolution fusion | flops 2147483648 | bytes 25296896 | tf_op jit(solution)/shard_map/ibu,bjum->ijm/dot_general | solution.py:59
  348.0 11.5 %fusion.29 = f32[128,128,128]{2,0,1:T(8,128)} fusion(bf16[7,128,128,128]{3,2,0,1:T(8,128)(2,1)} %get-tuple-element.46, bf16[128,4,128]{2,0,1:T(8,128)(2,1)S(1)} %copy-done.3), kind=kOutput, calls=%fused_computation.35 | convolution fusion | flops 2147483648 | bytes 25296896 | tf_op jit(solution)/shard_map/ibu,bjum->ijm/dot_general | solution.py:59
  359.5 4.9 copy.47
  364.4 8.4 copy.45
  380.5 8.4 copy.43
  392.9 8.8 copy.49
  405.7 4.9 copy.54
  410.5 8.4 copy.53
  426.8 8.6 copy.52
  439.3 5.3 copy.51
  451.0 4.9 fusion.25
  459.6 69.2 %all-reduce.3 = f32[1024]{0:T(1024)S(1)} all-reduce(f32[1024]{0:T(1024)S(1)} %bitcast.166), channel_id=3, replica_groups=mesh['src'=4,'rcv'=32] {'src','rcv'}, use_global_device_ids=true, to_apply=%region_10.11.clone | all-reduce | flops 1024 | bytes 8192
  528.8 569.7 %reduce-scatter.2.cloned.1.call-done = f32[8,512]{1,0:T(8,128)} async-done(((f32[1024,512]{1,0:T(8,128)}), f32[8,512]{1,0:T(8,128)}) %reduce-scatter.2.cloned.1.call-update) | async-done | bytes 16400 | tf_op jit(solution)/shard_map/reduce_scatter | solution.py:101
  (85 shorter events, 88.1 us)
Async XLA Ops:
  6.5 0.7 copy-start
  6.5 263.1 %all-reduce.7.cloned.1.call-start = ((), (), s32[]{:S(2)}) async-start(), calls=%async_computation.2 | async-start | bytes 524288 | tf_op jit(solution)/shard_map/psum | solution.py:16
  11.8 1086.7 %reduce-scatter.2.cloned.1.call-start = ((), (), s32[]{:S(2)}) async-start(), calls=%async_computation.1 | async-start | bytes 2113536 | tf_op jit(solution)/shard_map/reduce_scatter | solution.py:101
  12.0 255.5 %copy-start.2 = (s32[2,128,128]{2,1,0:T(8,128)S(1)}, s32[2,128,128]{2,1,0:T(8,128)}, u32[]{:S(2)}) copy-start(s32[2,128,128]{2,1,0:T(8,128)} %param.10) | copy-start | bytes 393220
  269.7 8.5 copy-start.4
  301.2 11.6 %copy-start.3 = (bf16[128,4,128]{2,0,1:T(8,128)(2,1)S(1)}, bf16[128,4,128]{2,0,1:T(8,128)(2,1)}, u32[]{:S(2)}) copy-start(bf16[128,4,128]{2,0,1:T(8,128)(2,1)} %get-tuple-element.56) | copy-start | bytes 393220
  389.0 16.6 %slice-start.2 = ((s8[8388608]{0:T(1024)(128)(4,1)}), s8[4194304]{0:T(1024)(128)(4,1)S(1)}, s32[]{:S(2)}) async-start(s8[8388608]{0:T(1024)(128)(4,1)} %bitcast.160), calls=%async_computation.5 | async-start | bytes 8388608
  392.9 12.7 %slice-start.3 = ((s8[8388608]{0:T(1024)(128)(4,1)}), s8[4194304]{0:T(1024)(128)(4,1)S(1)}, s32[]{:S(2)}) async-start(s8[8388608]{0:T(1024)(128)(4,1)} %bitcast.160), calls=%async_computation.6 | async-start | bytes 8388608
  422.8 16.4 %slice-start = ((s8[8388608]{0:T(1024)(128)(4,1)}), s8[4194304]{0:T(1024)(128)(4,1)S(1)}, s32[]{:S(2)}) async-start(s8[8388608]{0:T(1024)(128)(4,1)} %bitcast.158), calls=%async_computation.3 | async-start | bytes 8388608
  426.8 12.5 %slice-start.1 = ((s8[8388608]{0:T(1024)(128)(4,1)}), s8[4194304]{0:T(1024)(128)(4,1)S(1)}, s32[]{:S(2)}) async-start(s8[8388608]{0:T(1024)(128)(4,1)} %bitcast.158), calls=%async_computation.4 | async-start | bytes 8388608
  444.6 6.5 copy-start.5
  448.5 651.4 %copy-start.1 = (f32[24,32]{1,0:T(8,128)S(1)}, f32[24,32]{1,0:T(8,128)}, u32[]{:S(2)}) copy-start(f32[24,32]{1,0:T(8,128)} %param.9) | copy-start | bytes 9220
Sparse Core Ops, SparseCore 0:
  11.9 104.2 all-reduce.6
  456.1 642.3 reduce-scatter.1
where the time goes:
time: 1120 us; the launch traced here: 1110 us
  waiting for transfers between devices  570 us (51%)
  local copies, waits for them, and re-layouts  319 us (28%)
  matrix products  129 us (12%)
  blocking collectives  69.2 us (6%)
  between operations  15.3 us (1%)
    reduce_scatter x1, waiting for transfers between devices, shards(): lax.psum_scatter(ordered, ('src', 'rcv'), scatter_dimension=0, tiled=True)  570 us
    reshape x7, local copies, waits for them, and re-layouts, hankel_rows(): return tiled.reshape(rows, half, width + 1)[:, :, :half]  90.6 us
    dot_general x8, matrix products, correlate_window(): jnp.einsum('ibu,bjum->ijm', shaped, hankel[shift:shift + nblocks], prefer...  89.8 us
    dynamic_update_slice x14, local copies, waits for them, and re-layouts, build_hankel(): return lax.map(hankel_rows, jnp.transpose(windows, (1, 0, 2)))  88.2 us
    unnamed x1, blocking collectives  69.2 us
    dot_general x8, local copies, waits for them, and re-layouts, correlate_window(): jnp.einsum('ibu,bjum->ijm', shaped, hankel[shift:shift + nblocks], prefer...  57.6 us
    broadcast_in_dim x7, local copies, waits for them, and re-layouts, build_hankel(): return lax.map(hankel_rows, jnp.transpose(windows, (1, 0, 2)))  33.5 us
    dot_general x8, matrix products, correlate_window(): jnp.dot(selector, corr.reshape(-1, LAGBLK), precision=lax.Precision.HIGHEST)  31.2 us
  transfers between devices with their start and end apart: 2, of which 1 were waited for; matrix products, arithmetic and copies ran while one was open for 23% of the time, Pallas kernels for 0%

commit v1 on v0

v1 whole, which is shorter than its diff:
```python
import functools

import jax
import jax.numpy as jnp
import numpy as np
from jax import lax
from jax.experimental import pallas as pl
from jax.experimental.pallas import tpu as pltpu
from jax.sharding import PartitionSpec as P

LAGS = 512
SAMPLES = 512
TAPS = 32
FREQS = 384
PERIOD = 2 * FREQS
CH = 128
GROUP = 8
SPAN = 72
WIN = 128
RING = 4
BF = jnp.bfloat16
F32 = jnp.float32


def split_bf16(matrix):
    high = matrix.astype(np.float32).astype(jnp.bfloat16)
    low = (matrix - high.astype(np.float64)).astype(np.float32).astype(jnp.bfloat16)
    return np.stack([high, low])


@functools.lru_cache(None)
def transforms():
    odd = 2 * np.arange(FREQS) + 1
    t = np.arange(SAMPLES)
    angle = np.pi / PERIOD * ((t[:, None] * odd[None, :]) % (2 * PERIOD))
    forward = np.concatenate([np.cos(angle), -np.sin(angle)], axis=1)
    lag = np.arange(LAGS) - LAGS // 2
    angle = np.pi / PERIOD * ((odd[:, None] * lag[None, :]) % (2 * PERIOD))
    back = np.concatenate([np.cos(angle), -np.sin(angle)], axis=0) * (2.0 / PERIOD)
    return split_bf16(forward), split_bf16(back)


def device(src, z, y, core):
    return src * 32 + (z % RING) * 8 + (y % RING) * 2 + core


def owners():
    for s in range(4):
        for k in range(2):
            yield s, k, 2 * (s % 2), 2 * k + s // 2


def plans():
    first, second = [], []
    for s, k, y, z in owners():
        first.append((device(s, z, y, k), device(s, z, y + 1, k)))
        first.append((device(s, z, y, 1 - k), device(s, z, y - 1, k)))
        second.append((device(s, z, y, k), device(s, z, y + 2, k)))
    along = []
    for d in (1, 3, 2):
        along.append(
            [
                (device(s, z, yy, k), device(s, z + d, yy, k))
                for s, k, y, z in owners()
                for yy in range(RING)
            ]
        )
    return [first, second], along


def vmem(n):
    return [pl.BlockSpec(memory_space=pltpu.VMEM)] * n


def prefilter_kernel(traces_ref, band_ref, filters_ref, out_ref, pad_ref):
    bands = filters_ref.shape[0]
    onehot = (lax.broadcasted_iota(jnp.int32, (bands, CH), 0) == band_ref[...]).astype(F32)
    taps = lax.dot_general(
        filters_ref[...],
        onehot,
        (((0,), (0,)), ((), ())),
        precision=lax.Precision.HIGHEST,
        preferred_element_type=F32,
    )
    pad_ref[0:TAPS, :] = jnp.zeros((TAPS, CH), F32)
    pad_ref[TAPS:, :] = traces_ref[...].astype(F32).T
    rows = 128
    power = jnp.zeros((1, CH), F32)
    parts = []
    for start in range(0, SAMPLES, rows):
        total = jnp.zeros((rows, CH), F32)
        for k in range(TAPS):
            low = TAPS + start - k
            total = total + taps[k : k + 1, :] * pad_ref[low : low + rows, :]
        power = power + jnp.sum(total * total, axis=0, keepdims=True)
        parts.append(total)
    scale = lax.rsqrt(power * (1.0 / SAMPLES) + 1e-06)
    for i, total in enumerate(parts):
        out_ref[:, i * rows : (i + 1) * rows] = (total * scale).T.astype(BF)


def prefilter(traces, band_group, filters):
    return pl.pallas_call(
        prefilter_kernel,
        out_shape=jax.ShapeDtypeStruct((CH, SAMPLES), BF),
        in_specs=vmem(3),
        out_specs=pl.BlockSpec(memory_space=pltpu.VMEM),
        scratch_shapes=[pltpu.VMEM((TAPS + SAMPLES, CH), F32)],
        name="prefilter",
    )(traces, band_group.reshape(1, CH), filters)


def receivers_kernel(mine_ref, other_ref, w_ref, out_ref):
    for i, ref in enumerate((mine_ref, other_ref)):
        value = jnp.dot(ref[...], w_ref[0], preferred_element_type=F32)
        value = value + jnp.dot(ref[...], w_ref[1], preferred_element_type=F32)
        out_ref[i * CH : (i + 1) * CH, :] = value.astype(BF)


def receivers(mine, other, w):
    return pl.pallas_call(
        receivers_kernel,
        out_shape=jax.ShapeDtypeStruct((2 * CH, PERIOD), BF),
        in_specs=vmem(3),
        out_specs=pl.BlockSpec(memory_space=pltpu.VMEM),
        compiler_params=pltpu.CompilerParams(vmem_limit_bytes=40 * 1024 * 1024),
        cost_estimate=pl.CostEstimate(
            flops=2 * 2 * 2 * CH * SAMPLES * PERIOD, bytes_accessed=2 * 1024 * 1024, transcendentals=0
        ),
        name="receivers",
    )(mine, other, w)


def correlate_kernel(
    low_ref, held_ref, r0, r1, r2, w_ref, fc_ref, bins_ref, back_ref, out_ref, fs, total, g0, g1
):
    block = ((held_ref[...] + r0[...]) + (r1[...] + r2[...])).astype(BF)
    fs[...] = jnp.dot(block, w_ref[0], preferred_element_type=F32) + jnp.dot(
        block, w_ref[1], preferred_element_type=F32
    )
    total[...] = jnp.zeros_like(total)
    n_groups = CH // GROUP

    def spread(g, span, buffer):
        first = pl.multiple_of(g * GROUP, GROUP)
        rel = bins_ref[pl.ds(first, GROUP), :] - low_ref[g]
        offsets = lax.broadcasted_iota(jnp.int32, (span, 2 * CH), 0)
        for p in range(0, GROUP, 2):
            pair = jnp.concatenate(
                [jnp.where(rel[q : q + 1, :] == offsets, 1.0, 0.0) for q in (p, p + 1)], axis=0
            ).astype(BF)
            buffer[p * span : (p + 2) * span, :] = jnp.dot(
                pair, fc_ref[...], preferred_element_type=F32
            )

    def gather(g, span, buffer):
        first = pl.multiple_of(g * GROUP, GROUP)
        low = low_ref[g] - low_ref[n_groups]
        shift = low % 8
        start = pl.multiple_of(low - shift, 8)
        room = jnp.zeros((8, 128), F32)
        for j in range(0, FREQS, 128):
            re, im = slice(j, j + 128), slice(FREQS + j, FREQS + j + 128)
            fr, fi = fs[pl.ds(first, GROUP), re], fs[pl.ds(first, GROUP), im]
            sum_re = jnp.zeros((span, 128), F32)
            sum_im = jnp.zeros((span, 128), F32)
            for p in range(GROUP):
                rows = slice(p * span, (p + 1) * span)
                gr, gi = buffer[rows, re], buffer[rows, im]
                a, b = fr[p : p + 1, :], fi[p : p + 1, :]
                sum_re = sum_re + (a * gr + b * gi)
                sum_im = sum_im + (a * gi - b * gr)
            for part, value in ((re, sum_re), (im, sum_im)):
                moved = pltpu.roll(jnp.concatenate([value, room], axis=0), shift, 0)
                total[pl.ds(start, span + 8), part] += moved

    fits = low_ref[n_groups + 1] == 1

    @pl.when(fits)
    def _():
        spread(0, SPAN, g0)

        def body(h, carry):
            g = 2 * h
            spread(g + 1, SPAN, g1)
            gather(g, SPAN, g0)
            spread(jnp.minimum(g + 2, n_groups - 1), SPAN, g0)
            gather(g + 1, SPAN, g1)
            return carry

        lax.fori_loop(0, n_groups // 2, body, 0)

    @pl.when(jnp.logical_not(fits))
    def _():
        def body(g, carry):
            spread(g, WIN, g0)
            gather(g, WIN, g0)
            return carry

        lax.fori_loop(0, n_groups, body, 0)

    for start in range(0, WIN, 128):
        value = total[start : start + 128, :]
        high = value.astype(BF)
        low = (value - high.astype(F32)).astype(BF)
        out_ref[start : start + 128, :] = (
            jnp.dot(high, back_ref[0], preferred_element_type=F32)
            + jnp.dot(low, back_ref[0], preferred_element_type=F32)
            + jnp.dot(high, back_ref[1], preferred_element_type=F32)
        )


def correlate(lows, held, parts, w, fc, bins, back):
    return pl.pallas_call(
        correlate_kernel,
        out_shape=jax.ShapeDtypeStruct((WIN, LAGS), F32),
        in_specs=[pl.BlockSpec(memory_space=pltpu.SMEM)] + vmem(8),
        out_specs=pl.BlockSpec(memory_space=pltpu.VMEM),
        scratch_shapes=[
            pltpu.VMEM((CH, PERIOD), F32),
            pltpu.VMEM((2 * WIN, PERIOD), F32),
            pltpu.VMEM((GROUP * WIN, PERIOD), F32),
            pltpu.VMEM((GROUP * SPAN, PERIOD), F32),
        ],
        compiler_params=pltpu.CompilerParams(vmem_limit_bytes=40 * 1024 * 1024),
        cost_estimate=pl.CostEstimate(
            flops=2 * 128 * SPAN * 256 * PERIOD, bytes_accessed=6 * 1024 * 1024, transcendentals=0
        ),
        name="correlate",
    )(lows, held, *parts, w, fc, bins, back)


def arrange_kernel(base_ref, order_ref, mine_ref, other_ref, counts_ref, out_ref):
    columns = lax.broadcasted_iota(jnp.int32, (512, WIN), 1)
    order = order_ref[...]
    result = None
    tally = None
    for i, ref in enumerate((mine_ref, other_ref)):
        pick = jnp.where(order - base_ref[i] == columns, 1.0, 0.0).astype(BF)
        value = ref[...]
        high = value.astype(BF)
        low = (value - high.astype(F32)).astype(BF)
        part = jnp.dot(pick, high, preferred_element_type=F32) + jnp.dot(
            pick, low, preferred_element_type=F32
        )
        count = jnp.dot(pick, counts_ref[i], preferred_element_type=F32)
        result = part if result is None else result + part
        tally = count if tally is None else tally + count
    out_ref[:, :LAGS] = result.astype(BF)
    out_ref[:, LAGS:] = tally.astype(BF)


def arrange(bases, order, mine, other, counts):
    return pl.pallas_call(
        arrange_kernel,
        out_shape=jax.ShapeDtypeStruct((512, LAGS + 128), BF),
        in_specs=[pl.BlockSpec(memory_space=pltpu.SMEM)] + vmem(4),
        out_specs=pl.BlockSpec(memory_space=pltpu.VMEM),
        compiler_params=pltpu.CompilerParams(vmem_limit_bytes=40 * 1024 * 1024),
        name="arrange",
    )(bases, order, mine, other, counts)


def finish_kernel(parts_ref, out_ref):
    value = jnp.sum(parts_ref[...].astype(F32).reshape(64, 8, LAGS + 128), axis=0)
    totals = jnp.sum(value[:, LAGS:], axis=1, keepdims=True)
    out_ref[...] = value[:, :LAGS] / jnp.sqrt(SAMPLES * totals)


def finish(parts):
    return pl.pallas_call(
        finish_kernel,
        out_shape=jax.ShapeDtypeStruct((8, LAGS), F32),
        in_specs=vmem(1),
        out_specs=pl.BlockSpec(memory_space=pltpu.VMEM),
        compiler_params=pltpu.CompilerParams(vmem_limit_bytes=40 * 1024 * 1024),
        name="finish",
    )(parts)


def shards(traces, band_group, filters, pair_bin, bin_order):
    both = ("src", "rcv")
    swap = [(i, i ^ 1) for i in range(32)]
    forward, back = transforms()
    w, back = jnp.asarray(forward), jnp.asarray(back)
    src, rcv = lax.axis_index("src"), lax.axis_index("rcv")
    core = rcv % 2
    y, z = (rcv // 2) % RING, rcv // 8
    owner = jnp.logical_and(y == 2 * (src % 2), z == 2 * core + src // 2)

    own_bins = lax.dynamic_index_in_dim(pair_bin, core, 0, keepdims=False)
    other_bins = lax.dynamic_index_in_dim(pair_bin, 1 - core, 0, keepdims=False)
    bins = jnp.concatenate([own_bins, lax.ppermute(other_bins, "rcv", swap)], axis=1)

    filtered = prefilter(traces, band_group, filters)
    partner = lax.ppermute(filtered, "rcv", swap)
    seed = jnp.where(core == 0, filtered, partner)
    across, along = plans()
    got = [lax.ppermute(seed, both, plan) for plan in across]
    held = jnp.where(owner, seed, got[0] + got[1])
    parts = [lax.ppermute(held, both, plan) for plan in along]

    fc = receivers(filtered, partner, w)
    lowest = jnp.min(bins)
    grouped = bins.reshape(CH // GROUP, GROUP * 2 * CH)
    lows, highs = jnp.min(grouped, axis=1), jnp.max(grouped, axis=1)
    fits = jnp.all(highs - lows < SPAN)
    lows = jnp.minimum(jnp.where(fits, lows, lowest), lowest + WIN)
    table = jnp.concatenate([lows, lowest[None], fits.astype(jnp.int32)[None]])
    counts = jnp.sum(
        (bins.reshape(1, -1) - lowest == jnp.arange(WIN, dtype=jnp.int32)[:, None]).astype(jnp.int32),
        axis=1,
    )
    message = jnp.concatenate([counts, lowest[None]])
    theirs = lax.ppermute(message, "rcv", swap)
    tallies = jnp.stack([counts, theirs[:WIN]])
    bases = jnp.stack([lowest, theirs[WIN]])
    lane = jnp.arange(128, dtype=jnp.int32)
    place = jnp.arange(2, dtype=jnp.int32)[:, None, None] * 2
    tallies = tallies[:, :, None]
    tallies = jnp.where(lane == place, tallies // 256 * 256, 0) + jnp.where(
        lane == place + 1, tallies % 256, 0
    )
    tallies = tallies.astype(BF)
    order = lax.dynamic_index_in_dim(bin_order.reshape(64, 2, 8), core, 1, keepdims=False)
    order = order.reshape(512, 1)

    window = correlate(table, held, parts, w, fc, bins, back)
    other_window = lax.ppermute(window, "rcv", swap)
    payload = arrange(bases, order, window, other_window, tallies)
    groups = [[2 * i + c for i in range(64)] for c in range(2)]
    arrived = lax.all_to_all(payload, both, 0, 0, tiled=True, axis_index_groups=groups)
    return finish(arrived)


def solution(mesh):
    in_specs = (P("rcv", None), P("rcv"), P(), P(None, "src", "rcv"), P())
    out_specs = P(("src", "rcv"), None)
    return jax.shard_map(shards, mesh=mesh, in_specs=in_specs, out_specs=out_specs, check_vma=False)
```

time: 1120 us -> 70.3 us (0.06); the launches traced: 1110 us -> 69.9 us
  waiting for transfers between devices: 570 us -> 6.21 us
  local copies, waits for them, and re-layouts: 319 us -> 1.8 us
  matrix products: 129 us -> 0 us
  blocking collectives: 69.2 us -> 23.3 us
  Pallas kernels: 0 us -> 15.4 us
  starting transfers between devices: 0.04 us -> 13.6 us
  between operations: 15.3 us -> 2.03 us
    reduce_scatter x1 -> x0, waiting for transfers between devices: 570 us -> none  [shards(): lax.psum_scatter(ordered, ('src', 'rcv'), scatter_dimension=0, tiled=True)]
    dot_general x19 -> x0, matrix products: 129 us -> none  [the longest x8 89.8 us: correlate_window(): jnp.einsum('ibu,bjum->ijm', shaped, hankel[shift:shift + nblocks], prefer...]
    reshape x9 -> x2, local copies, waits for them, and re-layouts: 92.1 us -> 0.95 us  [the longest x1 0.83 us: shards(): bin_order.reshape(64, 2, 8)]
    dynamic_update_slice x17 -> x0, local copies, waits for them, and re-layouts: 90.7 us -> none  [the longest x14 88.2 us: build_hankel(): return lax.map(hankel_rows, jnp.transpose(windows, (1, 0, 2)))]
    unnamed x1 -> x0, blocking collectives: 69.2 us -> none
    dot_general x8 -> x0, local copies, waits for them, and re-layouts: 57.6 us -> none  [correlate_window(): jnp.einsum('ibu,bjum->ijm', shaped, hankel[shift:shift + nblocks], prefer...]
    broadcast_in_dim x9 -> x0, local copies, waits for them, and re-layouts: 33.8 us -> none  [the longest x7 33.5 us: build_hankel(): return lax.map(hankel_rows, jnp.transpose(windows, (1, 0, 2)))]
    pad x8 -> x0, local copies, waits for them, and re-layouts: 28.6 us -> none  [the longest x7 28.6 us: hankel_rows(): tiled = jnp.pad(tiled, ((0, 0), (0, half)))]
  transfers between devices with their start and end apart: 2 -> 9, of which waited for: 1 -> 6; matrix products, arithmetic and copies ran while one was open for 23% -> 9% of each run, Pallas kernels for 0% -> 5%
where the time goes in v1:
time: 70.3 us; the launch traced here: 69.9 us
  blocking collectives  23.3 us (33%)
  Pallas kernels  15.4 us (22%)
  starting transfers between devices  13.6 us (19%)
  other arithmetic  7.54 us (11%)
  waiting for transfers between devices  6.21 us (9%)
  between operations  2.03 us (3%)
  local copies, waits for them, and re-layouts  1.8 us (3%)
    all_to_all x1, blocking collectives, shards(): lax.all_to_all(payload, both, 0, 0, tiled=True, axis_index_groups=groups)  23.3 us
    pallas_call x1, Pallas kernels, correlate(): pl.pallas_call(correlate_kernel, out_shape=jax.ShapeDtypeStruct((WIN, LAG...  10 us
    ppermute x2, starting transfers between devices, shards(): got = [lax.ppermute(seed, both, plan) for plan in across]  6.49 us
    ppermute x3, starting transfers between devices, shards(): parts = [lax.ppermute(held, both, plan) for plan in along]  6.42 us
    pallas_call x1, Pallas kernels, prefilter(): pl.pallas_call(prefilter_kernel, out_shape=jax.ShapeDtypeStruct((CH, SAMP...  2.68 us
    ppermute x2, waiting for transfers between devices, shards(): got = [lax.ppermute(seed, both, plan) for plan in across]  2.55 us
    reduce_min x4, other arithmetic, shards(): lows, highs = (jnp.min(grouped, axis=1), jnp.max(grouped, axis=1))  2.49 us
    ppermute x3, waiting for transfers between devices, shards(): parts = [lax.ppermute(held, both, plan) for plan in along]  1.86 us
  transfers between devices with their start and end apart: 9, of which 6 were waited for; matrix products, arithmetic and copies ran while one was open for 9% of the time, Pallas kernels for 5%

profile of v1, /device:TPU:0, one launch (start us, length us, event | category | flops | bytes accessed | tf_op | source)
XLA Modules:
  0.0 69.9 jit_solution(12243323524985267088)
XLA Ops:
  0.0 0.0 copy-start
  0.0 1.7 %dynamic-slice_reduce_fusion = (s32[128]{0:T(128)S(1)}, s32[128]{0:T(128)S(1)}, s32[]{:T(128)}, s32[128,128]{1,0:T(8,128)S(1)}, s32[128,128]{1,0:T(8,128)S(1)}) fusion(s32[2,128,128]{2,1,0:T(8,128)} %param.10, s32[]{:T(128)S(6)} %select_n.85, s32[]{:T(128)S(6)} %select_n.86), kind=kLoop, calls=%fused_computation.8 | loop fusion | flops 48895 | bytes 263180 | tf_op jit(solution)/shard_map/reduce_min | solution.py:306
  1.7 0.0 collective-permute-start
  1.7 2.7 %prefilter.1.mine_ref = bf16[128,512]{1,0:T(8,128)(2,1)} custom-call(bf16[128,512]{1,0:T(8,128)(2,1)} %traces_ref.1, s32[1,128]{1,0:T(1,128)} %bitcast.19, f32[24,32]{1,0:T(8,128)} %filters_ref.1), custom_call_target="tpu_custom_call" | custom-call | tf_op jit(solution)/shard_map/prefilter/pallas_call | solution.py:103
  4.4 0.0 copy-start.1
  4.4 0.5 collective-permute-start.2
  4.9 0.1 iota_compare_fusion.1
  5.0 0.8 %reshape.227 = s32[64,2,8]{2,1,0:T(2,128)S(1)} reshape(s32[1024]{0:T(1024)} %param.11) | data formatting | bytes 8192 | tf_op jit(solution)/shard_map/reshape | solution.py:325
  5.8 0.1 dynamic-slice_reduce_fusion.3
  6.0 0.1 reshape.231.order_ref
  6.1 0.0 collective-permute-done
  6.1 0.6 fusion.2
  6.8 0.1 reduce_max.29
  6.9 0.1 reduce_min.49
  8.2 0.1 copy.10
  8.3 1.7 %convert_reduce_fusion = s32[128]{0:T(128)S(1)} fusion(s32[32768]{0:T(1024)S(1)} %bitcast.17), kind=kLoop, calls=%fused_computation | loop fusion | flops 12582784 | bytes 131584 | tf_op jit(solution)/shard_map/reduce_sum | solution.py:310
  10.0 0.1 reduce_max.30
  10.1 0.1 reduce_min.50
  10.2 0.6 compare_reduce_fusion
  10.9 0.6 fusion.1
  12.0 0.1 collective-permute-start.1
  12.1 0.1 pad_add_fusion.4.low_ref
  12.2 1.0 %collective-permute-done.1 = s32[129]{0:T(256)S(1)} collective-permute-done((s32[129]{0:T(256)S(1)}, s32[129]{0:T(256)S(1)}, u32[]{:S(2)}, u32[]{:S(2)}) %collective-permute-start.1) | collective-permute-done | bytes 548 | tf_op jit(solution)/shard_map/ppermute | solution.py:315
  13.2 0.5 slice.6
  13.7 0.0 collective-permute-done.2.other_ref
  13.7 1.0 %broadcast_select_fusion = bf16[128,512]{1,0:T(8,128)(2,1)S(1)} fusion(bf16[128,512]{1,0:T(8,128)(2,1)} %prefilter.1.mine_ref, bf16[128,512]{1,0:T(8,128)(2,1)S(1)} %collective-permute-done.2.other_ref, pred[]{:T(512)S(6)} %eq.69), kind=kLoop, calls=%fused_computation.6 | loop fusion | flops 65536 | bytes 393217 | tf_op jit(solution)/shard_map/jit(_where)/select_n | solution.py:297
  14.8 5.2 %collective-permute-start.4 = (bf16[128,512]{1,0:T(8,128)(2,1)S(1)}, bf16[128,512]{1,0:T(8,128)(2,1)S(1)}, u32[]{:S(2)}, u32[]{:S(2)}) collective-permute-start(bf16[128,512]{1,0:T(8,128)(2,1)S(1)} %broadcast_select_fusion), channel_id=1, source_target_pairs={{0,4},{17,21},{36,32},{53,49},{72,76},{89,93},{108,104},{125,121}} | collective-permute-start | bytes 393224 | tf_op jit(solution)/shard_map/ppermute | solution.py:299
  20.0 1.3 %collective-permute-start.3 = (bf16[128,512]{1,0:T(8,128)(2,1)S(1)}, bf16[128,512]{1,0:T(8,128)(2,1)S(1)}, u32[]{:S(2)}, u32[]{:S(2)}) collective-permute-start(bf16[128,512]{1,0:T(8,128)(2,1)S(1)} %broadcast_select_fusion), channel_id=1, source_target_pairs={{0,2},{1,6},{17,19},{16,23},{36,38},{37,34},{53,55},{52,51},{72,74... | collective-permute-start | bytes 393224 | tf_op jit(solution)/shard_map/ppermute | solution.py:299
  21.3 1.2 %collective-permute-done.4 = bf16[128,512]{1,0:T(8,128)(2,1)S(1)} collective-permute-done((bf16[128,512]{1,0:T(8,128)(2,1)S(1)}, bf16[128,512]{1,0:T(8,128)(2,1)S(1)}, u32[]{:S(2)}, u32[]{:S(2)}) %collective-permute-start.4) | collective-permute-done | bytes 131104 | tf_op jit(solution)/shard_map/ppermute | solution.py:299
  22.5 1.4 %collective-permute-done.3 = bf16[128,512]{1,0:T(8,128)(2,1)S(1)} collective-permute-done((bf16[128,512]{1,0:T(8,128)(2,1)S(1)}, bf16[128,512]{1,0:T(8,128)(2,1)S(1)}, u32[]{:S(2)}, u32[]{:S(2)}) %collective-permute-start.3) | collective-permute-done | bytes 131104 | tf_op jit(solution)/shard_map/ppermute | solution.py:299
  23.9 3.8 %collective-permute-start.7 = (bf16[128,512]{1,0:T(8,128)(2,1)S(1)}, bf16[128,512]{1,0:T(8,128)(2,1)S(1)}, u32[]{:S(2)}, u32[]{:S(2)}) collective-permute-start(bf16[128,512]{1,0:T(8,128)(2,1)S(1)} %add_select_fusion.held_ref), channel_id=1, source_target_pairs={{0,16},{2,18},{4,20},{6,22},{17,1},{19,3},{21,5},{23,7},{32,48},{3... | collective-permute-start | bytes 393224 | tf_op jit(solution)/shard_map/ppermute | solution.py:301
  27.7 1.3 %collective-permute-start.6 = (bf16[128,512]{1,0:T(8,128)(2,1)S(1)}, bf16[128,512]{1,0:T(8,128)(2,1)S(1)}, u32[]{:S(2)}, u32[]{:S(2)}) collective-permute-start(bf16[128,512]{1,0:T(8,128)(2,1)S(1)} %add_select_fusion.held_ref), channel_id=1, source_target_pairs={{0,24},{2,26},{4,28},{6,30},{17,9},{19,11},{21,13},{23,15},{32,56}... | collective-permute-start | bytes 393224 | tf_op jit(solution)/shard_map/ppermute | solution.py:301
  29.0 1.3 %collective-permute-start.5 = (bf16[128,512]{1,0:T(8,128)(2,1)S(1)}, bf16[128,512]{1,0:T(8,128)(2,1)S(1)}, u32[]{:S(2)}, u32[]{:S(2)}) collective-permute-start(bf16[128,512]{1,0:T(8,128)(2,1)S(1)} %add_select_fusion.held_ref), channel_id=1, source_target_pairs={{0,8},{2,10},{4,12},{6,14},{17,25},{19,27},{21,29},{23,31},{32,40}... | collective-permute-start | bytes 393224 | tf_op jit(solution)/shard_map/ppermute | solution.py:301
  30.3 0.0 copy-done
  30.3 0.0 copy-done.1
  30.3 0.6 receivers.1.fc_ref
  30.9 0.0 collective-permute-done.7.r2
  30.9 0.6 collective-permute-done.6.r1
  31.5 1.3 %collective-permute-done.5.r0 = bf16[128,512]{1,0:T(8,128)(2,1)S(1)} collective-permute-done((bf16[128,512]{1,0:T(8,128)(2,1)S(1)}, bf16[128,512]{1,0:T(8,128)(2,1)S(1)}, u32[]{:S(2)}, u32[]{:S(2)}) %collective-permute-start.5) | collective-permute-done | bytes 131104 | tf_op jit(solution)/shard_map/ppermute | solution.py:301
  32.8 0.0 copy-done.2
  32.8 10.0 %correlate.1.mine_ref = f32[128,512]{1,0:T(8,128)S(1)} custom-call(s32[18]{0:T(128)S(1)} %pad_add_fusion.4.low_ref, bf16[128,512]{1,0:T(8,128)(2,1)S(1)} %add_select_fusion.held_ref, bf16[128,512]{1,0:T(8,128)(2,1)S(1)} %collective-permute-done.5.r0, bf16[128,512]{1,0:T(8,128)(2,1)S(1)} %collective-permute-done.6.r1, ...), custom_call_target="tpu_custom_call" | custom-call | flops 3623878656 | bytes 6291456 | tf_op jit(solution)/shard_map/correlate/pallas_call | solution.py:214
  42.9 0.1 collective-permute-start.8
  42.9 0.6 pad_add_fusion.3.base_ref
  43.6 0.1 add_convert_fusion.counts_ref
  43.7 0.8 %collective-permute-done.8.other_ref = f32[128,512]{1,0:T(8,128)S(1)} collective-permute-done((f32[128,512]{1,0:T(8,128)S(1)}, f32[128,512]{1,0:T(8,128)S(1)}, u32[]{:S(2)}, u32[]{:S(2)}) %collective-permute-start.8) | collective-permute-done | bytes 262176 | tf_op jit(solution)/shard_map/ppermute | solution.py:329
  44.5 1.4 %arrange.1 = bf16[512,640]{1,0:T(8,128)(2,1)S(1)} custom-call(s32[2]{0:T(128)S(1)} %pad_add_fusion.3.base_ref, s32[512,1]{1,0:T(8,128)S(1)} %reshape.231.order_ref, f32[128,512]{1,0:T(8,128)S(1)} %correlate.1.mine_ref, f32[128,512]{1,0:T(8,128)S(1)} %collective-permute-done.8.other_ref, bf16[2,128,128]{2,1,0:T(8,128)(2,1)S(1)} %add_convert_fusion.counts_ref), custom_call_target="tpu_custom_call" | custom-call | tf_op jit(solution)/shard_map/arrange/pallas_call | solution.py:254
  45.8 23.3 %all_to_all.11 = bf16[64,8,640]{2,1,0:T(8,128)(2,1)S(1)} all-to-all(bf16[64,8,640]{2,1,0:T(8,128)(2,1)S(1)} %bitcast.15), channel_id=1, replica_groups={{0,2,4,6,8,10,12,14,16,18,20,22,24,26,28,30,32,34,36,38,40,42,44,46,48,..., dimensions={0} | all-to-all | bytes 1310720 | tf_op jit(solution)/shard_map/all_to_all | solution.py:332
  69.2 0.8 %finish.1 = f32[8,512]{1,0:T(8,128)} custom-call(bf16[512,640]{1,0:T(8,128)(2,1)S(1)} %bitcast.16), custom_call_target="tpu_custom_call" | custom-call | tf_op jit(solution)/shard_map/finish/pallas_call | solution.py:271
  (10 shorter events, 0.1 us)
Async XLA Ops:
  0.0 30.3 %copy-start = (bf16[2,512,768]{2,1,0:T(8,128)(2,1)S(1)}, bf16[2,512,768]{2,1,0:T(8,128)(2,1)}, u32[]{:S(2)}) copy-start(bf16[2,512,768]{2,1,0:T(8,128)(2,1)} %constant.119.clone.w_ref) | copy-start | bytes 4718596
  1.7 4.4 %collective-permute-start = (s32[128,128]{1,0:T(8,128)S(1)}, s32[128,128]{1,0:T(8,128)S(1)}, u32[]{:S(2)}, u32[]{:S(2)}) collective-permute-start(s32[128,128]{1,0:T(8,128)S(1)} %get-tuple-element.14), channel_id=1, source_target_pairs={{0,1},{1,0},{2,3},{3,2},{4,5},{5,4},{6,7},{7,6},{8,9},{9,8},{10,11... | collective-permute-start | bytes 196616 | tf_op jit(solution)/shard_map/ppermute | solution.py:293
  4.4 25.9 %copy-start.1 = (bf16[128,512]{1,0:T(8,128)(2,1)S(1)}, bf16[128,512]{1,0:T(8,128)(2,1)}, u32[]{:S(2)}) copy-start(bf16[128,512]{1,0:T(8,128)(2,1)} %prefilter.1.mine_ref) | copy-start | bytes 393220
  4.4 9.3 %collective-permute-start.2 = (bf16[128,512]{1,0:T(8,128)(2,1)}, bf16[128,512]{1,0:T(8,128)(2,1)S(1)}, u32[]{:S(2)}, u32[]{:S(2)}) collective-permute-start(bf16[128,512]{1,0:T(8,128)(2,1)} %prefilter.1.mine_ref), channel_id=1, source_target_pairs={{0,1},{1,0},{2,3},{3,2},{4,5},{5,4},{6,7},{7,6},{8,9},{9,8},{10,11... | collective-permute-start | bytes 393224 | tf_op jit(solution)/shard_map/ppermute | solution.py:296
  12.0 1.2 %collective-permute-start.1 = (s32[129]{0:T(256)S(1)}, s32[129]{0:T(256)S(1)}, u32[]{:S(2)}, u32[]{:S(2)}) collective-permute-start(s32[129]{0:T(256)S(1)} %pad_add_fusion.1), channel_id=1, source_target_pairs={{0,1},{1,0},{2,3},{3,2},{4,5},{5,4},{6,7},{7,6},{8,9},{9,8},{10,11... | collective-permute-start | bytes 1556 | tf_op jit(solution)/shard_map/ppermute | solution.py:315
  13.7 19.1 %copy-start.2 = (bf16[2,768,512]{2,1,0:T(8,128)(2,1)S(1)}, bf16[2,768,512]{2,1,0:T(8,128)(2,1)}, u32[]{:S(2)}) copy-start(bf16[2,768,512]{2,1,0:T(8,128)(2,1)} %constant.120.clone.back_ref) | copy-start | bytes 4718596
  14.8 7.7 %collective-permute-start.4 = (bf16[128,512]{1,0:T(8,128)(2,1)S(1)}, bf16[128,512]{1,0:T(8,128)(2,1)S(1)}, u32[]{:S(2)}, u32[]{:S(2)}) collective-permute-start(bf16[128,512]{1,0:T(8,128)(2,1)S(1)} %broadcast_select_fusion), channel_id=1, source_target_pairs={{0,4},{17,21},{36,32},{53,49},{72,76},{89,93},{108,104},{125,121}} | collective-permute-start | bytes 393224 | tf_op jit(solution)/shard_map/ppermute | solution.py:299
  20.0 3.9 %collective-permute-start.3 = (bf16[128,512]{1,0:T(8,128)(2,1)S(1)}, bf16[128,512]{1,0:T(8,128)(2,1)S(1)}, u32[]{:S(2)}, u32[]{:S(2)}) collective-permute-start(bf16[128,512]{1,0:T(8,128)(2,1)S(1)} %broadcast_select_fusion), channel_id=1, source_target_pairs={{0,2},{1,6},{17,19},{16,23},{36,38},{37,34},{53,55},{52,51},{72,74... | collective-permute-start | bytes 393224 | tf_op jit(solution)/shard_map/ppermute | solution.py:299
  23.9 7.1 %collective-permute-start.7 = (bf16[128,512]{1,0:T(8,128)(2,1)S(1)}, bf16[128,512]{1,0:T(8,128)(2,1)S(1)}, u32[]{:S(2)}, u32[]{:S(2)}) collective-permute-start(bf16[128,512]{1,0:T(8,128)(2,1)S(1)} %add_select_fusion.held_ref), channel_id=1, source_target_pairs={{0,16},{2,18},{4,20},{6,22},{17,1},{19,3},{21,5},{23,7},{32,48},{3... | collective-permute-start | bytes 393224 | tf_op jit(solution)/shard_map/ppermute | solution.py:301
  27.7 3.8 %collective-permute-start.6 = (bf16[128,512]{1,0:T(8,128)(2,1)S(1)}, bf16[128,512]{1,0:T(8,128)(2,1)S(1)}, u32[]{:S(2)}, u32[]{:S(2)}) collective-permute-start(bf16[128,512]{1,0:T(8,128)(2,1)S(1)} %add_select_fusion.held_ref), channel_id=1, source_target_pairs={{0,24},{2,26},{4,28},{6,30},{17,9},{19,11},{21,13},{23,15},{32,56}... | collective-permute-start | bytes 393224 | tf_op jit(solution)/shard_map/ppermute | solution.py:301
  29.0 3.8 %collective-permute-start.5 = (bf16[128,512]{1,0:T(8,128)(2,1)S(1)}, bf16[128,512]{1,0:T(8,128)(2,1)S(1)}, u32[]{:S(2)}, u32[]{:S(2)}) collective-permute-start(bf16[128,512]{1,0:T(8,128)(2,1)S(1)} %add_select_fusion.held_ref), channel_id=1, source_target_pairs={{0,8},{2,10},{4,12},{6,14},{17,25},{19,27},{21,29},{23,31},{32,40}... | collective-permute-start | bytes 393224 | tf_op jit(solution)/shard_map/ppermute | solution.py:301
  42.9 1.6 %collective-permute-start.8 = (f32[128,512]{1,0:T(8,128)S(1)}, f32[128,512]{1,0:T(8,128)S(1)}, u32[]{:S(2)}, u32[]{:S(2)}) collective-permute-start(f32[128,512]{1,0:T(8,128)S(1)} %correlate.1.mine_ref), channel_id=1, source_target_pairs={{0,1},{1,0},{2,3},{3,2},{4,5},{5,4},{6,7},{7,6},{8,9},{9,8},{10,11... | collective-permute-start | bytes 786440 | tf_op jit(solution)/shard_map/ppermute | solution.py:329

commit v2 on v1

v2 whole, which is shorter than its diff:
```python
import functools

import jax
import jax.numpy as jnp
import numpy as np
from jax import lax
from jax.experimental import pallas as pl
from jax.experimental.pallas import tpu as pltpu
from jax.sharding import PartitionSpec as P

LAGS = 512
SAMPLES = 512
TAPS = 32
FREQS = 384
PERIOD = 2 * FREQS
CH = 128
GROUP = 16
SPAN = 72
WIN = 128
LIMIT = 16 * 1024 * 1024
RING = 4
BF = jnp.bfloat16
F32 = jnp.float32


def split_bf16(matrix):
    high = matrix.astype(np.float32).astype(jnp.bfloat16)
    low = (matrix - high.astype(np.float64)).astype(np.float32).astype(jnp.bfloat16)
    return np.stack([high, low])


@functools.lru_cache(None)
def transforms():
    odd = 2 * np.arange(FREQS) + 1
    t = np.arange(SAMPLES)
    angle = np.pi / PERIOD * ((t[:, None] * odd[None, :]) % (2 * PERIOD))
    forward = np.stack([np.cos(angle), -np.sin(angle)], axis=1).reshape(SAMPLES, 2, -1, 128)
    forward = forward.transpose(0, 2, 1, 3).reshape(SAMPLES, PERIOD)
    lag = np.arange(LAGS) - LAGS // 2
    angle = np.pi / PERIOD * ((odd[:, None] * lag[None, :]) % (2 * PERIOD))
    back = np.stack([np.cos(angle), -np.sin(angle)], axis=0).reshape(2, -1, 128, LAGS)
    back = back.transpose(1, 0, 2, 3).reshape(PERIOD, LAGS) * (2.0 / PERIOD)
    return split_bf16(forward), split_bf16(back)


def device(src, z, y, core):
    return src * 32 + (z % RING) * 8 + (y % RING) * 2 + core


def owners():
    for s in range(4):
        for k in range(2):
            yield s, k, 2 * (s % 2), 2 * k + s // 2


def plans():
    across, up, along = [[], []], [[], []], []
    for s, k, y, z in owners():
        across[0].append((device(s, z, y, 0), device(s, z, y + 2, k)))
        across[1].append((device(s, z, y, 0), device(s, z, y - 1, k)))
        across[1].append((device(s, z, y, 1), device(s, z, y + 1, k)))
        up[0].append((device(s, z, y, 0), device(s, z + 2, y, k)))
        up[1].append((device(s, z, y, 0), device(s, z - 1, y, k)))
        up[1].append((device(s, z, y, 1), device(s, z + 1, y, k)))
    for d in (2, 1, 3):
        along.append(
            [
                (device(s, z, y + yy, k), device(s, z + d, y + yy, k))
                for s, k, y, z in owners()
                for yy in range(1, RING)
            ]
        )
    return across, up, along


def in_hbm(value):
    return pltpu.with_memory_space_constraint(value, pltpu.HBM)


def vmem(n):
    return [pl.BlockSpec(memory_space=pltpu.VMEM)] * n


def prefilter_kernel(traces_ref, band_ref, filters_ref, out_ref, pad_ref):
    bands = filters_ref.shape[0]
    onehot = (lax.broadcasted_iota(jnp.int32, (bands, CH), 0) == band_ref[...]).astype(F32)
    taps = lax.dot_general(
        filters_ref[...],
        onehot,
        (((0,), (0,)), ((), ())),
        precision=lax.Precision.HIGHEST,
        preferred_element_type=F32,
    )
    pad_ref[0:TAPS, :] = jnp.zeros((TAPS, CH), F32)
    pad_ref[TAPS:, :] = traces_ref[...].astype(F32).T
    rows = 128
    power = jnp.zeros((1, CH), F32)
    parts = []
    for start in range(0, SAMPLES, rows):
        total = jnp.zeros((rows, CH), F32)
        for k in range(TAPS):
            low = TAPS + start - k
            total = total + taps[k : k + 1, :] * pad_ref[low : low + rows, :]
        power = power + jnp.sum(total * total, axis=0, keepdims=True)
        parts.append(total)
    scale = lax.rsqrt(power * (1.0 / SAMPLES) + 1e-06)
    for i, total in enumerate(parts):
        out_ref[:, i * rows : (i + 1) * rows] = (total * scale).T.astype(BF)


def prefilter(traces, band_group, filters):
    return pl.pallas_call(
        prefilter_kernel,
        out_shape=pltpu.VMEM((CH, SAMPLES), BF),
        in_specs=vmem(3),
        out_specs=pl.BlockSpec(memory_space=pltpu.VMEM),
        scratch_shapes=[pltpu.VMEM((TAPS + SAMPLES, CH), F32)],
        name="prefilter",
    )(traces, band_group.reshape(1, CH), filters)


def correlate_kernel(
    scalars, low_ref, held_ref, r0, r1, r2, r3, r4, w_ref, fc_ref, bins_ref, hot_ref, back_ref, out_ref,
    fs, total, wide,
):
    held = held_ref[...].astype(F32) * scalars[2].astype(F32)
    rest = (r0[...] + r1[...]) + (r2[...] + r3[...]) + r4[...]
    block = (held + rest.astype(F32)).astype(BF)
    fs[...] = jnp.dot(block, w_ref[0], preferred_element_type=F32) + jnp.dot(
        block, w_ref[1], preferred_element_type=F32
    )
    total[...] = jnp.zeros_like(total)
    n_groups = CH // GROUP

    def spread(hot, j):
        return jnp.dot(hot, fc_ref[:, j * 256 : (j + 1) * 256], preferred_element_type=F32)

    def gather(g, j, span, buffer):
        first = pl.multiple_of(g * GROUP, GROUP)
        low = low_ref[g, 0]
        shift = low % 8
        start = pl.multiple_of(low - shift, 8)
        room = jnp.zeros((8, 128), F32)
        re, im = slice(j * 256, j * 256 + 128), slice(j * 256 + 128, (j + 1) * 256)
        fr, fi = fs[pl.ds(first, GROUP), re], fs[pl.ds(first, GROUP), im]
        sum_re = jnp.zeros((span, 128), F32)
        sum_im = jnp.zeros((span, 128), F32)
        for p in range(GROUP):
            rows = slice(p * span, (p + 1) * span)
            gr, gi = buffer[rows, 0:128], buffer[rows, 128:256]
            a, b = fr[p : p + 1, :], fi[p : p + 1, :]
            sum_re = sum_re + (a * gr + b * gi)
            sum_im = sum_im + (a * gi - b * gr)
        for part, value in ((re, sum_re), (im, sum_im)):
            moved = pltpu.roll(jnp.concatenate([value, room], axis=0), shift, 0)
            total[pl.ds(start, span + 8), part] += moved

    fits = low_ref[n_groups, 0] == 1

    @pl.when(fits)
    def _():
        def body(g, carry):
            for j in range(3):
                gather(g, j, SPAN, spread(hot_ref[g], j))
            return carry

        lax.fori_loop(0, n_groups, body, 0)

    @pl.when(jnp.logical_not(fits))
    def _():
        offsets = lax.broadcasted_iota(jnp.int32, (WIN, 2 * CH), 0)

        def body(g, carry):
            rel = bins_ref[pl.ds(pl.multiple_of(g * GROUP, GROUP), GROUP), :]
            for p in range(GROUP):
                row = jnp.where(rel[p : p + 1, :] == offsets, 1.0, 0.0)
                wide[p * WIN : (p + 1) * WIN, :] = row.astype(BF)
            for j in range(3):
                gather(g, j, WIN, spread(wide[...], j))
            return carry

        lax.fori_loop(0, n_groups, body, 0)

    for start in range(0, WIN, 128):
        value = total[start : start + 128, :]
        high = value.astype(BF)
        low = (value - high.astype(F32)).astype(BF)
        value = (
            jnp.dot(high, back_ref[0], preferred_element_type=F32)
            + jnp.dot(low, back_ref[0], preferred_element_type=F32)
            + jnp.dot(high, back_ref[1], preferred_element_type=F32)
        )
        out_ref[start : start + 128, :] = value.astype(BF)


def correlate(scalars, lows, held, parts, w, fc, bins, hot, back):
    return pl.pallas_call(
        correlate_kernel,
        out_shape=jax.ShapeDtypeStruct((WIN, LAGS), BF),
        in_specs=[pl.BlockSpec(memory_space=pltpu.SMEM)] * 2 + vmem(11),
        out_specs=pl.BlockSpec(memory_space=pltpu.VMEM),
        scratch_shapes=[
            pltpu.VMEM((CH, PERIOD), F32),
            pltpu.VMEM((2 * WIN, PERIOD), F32),
            pltpu.VMEM((GROUP * WIN, 2 * CH), BF),
        ],
        compiler_params=pltpu.CompilerParams(vmem_limit_bytes=LIMIT),
        cost_estimate=pl.CostEstimate(
            flops=2 * 128 * SPAN * 256 * PERIOD, bytes_accessed=6 * 1024 * 1024, transcendentals=0
        ),
        name="correlate",
    )(scalars, lows, held, *parts, w, fc, bins, hot, back)


def survey_kernel(
    scalars, pair_ref, other_ref, mine_ref, partner_ref, w_ref, bins_ref, table_ref, fc_ref, flag_ref,
    raw, w, sems,
):
    core = scalars[0]
    copies = [pltpu.make_async_copy(pair_ref.at[core], raw, sems.at[0])] + [
        pltpu.make_async_copy(w_ref.at[i, pl.ds(j, 128)], w.at[i, pl.ds(j, 128)], sems.at[1 + 4 * i + j // 128])
        for i in range(2)
        for j in range(0, SAMPLES, 128)
    ]
    for copy in copies:
        copy.start()
    flag_ref[...] = jnp.full(flag_ref.shape, scalars[1], jnp.int32)
    copies[0].wait()
    bins = jnp.concatenate([raw[...], other_ref[core]], axis=1)
    lowest = jnp.min(jnp.min(bins, axis=0, keepdims=True), axis=1, keepdims=True)
    rel = bins - lowest
    bins_ref[...] = rel
    n_groups = CH // GROUP
    grouped = rel.reshape(n_groups, GROUP, 2 * CH)
    low = jnp.min(jnp.min(grouped, axis=1), axis=1, keepdims=True)
    high = jnp.max(jnp.max(grouped, axis=1), axis=1, keepdims=True)
    widest = jnp.max(high - low, axis=0, keepdims=True)
    fits = (widest < SPAN).astype(jnp.int32)
    low = jnp.minimum(low * fits, WIN)
    table_ref[0:n_groups, :] = jnp.broadcast_to(low, (n_groups, 128))
    table_ref[n_groups:, :] = jnp.broadcast_to(fits, (8, 128))
    for copy in copies[1:]:
        copy.wait()
    for i, ref in enumerate((mine_ref, partner_ref)):
        value = jnp.dot(ref[...], w[0], preferred_element_type=F32)
        value = value + jnp.dot(ref[...], w[1], preferred_element_type=F32)
        fc_ref[i * CH : (i + 1) * CH, :] = value.astype(BF)


def survey(scalars, pair, other, mine, partner, w):
    whole = pl.BlockSpec(memory_space=pltpu.VMEM)
    far = pl.BlockSpec(memory_space=pltpu.HBM)
    return pl.pallas_call(
        survey_kernel,
        out_shape=[
            pltpu.VMEM((CH, 2 * CH), jnp.int32),
            jax.ShapeDtypeStruct((CH // GROUP + 8, 128), jnp.int32),
            pltpu.VMEM((2 * CH, PERIOD), BF),
            pltpu.VMEM((8, SAMPLES), jnp.int32),
        ],
        in_specs=[pl.BlockSpec(memory_space=pltpu.SMEM), far] + vmem(3) + [far],
        out_specs=[whole] * 4,
        scratch_shapes=[
            pltpu.VMEM((CH, CH), jnp.int32),
            pltpu.VMEM((2, SAMPLES, PERIOD), BF),
            pltpu.SemaphoreType.DMA((9,)),
        ],
        compiler_params=pltpu.CompilerParams(vmem_limit_bytes=LIMIT),
        cost_estimate=pl.CostEstimate(
            flops=2 * 2 * 2 * CH * SAMPLES * PERIOD, bytes_accessed=2 * 1024 * 1024, transcendentals=0
        ),
        name="survey",
    )(scalars, in_hbm(pair), other, mine, partner, in_hbm(w))


def prepare_kernel(
    scalars, low_ref, order_ref, pair_ref, other_ref, bins_ref, after_ref, hot_ref, pick_ref, tally_ref,
    words, ranks,
):
    core = scalars[0]
    columns = lax.broadcasted_iota(jnp.int32, (512, WIN), 1)
    lane = lax.broadcasted_iota(jnp.int32, (WIN, 128), 1)
    turned = jnp.concatenate([order_ref[...], jnp.zeros((120, 128), jnp.int32)], axis=0).T
    ranks[...] = turned.reshape(8, 2, 8, 128)
    half = ranks[:, core].reshape(64, 128)
    order = jnp.concatenate([half[:, a : a + 1] for a in range(8)], axis=0)
    tally = jnp.zeros((512, 128), F32)
    for i in range(2):
        step = core if i == 0 else 1 - core
        bins = jnp.concatenate([pair_ref[step], other_ref[step]], axis=1)
        lowest = jnp.min(jnp.min(bins, axis=0, keepdims=True), axis=1, keepdims=True)
        rel = bins - lowest
        place = rel % 32
        unit = jnp.left_shift(1, rel // 32 * 8)

        def body(j, carry):
            hit = jnp.where(place == j, unit, 0)
            hit = hit[:, :CH] + hit[:, CH:]
            pieces = [hit[q : q + 8] for q in range(0, CH, 8)]
            while len(pieces) > 1:
                pieces = [x + y for x, y in zip(pieces[::2], pieces[1::2])]
            words[pl.ds(pl.multiple_of(j * 8, 8), 8), :] = pieces[0]
            return carry

        lax.fori_loop(0, 32, body, 0, unroll=4)
        packed = words[...]
        pieces = []
        for q in range(WIN // 32):
            part = jnp.bitwise_and(jnp.right_shift(packed, 8 * q), 255)
            part = jnp.sum(part.reshape(32, 8, CH), axis=1)
            pieces.append(jnp.sum(part, axis=1, keepdims=True))
        counts = jnp.concatenate(pieces, axis=0)
        pick = jnp.where(order - lowest == columns, 1.0, 0.0).astype(BF)
        pick_ref[:, i * WIN : (i + 1) * WIN] = pick
        parts = jnp.where(lane == 2 * i, counts - counts % 256, 0)
        parts = parts + jnp.where(lane == 2 * i + 1, counts % 256, 0)
        tally = tally + jnp.dot(pick, parts.astype(F32).astype(BF), preferred_element_type=F32)
    tally_ref[...] = tally.astype(BF)

    offsets = lax.broadcasted_iota(jnp.int32, (SPAN, 2 * CH), 0)

    def mark(g, carry):
        rel = bins_ref[pl.ds(pl.multiple_of(g * GROUP, GROUP), GROUP), :] - low_ref[g, 0]
        for p in range(0, GROUP, 2):
            hot_ref[g, p * SPAN : (p + 2) * SPAN, :] = jnp.concatenate(
                [jnp.where(rel[q : q + 1, :] == offsets, 1.0, 0.0) for q in (p, p + 1)], axis=0
            ).astype(BF)
        return carry

    lax.fori_loop(0, CH // GROUP, mark, 0)


def prepare(scalars, lows, order, pair, other, bins, after):
    return pl.pallas_call(
        prepare_kernel,
        out_shape=[
            pltpu.VMEM((CH // GROUP, GROUP * SPAN, 2 * CH), BF),
            pltpu.VMEM((512, 2 * WIN), BF),
            pltpu.VMEM((512, 128), BF),
        ],
        in_specs=[pl.BlockSpec(memory_space=pltpu.SMEM)] * 2 + vmem(4) + [pl.BlockSpec(memory_space=pl.ANY)],
        out_specs=vmem(3),
        scratch_shapes=[pltpu.VMEM((32 * 8, CH), jnp.int32), pltpu.VMEM((8, 2, 8, 128), jnp.int32)],
        compiler_params=pltpu.CompilerParams(vmem_limit_bytes=LIMIT),
        cost_estimate=pl.CostEstimate(flops=10**9, bytes_accessed=2**20, transcendentals=0),
        name="prepare",
    )(scalars, lows, order, pair, other, bins, after)


def arrange_kernel(pick_ref, tally_ref, mine_ref, other_ref, out_ref):
    window = jnp.concatenate([mine_ref[...], other_ref[...]], axis=0)
    result = jnp.dot(pick_ref[...], window, preferred_element_type=F32)
    out_ref[:, :LAGS] = result.astype(BF)
    out_ref[:, LAGS:] = tally_ref[...]


def arrange(pick, tally, mine, other):
    return pl.pallas_call(
        arrange_kernel,
        out_shape=jax.ShapeDtypeStruct((512, LAGS + 128), BF),
        in_specs=vmem(4),
        out_specs=pl.BlockSpec(memory_space=pltpu.VMEM),
        compiler_params=pltpu.CompilerParams(vmem_limit_bytes=LIMIT),
        name="arrange",
    )(pick, tally, mine, other)


def finish_kernel(parts_ref, out_ref):
    value = jnp.sum(parts_ref[...].astype(F32).reshape(64, 8, LAGS + 128), axis=0)
    totals = jnp.sum(value[:, LAGS:], axis=1, keepdims=True)
    out_ref[...] = value[:, :LAGS] / jnp.sqrt(SAMPLES * totals)


def finish(parts):
    return pl.pallas_call(
        finish_kernel,
        out_shape=jax.ShapeDtypeStruct((8, LAGS), F32),
        in_specs=vmem(1),
        out_specs=pl.BlockSpec(memory_space=pltpu.VMEM),
        compiler_params=pltpu.CompilerParams(vmem_limit_bytes=LIMIT),
        name="finish",
    )(parts)


def shards(traces, band_group, filters, pair_bin, bin_order):
    both = ("src", "rcv")
    swap = [(i, i ^ 1) for i in range(32)]
    forward, back = transforms()
    w, back = jnp.asarray(forward), jnp.asarray(back)
    src, rcv = lax.axis_index("src"), lax.axis_index("rcv")
    core = rcv % 2
    y, z = (rcv // 2) % RING, rcv // 8
    root = jnp.logical_and(y == 2 * (src % 2), z % 2 == src // 2)
    keep = jnp.logical_or(jnp.logical_not(root), z // 2 == core)
    scalars = jnp.stack([core, root.astype(jnp.int32), keep.astype(jnp.int32)])

    across, up, along = plans()
    other_pair = lax.ppermute(pair_bin, "rcv", swap)
    filtered = prefilter(traces, band_group, filters)
    filtered, other_pair = lax.optimization_barrier((filtered, other_pair))
    got = lax.ppermute(filtered, both, across[0])
    partner = lax.ppermute(filtered, "rcv", swap)
    seed = jnp.where(core == 0, filtered, partner)
    got = got + lax.ppermute(seed, both, across[1])
    parts = [lax.ppermute(seed, both, plan) for plan in up]
    bins, table, fc, flag = survey(scalars, pair_bin, other_pair, filtered, partner, w)
    held = jnp.where(flag[0:1] == 1, seed, got)
    parts = parts + [lax.ppermute(held, both, plan) for plan in along]
    hot, pick, tally = prepare(
        scalars, table, bin_order.reshape(8, 128), pair_bin, other_pair, bins, held
    )

    window = correlate(scalars, table, held, parts, w, fc, bins, hot, back)
    other_window = lax.ppermute(window, "rcv", swap)
    payload = arrange(pick, tally, window, other_window)
    groups = [[2 * i + c for i in range(64)] for c in range(2)]
    arrived = lax.all_to_all(payload, both, 0, 0, tiled=True, axis_index_groups=groups)
    return finish(arrived)


def solution(mesh):
    in_specs = (P("rcv", None), P("rcv"), P(), P(None, "src", "rcv"), P())
    out_specs = P(("src", "rcv"), None)
    return jax.shard_map(shards, mesh=mesh, in_specs=in_specs, out_specs=out_specs, check_vma=False)
```

time: 70.3 us -> 56.2 us (0.80)
  other arithmetic: 7.54 us -> 0.14 us
  waiting for transfers between devices: 6.21 us -> 1.36 us
  blocking collectives: 23.3 us -> 20.7 us
  starting transfers between devices: 13.6 us -> 16 us
  Pallas kernels: 15.4 us -> 17.4 us
  between operations: 2.03 us -> 0.23 us
  local copies, waits for them, and re-layouts: 1.8 us -> 0.02 us
    pallas_call x2 -> x3, Pallas kernels: 3.26 us -> 8.75 us  [the longest x1 4.02 us: prepare(): pl.pallas_call(prepare_kernel, out_shape=[pltpu.VMEM((CH // GROUP, GROUP...]
    ppermute x7 -> x8, waiting for transfers between devices: 5.46 us -> 0.02 us  [the longest x3 0.01 us: shards(): parts = parts + [lax.ppermute(held, both, plan) for plan in along]]
    all_to_all x1, blocking collectives: 23.3 us -> 20.7 us  [shards(): lax.all_to_all(payload, both, 0, 0, tiled=True, axis_index_groups=groups)]
    reduce_min x4 -> x0, other arithmetic: 2.49 us -> none  [shards(): lows, highs = (jnp.min(grouped, axis=1), jnp.max(grouped, axis=1))]
    pallas_call x1, Pallas kernels: 10 us -> 7.61 us  [correlate(): pl.pallas_call(correlate_kernel, out_shape=jax.ShapeDtypeStruct((WIN, LAG...]
    ppermute x7 -> x8, starting transfers between devices: 13 us -> 15.3 us  [the longest x2 6.82 us: shards(): parts = [lax.ppermute(seed, both, plan) for plan in up]]
    reduce_sum x1 -> x0, other arithmetic: 1.7 us -> none  [shards(): jnp.sum((bins.reshape(1, -1) - lowest == jnp.arange(WIN, dtype=jnp.int32)...]
    pallas_call x1, Pallas kernels: 1.36 us -> 0.29 us  [arrange(): pl.pallas_call(arrange_kernel, out_shape=jax.ShapeDtypeStruct((512, LAGS...]
  transfers between devices with their start and end apart: 9 -> 10, of which waited for: 6 -> 1; matrix products, arithmetic and copies ran while one was open for 9% -> 0% of each run, Pallas kernels for 5% -> 16%
where the time goes in v2:
time: 56.2 us; the launch traced here: 55.9 us
  blocking collectives  20.7 us (37%)
  Pallas kernels  17.4 us (31%)
  starting transfers between devices  16 us (28%)
  waiting for transfers between devices  1.36 us (2%)
    all_to_all x1, blocking collectives, shards(): lax.all_to_all(payload, both, 0, 0, tiled=True, axis_index_groups=groups)  20.7 us
    pallas_call x1, Pallas kernels, correlate(): pl.pallas_call(correlate_kernel, out_shape=jax.ShapeDtypeStruct((WIN, LAG...  7.61 us
    ppermute x2, starting transfers between devices, shards(): parts = [lax.ppermute(seed, both, plan) for plan in up]  6.82 us
    ppermute x1, starting transfers between devices, shards(): got = lax.ppermute(filtered, both, across[0])  5.18 us
    pallas_call x1, Pallas kernels, prepare(): pl.pallas_call(prepare_kernel, out_shape=[pltpu.VMEM((CH // GROUP, GROUP...  4.02 us
    pallas_call x1, Pallas kernels, survey(): pl.pallas_call(survey_kernel, out_shape=[pltpu.VMEM((CH, 2 * CH), jnp.int...  2.69 us
    pallas_call x1, Pallas kernels, prefilter(): pl.pallas_call(prefilter_kernel, out_shape=pltpu.VMEM((CH, SAMPLES), BF),...  2.04 us
    ppermute x3, starting transfers between devices, shards(): parts = parts + [lax.ppermute(held, both, plan) for plan in along]  2.01 us
  transfers between devices with their start and end apart: 10, of which 1 were waited for; matrix products, arithmetic and copies ran while one was open for 0% of the time, Pallas kernels for 16%

profile of v2, /device:TPU:0, one launch (start us, length us, event | category | flops | bytes accessed | tf_op | source)
XLA Modules:
  0.0 55.9 jit_solution(8449784338656367951)
XLA Ops:
  0.0 0.0 collective-permute-start
  0.0 2.0 %prefilter.1.mine_ref = bf16[128,512]{1,0:T(8,128)(2,1)S(1)} custom-call(bf16[128,512]{1,0:T(8,128)(2,1)} %traces_ref.1, s32[1,128]{1,0:T(1,128)} %bitcast.10, f32[24,32]{1,0:T(8,128)} %filters_ref.1), custom_call_target="tpu_custom_call" | custom-call | tf_op jit(solution)/shard_map/prefilter/pallas_call | solution.py:112
  2.0 0.0 collective-permute-done.other_ref
  2.1 0.6 %collective-permute-start.1 = (bf16[128,512]{1,0:T(8,128)(2,1)S(1)}, bf16[128,512]{1,0:T(8,128)(2,1)S(1)}, u32[]{:S(2)}, u32[]{:S(2)}) collective-permute-start(bf16[128,512]{1,0:T(8,128)(2,1)S(1)} %prefilter.1.mine_ref), channel_id=1, source_target_pairs={{0,1},{1,0},{2,3},{3,2},{4,5},{5,4},{6,7},{7,6},{8,9},{9,8},{10,11... | collective-permute-start | bytes 393224 | tf_op jit(solution)/shard_map/ppermute | solution.py:402
  2.6 0.0 copy-start.1
  2.6 0.0 copy-start.2
  2.7 0.1 pad_add_fusion.scalars
  2.7 5.2 %collective-permute-start.2 = (bf16[128,512]{1,0:T(8,128)(2,1)S(1)}, bf16[128,512]{1,0:T(8,128)(2,1)S(1)}, u32[]{:S(2)}, u32[]{:S(2)}) collective-permute-start(bf16[128,512]{1,0:T(8,128)(2,1)S(1)} %prefilter.1.mine_ref), channel_id=1, source_target_pairs={{0,4},{16,21},{36,32},{52,49},{72,76},{88,93},{108,104},{124,121}} | collective-permute-start | bytes 393224 | tf_op jit(solution)/shard_map/ppermute | solution.py:401
  7.9 0.0 collective-permute-done.1.partner_ref
  7.9 1.3 %collective-permute-start.3 = (bf16[128,512]{1,0:T(8,128)(2,1)S(1)}, bf16[128,512]{1,0:T(8,128)(2,1)S(1)}, u32[]{:S(2)}, u32[]{:S(2)}) collective-permute-start(bf16[128,512]{1,0:T(8,128)(2,1)S(1)} %broadcast_select_fusion), channel_id=1, source_target_pairs={{0,6},{1,2},{16,23},{17,19},{36,34},{37,38},{52,51},{53,55},{72,78... | collective-permute-start | bytes 393224 | tf_op jit(solution)/shard_map/ppermute | solution.py:404
  9.3 5.5 %collective-permute-start.4 = (bf16[128,512]{1,0:T(8,128)(2,1)S(1)}, bf16[128,512]{1,0:T(8,128)(2,1)S(1)}, u32[]{:S(2)}, u32[]{:S(2)}) collective-permute-start(bf16[128,512]{1,0:T(8,128)(2,1)S(1)} %broadcast_select_fusion), channel_id=1, source_target_pairs={{0,16},{16,1},{36,52},{52,37},{72,88},{88,73},{108,124},{124,109}} | collective-permute-start | bytes 393224 | tf_op jit(solution)/shard_map/ppermute | solution.py:405
  14.8 1.3 %collective-permute-start.5 = (bf16[128,512]{1,0:T(8,128)(2,1)S(1)}, bf16[128,512]{1,0:T(8,128)(2,1)S(1)}, u32[]{:S(2)}, u32[]{:S(2)}) collective-permute-start(bf16[128,512]{1,0:T(8,128)(2,1)S(1)} %broadcast_select_fusion), channel_id=1, source_target_pairs={{0,24},{1,8},{16,9},{17,25},{36,60},{37,44},{52,45},{53,61},{72,64... | collective-permute-start | bytes 393224 | tf_op jit(solution)/shard_map/ppermute | solution.py:405
  16.1 2.7 %survey.1 = (s32[128,256]{1,0:T(8,128)S(1)}, s32[16,128]{1,0:T(8,128)S(1)}, bf16[256,768]{1,0:T(8,128)(2,1)S(1)}, s32[8,512]{1,0:T(8,128)S(1)}) custom-call(s32[3]{0:T(128)S(1)} %pad_add_fusion.scalars, s32[2,128,128]{2,1,0:T(8,128)} %pair_ref.3, s32[2,128,128]{2,1,0:T(8,128)S(1)} %collective-permute-done.other_ref, bf16[128,512]{1,0:T(8,128)(2,1)S(1)} %prefilter.1.mine_ref, ...), custom_call_target="tpu_custom_call" | custom-call | flops 402653184 | bytes 2097152 | tf_op jit(solution)/shard_map/survey/pallas_call | solution.py:253
  18.8 0.0 collective-permute-done.2
  18.8 0.0 collective-permute-done.3
  18.9 0.7 %collective-permute-start.6 = (bf16[128,512]{1,0:T(8,128)(2,1)S(1)}, bf16[128,512]{1,0:T(8,128)(2,1)S(1)}, u32[]{:S(2)}, u32[]{:S(2)}) collective-permute-start(bf16[128,512]{1,0:T(8,128)(2,1)S(1)} %add_select_fusion.after_ref.held_ref), channel_id=1, source_target_pairs={{2,18},{4,20},{6,22},{19,3},{21,5},{23,7},{38,54},{32,48},{34,50},... | collective-permute-start | bytes 393224 | tf_op jit(solution)/shard_map/ppermute | solution.py:408
  19.5 0.7 %collective-permute-start.7 = (bf16[128,512]{1,0:T(8,128)(2,1)S(1)}, bf16[128,512]{1,0:T(8,128)(2,1)S(1)}, u32[]{:S(2)}, u32[]{:S(2)}) collective-permute-start(bf16[128,512]{1,0:T(8,128)(2,1)S(1)} %add_select_fusion.after_ref.held_ref), channel_id=1, source_target_pairs={{2,10},{4,12},{6,14},{19,27},{21,29},{23,31},{38,46},{32,40},{34,4... | collective-permute-start | bytes 393224 | tf_op jit(solution)/shard_map/ppermute | solution.py:408
  20.2 0.7 %collective-permute-start.8 = (bf16[128,512]{1,0:T(8,128)(2,1)S(1)}, bf16[128,512]{1,0:T(8,128)(2,1)S(1)}, u32[]{:S(2)}, u32[]{:S(2)}) collective-permute-start(bf16[128,512]{1,0:T(8,128)(2,1)S(1)} %add_select_fusion.after_ref.held_ref), channel_id=1, source_target_pairs={{2,26},{4,28},{6,30},{19,11},{21,13},{23,15},{38,62},{32,56},{34,5... | collective-permute-start | bytes 393224 | tf_op jit(solution)/shard_map/ppermute | solution.py:408
  20.9 0.0 copy-done.1
  20.9 0.0 copy-done.2
  20.9 0.0 copy-start
  20.9 0.0 copy-start.3
  20.9 4.0 %prepare.1 = (bf16[8,1152,256]{2,1,0:T(8,128)(2,1)S(1)}, bf16[512,256]{1,0:T(8,128)(2,1)S(1)}, bf16[512,128]{1,0:T(8,128)(2,1)S(1)}) custom-call(s32[3]{0:T(128)S(1)} %pad_add_fusion.scalars, s32[16,128]{1,0:T(8,128)S(1)} %get-tuple-element.16.low_ref, s32[8,128]{1,0:T(8,128)S(1)} %bitcast.9, s32[2,128,128]{2,1,0:T(8,128)S(1)} %copy-done.1, ...), custom_call_target="tpu_custom_call" | custom-call | flops 1000000000 | bytes 1048576 | tf_op jit(solution)/shard_map/prepare/pallas_call | solution.py:334
  25.0 0.0 collective-permute-done.4.r0
  25.0 0.0 collective-permute-done.5.r1
  25.0 0.0 collective-permute-done.6.r2
  25.0 0.0 collective-permute-done.7.r3
  25.0 0.0 collective-permute-done.8.r4
  25.0 0.0 copy-done
  25.0 0.0 copy-done.3
  25.0 7.6 %correlate.1.mine_ref = bf16[128,512]{1,0:T(8,128)(2,1)S(1)} custom-call(s32[3]{0:T(128)S(1)} %pad_add_fusion.scalars, s32[16,128]{1,0:T(8,128)S(1)} %get-tuple-element.16.low_ref, bf16[128,512]{1,0:T(8,128)(2,1)S(1)} %add_select_fusion.after_ref.held_ref, bf16[128,512]{1,0:T(8,128)(2,1)S(1)} %collective-permute-done.4.r0, ...), custom_call_target="tpu_custom_call" | custom-call | flops 3623878656 | bytes 6291456 | tf_op jit(solution)/shard_map/correlate/pallas_call | solution.py:197
  32.7 0.1 collective-permute-start.9
  32.7 1.3 %collective-permute-done.9.other_ref = bf16[128,512]{1,0:T(8,128)(2,1)S(1)} collective-permute-done((bf16[128,512]{1,0:T(8,128)(2,1)S(1)}, bf16[128,512]{1,0:T(8,128)(2,1)S(1)}, u32[]{:S(2)}, u32[]{:S(2)}) %collective-permute-start.9) | collective-permute-done | bytes 131104 | tf_op jit(solution)/shard_map/ppermute | solution.py:414
  34.1 0.3 arrange.1
  34.4 20.7 %all_to_all.11 = bf16[64,8,640]{2,1,0:T(8,128)(2,1)S(1)} all-to-all(bf16[64,8,640]{2,1,0:T(8,128)(2,1)S(1)} %bitcast.7), channel_id=1, replica_groups={{0,2,4,6,8,10,12,14,16,18,20,22,24,26,28,30,32,34,36,38,40,42,44,46,48,..., dimensions={0} | all-to-all | bytes 1310720 | tf_op jit(solution)/shard_map/all_to_all | solution.py:417
  55.1 0.8 %finish.1 = f32[8,512]{1,0:T(8,128)} custom-call(bf16[512,640]{1,0:T(8,128)(2,1)S(1)} %bitcast.8), custom_call_target="tpu_custom_call" | custom-call | tf_op jit(solution)/shard_map/finish/pallas_call | solution.py:375
  (3 shorter events, 0.1 us)
Async XLA Ops:
  0.0 2.1 %collective-permute-start = (s32[2,128,128]{2,1,0:T(8,128)}, s32[2,128,128]{2,1,0:T(8,128)S(1)}, u32[]{:S(2)}, u32[]{:S(2)}) collective-permute-start(s32[2,128,128]{2,1,0:T(8,128)} %pair_ref.3), channel_id=1, source_target_pairs={{0,1},{1,0},{2,3},{3,2},{4,5},{5,4},{6,7},{7,6},{8,9},{9,8},{10,11... | collective-permute-start | bytes 393224 | tf_op jit(solution)/shard_map/ppermute | solution.py:398
  2.1 5.9 %collective-permute-start.1 = (bf16[128,512]{1,0:T(8,128)(2,1)S(1)}, bf16[128,512]{1,0:T(8,128)(2,1)S(1)}, u32[]{:S(2)}, u32[]{:S(2)}) collective-permute-start(bf16[128,512]{1,0:T(8,128)(2,1)S(1)} %prefilter.1.mine_ref), channel_id=1, source_target_pairs={{0,1},{1,0},{2,3},{3,2},{4,5},{5,4},{6,7},{7,6},{8,9},{9,8},{10,11... | collective-permute-start | bytes 393224 | tf_op jit(solution)/shard_map/ppermute | solution.py:402
  2.6 18.3 %copy-start.1 = (s32[2,128,128]{2,1,0:T(8,128)S(1)}, s32[2,128,128]{2,1,0:T(8,128)}, u32[]{:S(2)}) copy-start(s32[2,128,128]{2,1,0:T(8,128)} %pair_ref.3) | copy-start | bytes 393220
  2.6 18.3 %copy-start.2 = (s32[1024]{0:T(1024)S(1)}, s32[1024]{0:T(1024)}, u32[]{:S(2)}) copy-start(s32[1024]{0:T(1024)} %param.11) | copy-start | bytes 12292
  2.7 16.1 %collective-permute-start.2 = (bf16[128,512]{1,0:T(8,128)(2,1)S(1)}, bf16[128,512]{1,0:T(8,128)(2,1)S(1)}, u32[]{:S(2)}, u32[]{:S(2)}) collective-permute-start(bf16[128,512]{1,0:T(8,128)(2,1)S(1)} %prefilter.1.mine_ref), channel_id=1, source_target_pairs={{0,4},{16,21},{36,32},{52,49},{72,76},{88,93},{108,104},{124,121}} | collective-permute-start | bytes 393224 | tf_op jit(solution)/shard_map/ppermute | solution.py:401
  7.9 10.9 %collective-permute-start.3 = (bf16[128,512]{1,0:T(8,128)(2,1)S(1)}, bf16[128,512]{1,0:T(8,128)(2,1)S(1)}, u32[]{:S(2)}, u32[]{:S(2)}) collective-permute-start(bf16[128,512]{1,0:T(8,128)(2,1)S(1)} %broadcast_select_fusion), channel_id=1, source_target_pairs={{0,6},{1,2},{16,23},{17,19},{36,34},{37,38},{52,51},{53,55},{72,78... | collective-permute-start | bytes 393224 | tf_op jit(solution)/shard_map/ppermute | solution.py:404
  9.3 15.7 %collective-permute-start.4 = (bf16[128,512]{1,0:T(8,128)(2,1)S(1)}, bf16[128,512]{1,0:T(8,128)(2,1)S(1)}, u32[]{:S(2)}, u32[]{:S(2)}) collective-permute-start(bf16[128,512]{1,0:T(8,128)(2,1)S(1)} %broadcast_select_fusion), channel_id=1, source_target_pairs={{0,16},{16,1},{36,52},{52,37},{72,88},{88,73},{108,124},{124,109}} | collective-permute-start | bytes 393224 | tf_op jit(solution)/shard_map/ppermute | solution.py:405
  14.8 10.2 %collective-permute-start.5 = (bf16[128,512]{1,0:T(8,128)(2,1)S(1)}, bf16[128,512]{1,0:T(8,128)(2,1)S(1)}, u32[]{:S(2)}, u32[]{:S(2)}) collective-permute-start(bf16[128,512]{1,0:T(8,128)(2,1)S(1)} %broadcast_select_fusion), channel_id=1, source_target_pairs={{0,24},{1,8},{16,9},{17,25},{36,60},{37,44},{52,45},{53,61},{72,64... | collective-permute-start | bytes 393224 | tf_op jit(solution)/shard_map/ppermute | solution.py:405
  18.9 6.1 %collective-permute-start.6 = (bf16[128,512]{1,0:T(8,128)(2,1)S(1)}, bf16[128,512]{1,0:T(8,128)(2,1)S(1)}, u32[]{:S(2)}, u32[]{:S(2)}) collective-permute-start(bf16[128,512]{1,0:T(8,128)(2,1)S(1)} %add_select_fusion.after_ref.held_ref), channel_id=1, source_target_pairs={{2,18},{4,20},{6,22},{19,3},{21,5},{23,7},{38,54},{32,48},{34,50},... | collective-permute-start | bytes 393224 | tf_op jit(solution)/shard_map/ppermute | solution.py:408
  19.5 5.5 %collective-permute-start.7 = (bf16[128,512]{1,0:T(8,128)(2,1)S(1)}, bf16[128,512]{1,0:T(8,128)(2,1)S(1)}, u32[]{:S(2)}, u32[]{:S(2)}) collective-permute-start(bf16[128,512]{1,0:T(8,128)(2,1)S(1)} %add_select_fusion.after_ref.held_ref), channel_id=1, source_target_pairs={{2,10},{4,12},{6,14},{19,27},{21,29},{23,31},{38,46},{32,40},{34,4... | collective-permute-start | bytes 393224 | tf_op jit(solution)/shard_map/ppermute | solution.py:408
  20.2 4.8 %collective-permute-start.8 = (bf16[128,512]{1,0:T(8,128)(2,1)S(1)}, bf16[128,512]{1,0:T(8,128)(2,1)S(1)}, u32[]{:S(2)}, u32[]{:S(2)}) collective-permute-start(bf16[128,512]{1,0:T(8,128)(2,1)S(1)} %add_select_fusion.after_ref.held_ref), channel_id=1, source_target_pairs={{2,26},{4,28},{6,30},{19,11},{21,13},{23,15},{38,62},{32,56},{34,5... | collective-permute-start | bytes 393224 | tf_op jit(solution)/shard_map/ppermute | solution.py:408
  20.9 4.1 %copy-start = (bf16[2,512,768]{2,1,0:T(8,128)(2,1)S(1)}, bf16[2,512,768]{2,1,0:T(8,128)(2,1)}, u32[]{:S(2)}) copy-start(bf16[2,512,768]{2,1,0:T(8,128)(2,1)} %constant.81.clone.w_ref) | copy-start | bytes 4718596
  20.9 4.1 %copy-start.3 = (bf16[2,768,512]{2,1,0:T(8,128)(2,1)S(1)}, bf16[2,768,512]{2,1,0:T(8,128)(2,1)}, u32[]{:S(2)}) copy-start(bf16[2,768,512]{2,1,0:T(8,128)(2,1)} %constant.82.clone.back_ref) | copy-start | bytes 4718596
  32.7 1.4 %collective-permute-start.9 = (bf16[128,512]{1,0:T(8,128)(2,1)S(1)}, bf16[128,512]{1,0:T(8,128)(2,1)S(1)}, u32[]{:S(2)}, u32[]{:S(2)}) collective-permute-start(bf16[128,512]{1,0:T(8,128)(2,1)S(1)} %correlate.1.mine_ref), channel_id=1, source_target_pairs={{0,1},{1,0},{2,3},{3,2},{4,5},{5,4},{6,7},{7,6},{8,9},{9,8},{10,11... | collective-permute-start | bytes 393224 | tf_op jit(solution)/shard_map/ppermute | solution.py:414

commit v3 on v2

--- a/solution.py
+++ b/solution.py
@@ -54,23 +54,20 @@
 
 
 def plans():
-    across, up, along = [[], []], [[], []], []
+    up, across, along = [[], []], [], []
     for s, k, y, z in owners():
-        across[0].append((device(s, z, y, 0), device(s, z, y + 2, k)))
-        across[1].append((device(s, z, y, 0), device(s, z, y - 1, k)))
-        across[1].append((device(s, z, y, 1), device(s, z, y + 1, k)))
-        up[0].append((device(s, z, y, 0), device(s, z + 2, y, k)))
-        up[1].append((device(s, z, y, 0), device(s, z - 1, y, k)))
+        up[k].append((device(s, z, y, 0), device(s, z + 2, y, k)))
+        up[1 - k].append((device(s, z, y, 0), device(s, z - 1, y, k)))
         up[1].append((device(s, z, y, 1), device(s, z + 1, y, k)))
+        across.append((device(s, z, y, 0), device(s, z, y + 2, k)))
+        across.append((device(s, z, y, 1), device(s, z, y + 1, k)))
     for d in (2, 1, 3):
-        along.append(
-            [
-                (device(s, z, y + yy, k), device(s, z + d, y + yy, k))
-                for s, k, y, z in owners()
-                for yy in range(1, RING)
-            ]
-        )
-    return across, up, along
+        plan = []
+        for s, k, y, z in owners():
+            for zz in range(0 if d == 3 else 1, RING):
+                plan.append((device(s, z + zz, y, k), device(s, z + zz, y + d, k)))
+        along.append(plan)
+    return up, across, along
 
 
 def in_hbm(value):
@@ -81,7 +78,25 @@
     return [pl.BlockSpec(memory_space=pltpu.VMEM)] * n
 
 
-def prefilter_kernel(traces_ref, band_ref, filters_ref, out_ref, pad_ref):
+def prefilter_kernel(
+    traces_hbm, band_hbm, filters_hbm, w_ref, out_ref, near_ref, pad_ref, traces_ref, band_ref, filters_ref, sems
+):
+    pairs = ((traces_hbm, traces_ref), (band_hbm, band_ref), (filters_hbm, filters_ref))
+    inputs = [pltpu.make_async_copy(a, b, sems.at[8 + i]) for i, (a, b) in enumerate(pairs)]
+    for copy in inputs:
+        copy.start()
+    copies = [
+        pltpu.make_async_copy(
+            w_ref.at[i, pl.ds(j, 128)], near_ref.at[i, pl.ds(j, 128)], sems.at[4 * i + j // 128]
+        )
+        for i in range(2)
+        for j in range(0, SAMPLES, 128)
+    ]
+    for copy in copies:
+        copy.start()
+    pad_ref[0:TAPS, :] = jnp.zeros((TAPS, CH), F32)
+    for copy in inputs:
+        copy.wait()
     bands = filters_ref.shape[0]
     onehot = (lax.broadcasted_iota(jnp.int32, (bands, CH), 0) == band_ref[...]).astype(F32)
     taps = lax.dot_general(
@@ -91,7 +106,6 @@
         precision=lax.Precision.HIGHEST,
         preferred_element_type=F32,
     )
-    pad_ref[0:TAPS, :] = jnp.zeros((TAPS, CH), F32)
     pad_ref[TAPS:, :] = traces_ref[...].astype(F32).T
     rows = 128
     power = jnp.zeros((1, CH), F32)
@@ -106,26 +120,33 @@
     scale = lax.rsqrt(power * (1.0 / SAMPLES) + 1e-06)
     for i, total in enumerate(parts):
         out_ref[:, i * rows : (i + 1) * rows] = (total * scale).T.astype(BF)
-
-
-def prefilter(traces, band_group, filters):
+    for copy in copies:
+        copy.wait()
+
+
+def prefilter(traces, band_group, filters, w):
     return pl.pallas_call(
         prefilter_kernel,
-        out_shape=pltpu.VMEM((CH, SAMPLES), BF),
-        in_specs=vmem(3),
-        out_specs=pl.BlockSpec(memory_space=pltpu.VMEM),
-        scratch_shapes=[pltpu.VMEM((TAPS + SAMPLES, CH), F32)],
+        out_shape=[pltpu.VMEM((CH, SAMPLES), BF), pltpu.VMEM((2, SAMPLES, PERIOD), BF)],
+        in_specs=[pl.BlockSpec(memory_space=pltpu.HBM)] * 4,
+        out_specs=vmem(2),
+        scratch_shapes=[
+            pltpu.VMEM((TAPS + SAMPLES, CH), F32),
+            pltpu.VMEM((CH, SAMPLES), BF),
+            pltpu.VMEM((1, CH), jnp.int32),
+            pltpu.VMEM(filters.shape, F32),
+            pltpu.SemaphoreType.DMA((11,)),
+        ],
+        compiler_params=pltpu.CompilerParams(vmem_limit_bytes=LIMIT),
         name="prefilter",
-    )(traces, band_group.reshape(1, CH), filters)
+    )(in_hbm(traces), in_hbm(band_group.reshape(1, CH)), in_hbm(filters), in_hbm(w))
 
 
 def correlate_kernel(
-    scalars, low_ref, held_ref, r0, r1, r2, r3, r4, w_ref, fc_ref, bins_ref, hot_ref, back_ref, out_ref,
+    low_ref, held_ref, r0, r1, r2, r3, w_ref, fc_ref, bins_ref, hot_ref, back_ref, out_ref,
     fs, total, wide,
 ):
-    held = held_ref[...].astype(F32) * scalars[2].astype(F32)
-    rest = (r0[...] + r1[...]) + (r2[...] + r3[...]) + r4[...]
-    block = (held + rest.astype(F32)).astype(BF)
+    block = held_ref[...] + ((r0[...] + r1[...]) + (r2[...] + r3[...]))
     fs[...] = jnp.dot(block, w_ref[0], preferred_element_type=F32) + jnp.dot(
         block, w_ref[1], preferred_element_type=F32
     )
@@ -164,7 +185,7 @@
                 gather(g, j, SPAN, spread(hot_ref[g], j))
             return carry
 
-        lax.fori_loop(0, n_groups, body, 0)
+        lax.fori_loop(0, n_groups, body, 0, unroll=2)
 
     @pl.when(jnp.logical_not(fits))
     def _():
@@ -193,11 +214,11 @@
         out_ref[start : start + 128, :] = value.astype(BF)
 
 
-def correlate(scalars, lows, held, parts, w, fc, bins, hot, back):
+def correlate(lows, held, parts, w, fc, bins, hot, back):
     return pl.pallas_call(
         correlate_kernel,
         out_shape=jax.ShapeDtypeStruct((WIN, LAGS), BF),
-        in_specs=[pl.BlockSpec(memory_space=pltpu.SMEM)] * 2 + vmem(11),
+        in_specs=[pl.BlockSpec(memory_space=pltpu.SMEM)] + vmem(10),
         out_specs=pl.BlockSpec(memory_space=pltpu.VMEM),
         scratch_shapes=[
             pltpu.VMEM((CH, PERIOD), F32),
@@ -209,23 +230,21 @@
             flops=2 * 128 * SPAN * 256 * PERIOD, bytes_accessed=6 * 1024 * 1024, transcendentals=0
         ),
         name="correlate",
-    )(scalars, lows, held, *parts, w, fc, bins, hot, back)
+    )(lows, held, *parts, w, fc, bins, hot, back)
 
 
 def survey_kernel(
-    scalars, pair_ref, other_ref, mine_ref, partner_ref, w_ref, bins_ref, table_ref, fc_ref, flag_ref,
-    raw, w, sems,
+    scalars, pair_ref, other_ref, mine_ref, partner_ref, w_ref, bins_ref, table_ref, fc_ref, flag_ref, raw, sem
 ):
     core = scalars[0]
-    copies = [pltpu.make_async_copy(pair_ref.at[core], raw, sems.at[0])] + [
-        pltpu.make_async_copy(w_ref.at[i, pl.ds(j, 128)], w.at[i, pl.ds(j, 128)], sems.at[1 + 4 * i + j // 128])
-        for i in range(2)
-        for j in range(0, SAMPLES, 128)
-    ]
-    for copy in copies:
-        copy.start()
+    copy = pltpu.make_async_copy(pair_ref.at[core], raw, sem)
+    copy.start()
     flag_ref[...] = jnp.full(flag_ref.shape, scalars[1], jnp.int32)
-    copies[0].wait()
+    for i, ref in enumerate((mine_ref, partner_ref)):
+        value = jnp.dot(ref[...], w_ref[0], preferred_element_type=F32)
+        value = value + jnp.dot(ref[...], w_ref[1], preferred_element_type=F32)
+        fc_ref[i * CH : (i + 1) * CH, :] = value.astype(BF)
+    copy.wait()
     bins = jnp.concatenate([raw[...], other_ref[core]], axis=1)
     lowest = jnp.min(jnp.min(bins, axis=0, keepdims=True), axis=1, keepdims=True)
     rel = bins - lowest
@@ -239,12 +258,28 @@
     low = jnp.minimum(low * fits, WIN)
     table_ref[0:n_groups, :] = jnp.broadcast_to(low, (n_groups, 128))
     table_ref[n_groups:, :] = jnp.broadcast_to(fits, (8, 128))
-    for copy in copies[1:]:
-        copy.wait()
-    for i, ref in enumerate((mine_ref, partner_ref)):
-        value = jnp.dot(ref[...], w[0], preferred_element_type=F32)
-        value = value + jnp.dot(ref[...], w[1], preferred_element_type=F32)
-        fc_ref[i * CH : (i + 1) * CH, :] = value.astype(BF)
+
+def tally_of(rel, words):
+    place = rel % 32
+    unit = jnp.left_shift(1, rel // 32 * 8)
+
+    def body(j, carry):
+        hit = jnp.where(place == j, unit, 0)
+        hit = hit[:, :CH] + hit[:, CH:]
+        pieces = [hit[q : q + 8] for q in range(0, CH, 8)]
+        while len(pieces) > 1:
+            pieces = [x + y for x, y in zip(pieces[::2], pieces[1::2])]
+        words[pl.ds(pl.multiple_of(j * 8, 8), 8), :] = pieces[0]
+        return carry
+
+    lax.fori_loop(0, 32, body, 0, unroll=4)
+    packed = words[...]
+    pieces = []
+    for q in range(WIN // 32):
+        part = jnp.bitwise_and(jnp.right_shift(packed, 8 * q), 255)
+        part = jnp.sum(part.reshape(32, 8, CH), axis=1)
+        pieces.append(jnp.sum(part, axis=1, keepdims=True))
+    return jnp.concatenate(pieces, axis=0)
 
 
 def survey(scalars, pair, other, mine, partner, w):
@@ -258,24 +293,23 @@
             pltpu.VMEM((2 * CH, PERIOD), BF),
             pltpu.VMEM((8, SAMPLES), jnp.int32),
         ],
-        in_specs=[pl.BlockSpec(memory_space=pltpu.SMEM), far] + vmem(3) + [far],
+        in_specs=[pl.BlockSpec(memory_space=pltpu.SMEM), far] + vmem(4),
         out_specs=[whole] * 4,
         scratch_shapes=[
             pltpu.VMEM((CH, CH), jnp.int32),
-            pltpu.VMEM((2, SAMPLES, PERIOD), BF),
-            pltpu.SemaphoreType.DMA((9,)),
+            pltpu.SemaphoreType.DMA,
         ],
         compiler_params=pltpu.CompilerParams(vmem_limit_bytes=LIMIT),
         cost_estimate=pl.CostEstimate(
             flops=2 * 2 * 2 * CH * SAMPLES * PERIOD, bytes_accessed=2 * 1024 * 1024, transcendentals=0
         ),
         name="survey",
-    )(scalars, in_hbm(pair), other, mine, partner, in_hbm(w))
+    )(scalars, in_hbm(pair), other, mine, partner, w)
 
 
 def prepare_kernel(
     scalars, low_ref, order_ref, pair_ref, other_ref, bins_ref, after_ref, hot_ref, pick_ref, tally_ref,
-    words, ranks,
+    ranks, words,
 ):
     core = scalars[0]
     columns = lax.broadcasted_iota(jnp.int32, (512, WIN), 1)
@@ -289,27 +323,7 @@
         step = core if i == 0 else 1 - core
         bins = jnp.concatenate([pair_ref[step], other_ref[step]], axis=1)
         lowest = jnp.min(jnp.min(bins, axis=0, keepdims=True), axis=1, keepdims=True)
-        rel = bins - lowest
-        place = rel % 32
-        unit = jnp.left_shift(1, rel // 32 * 8)
-
-        def body(j, carry):
-            hit = jnp.where(place == j, unit, 0)
-            hit = hit[:, :CH] + hit[:, CH:]
-            pieces = [hit[q : q + 8] for q in range(0, CH, 8)]
-            while len(pieces) > 1:
-                pieces = [x + y for x, y in zip(pieces[::2], pieces[1::2])]
-            words[pl.ds(pl.multiple_of(j * 8, 8), 8), :] = pieces[0]
-            return carry
-
-        lax.fori_loop(0, 32, body, 0, unroll=4)
-        packed = words[...]
-        pieces = []
-        for q in range(WIN // 32):
-            part = jnp.bitwise_and(jnp.right_shift(packed, 8 * q), 255)
-            part = jnp.sum(part.reshape(32, 8, CH), axis=1)
-            pieces.append(jnp.sum(part, axis=1, keepdims=True))
-        counts = jnp.concatenate(pieces, axis=0)
+        counts = tally_of(bins - lowest, words)
         pick = jnp.where(order - lowest == columns, 1.0, 0.0).astype(BF)
         pick_ref[:, i * WIN : (i + 1) * WIN] = pick
         parts = jnp.where(lane == 2 * i, counts - counts % 256, 0)
@@ -340,7 +354,7 @@
         ],
         in_specs=[pl.BlockSpec(memory_space=pltpu.SMEM)] * 2 + vmem(4) + [pl.BlockSpec(memory_space=pl.ANY)],
         out_specs=vmem(3),
-        scratch_shapes=[pltpu.VMEM((32 * 8, CH), jnp.int32), pltpu.VMEM((8, 2, 8, 128), jnp.int32)],
+        scratch_shapes=[pltpu.VMEM((8, 2, 8, 128), jnp.int32), pltpu.VMEM((32 * 8, CH), jnp.int32)],
         compiler_params=pltpu.CompilerParams(vmem_limit_bytes=LIMIT),
         cost_estimate=pl.CostEstimate(flops=10**9, bytes_accessed=2**20, transcendentals=0),
         name="prepare",
@@ -390,19 +404,18 @@
     src, rcv = lax.axis_index("src"), lax.axis_index("rcv")
     core = rcv % 2
     y, z = (rcv // 2) % RING, rcv // 8
-    root = jnp.logical_and(y == 2 * (src % 2), z % 2 == src // 2)
-    keep = jnp.logical_or(jnp.logical_not(root), z // 2 == core)
-    scalars = jnp.stack([core, root.astype(jnp.int32), keep.astype(jnp.int32)])
-
-    across, up, along = plans()
+    owner = jnp.logical_and(y == 2 * (src % 2), z == 2 * core + src // 2)
+    scalars = jnp.stack([core, owner.astype(jnp.int32)])
+
+    up, across, along = plans()
     other_pair = lax.ppermute(pair_bin, "rcv", swap)
-    filtered = prefilter(traces, band_group, filters)
+    filtered, w = prefilter(traces, band_group, filters, w)
     filtered, other_pair = lax.optimization_barrier((filtered, other_pair))
-    got = lax.ppermute(filtered, both, across[0])
+    got = lax.ppermute(filtered, both, up[0])
     partner = lax.ppermute(filtered, "rcv", swap)
     seed = jnp.where(core == 0, filtered, partner)
-    got = got + lax.ppermute(seed, both, across[1])
-    parts = [lax.ppermute(seed, both, plan) for plan in up]
+    got = got + lax.ppermute(seed, both, up[1])
+    parts = [lax.ppermute(seed, both, across)]
     bins, table, fc, flag = survey(scalars, pair_bin, other_pair, filtered, partner, w)
     held = jnp.where(flag[0:1] == 1, seed, got)
     parts = parts + [lax.ppermute(held, both, plan) for plan in along]
@@ -410,7 +423,7 @@
         scalars, table, bin_order.reshape(8, 128), pair_bin, other_pair, bins, held
     )
 
-    window = correlate(scalars, table, held, parts, w, fc, bins, hot, back)
+    window = correlate(table, held, parts, w, fc, bins, hot, back)
     other_window = lax.ppermute(window, "rcv", swap)
     payload = arrange(pick, tally, window, other_window)
     groups = [[2 * i + c for i in range(64)] for c in range(2)]

time: 56.2 us -> 54.9 us (0.977)
  blocking collectives: 20.7 us -> 23.8 us
  starting transfers between devices: 16 us -> 13.5 us
  Pallas kernels: 17.4 us -> 16 us
    ppermute x4 -> x3, starting transfers between devices: 13.3 us -> 8.45 us  [the longest x1 5.86 us: shards(): got = lax.ppermute(filtered, both, up[0])]
    all_to_all x1, blocking collectives: 20.7 us -> 23.8 us  [shards(): lax.all_to_all(payload, both, 0, 0, tiled=True, axis_index_groups=groups)]
    ppermute x1, starting transfers between devices: 0.09 us -> 1.78 us  [shards(): other_window = lax.ppermute(window, 'rcv', swap)]
    pallas_call x1, Pallas kernels: 2.69 us -> 1.81 us  [survey(): pl.pallas_call(survey_kernel, out_shape=[pltpu.VMEM((CH, 2 * CH), jnp.int...]
    ppermute x3, starting transfers between devices: 2.01 us -> 2.64 us  [shards(): parts = parts + [lax.ppermute(held, both, plan) for plan in along]]
    pallas_call x1, Pallas kernels: 7.61 us -> 7 us  [correlate(): pl.pallas_call(correlate_kernel, out_shape=jax.ShapeDtypeStruct((WIN, LAG...]
  transfers between devices with their start and end apart: 10 -> 9, of which waited for: 1 -> 1; matrix products, arithmetic and copies ran while one was open for 0% -> 0% of each run, Pallas kernels for 16% -> 15%
where the time goes in v3:
time: 54.9 us; the launch traced here: 54.6 us
  blocking collectives  23.8 us (43%)
  Pallas kernels  16 us (29%)
  starting transfers between devices  13.5 us (25%)
  waiting for transfers between devices  1.01 us (2%)
    all_to_all x1, blocking collectives, shards(): lax.all_to_all(payload, both, 0, 0, tiled=True, axis_index_groups=groups)  23.8 us
    pallas_call x1, Pallas kernels, correlate(): pl.pallas_call(correlate_kernel, out_shape=jax.ShapeDtypeStruct((WIN, LAG...  7 us
    ppermute x1, starting transfers between devices, shards(): got = lax.ppermute(filtered, both, up[0])  5.86 us
    pallas_call x1, Pallas kernels, prepare(): pl.pallas_call(prepare_kernel, out_shape=[pltpu.VMEM((CH // GROUP, GROUP...  4.02 us
    ppermute x3, starting transfers between devices, shards(): parts = parts + [lax.ppermute(held, both, plan) for plan in along]  2.64 us
    pallas_call x1, Pallas kernels, prefilter(): pl.pallas_call(prefilter_kernel, out_shape=[pltpu.VMEM((CH, SAMPLES), BF)...  2.14 us
    pallas_call x1, Pallas kernels, survey(): pl.pallas_call(survey_kernel, out_shape=[pltpu.VMEM((CH, 2 * CH), jnp.int...  1.81 us
    ppermute x1, starting transfers between devices, shards(): other_window = lax.ppermute(window, 'rcv', swap)  1.78 us
  transfers between devices with their start and end apart: 9, of which 1 were waited for; matrix products, arithmetic and copies ran while one was open for 0% of the time, Pallas kernels for 15%

profile of v3, /device:TPU:0, one launch (start us, length us, event | category | flops | bytes accessed | tf_op | source)
XLA Modules:
  0.0 54.6 jit_solution(13972739974902776843)
XLA Ops:
  0.0 0.0 collective-permute-start
  0.0 2.1 %prefilter.1 = (bf16[128,512]{1,0:T(8,128)(2,1)S(1)}, bf16[2,512,768]{2,1,0:T(8,128)(2,1)S(1)}) custom-call(bf16[128,512]{1,0:T(8,128)(2,1)} %traces_hbm.1, s32[1,128]{1,0:T(1,128)} %bitcast.9, f32[24,32]{1,0:T(8,128)} %filters_hbm.1, bf16[2,512,768]{2,1,0:T(8,128)(2,1)} %constant.70.clone.w_ref), custom_call_target="tpu_custom_call" | custom-call | tf_op jit(solution)/shard_map/prefilter/pallas_call | solution.py:128
  2.2 0.0 collective-permute-done.other_ref
  2.2 0.6 %collective-permute-start.1 = (bf16[128,512]{1,0:T(8,128)(2,1)S(1)}, bf16[128,512]{1,0:T(8,128)(2,1)S(1)}, u32[]{:S(2)}, u32[]{:S(2)}) collective-permute-start(bf16[128,512]{1,0:T(8,128)(2,1)S(1)} %get-tuple-element.18.mine_ref), channel_id=1, source_target_pairs={{0,1},{1,0},{2,3},{3,2},{4,5},{5,4},{6,7},{7,6},{8,9},{9,8},{10,11... | collective-permute-start | bytes 393224 | tf_op jit(solution)/shard_map/ppermute | solution.py:415
  2.7 0.0 copy-start
  2.8 0.0 copy-start.1
  2.8 0.1 pad_add_fusion.scalars
  2.8 5.9 %collective-permute-start.2 = (bf16[128,512]{1,0:T(8,128)(2,1)S(1)}, bf16[128,512]{1,0:T(8,128)(2,1)S(1)}, u32[]{:S(2)}, u32[]{:S(2)}) collective-permute-start(bf16[128,512]{1,0:T(8,128)(2,1)S(1)} %get-tuple-element.18.mine_ref), channel_id=1, source_target_pairs={{0,16},{16,9},{36,52},{52,45},{72,88},{88,81},{108,124},{124,117}} | collective-permute-start | bytes 393224 | tf_op jit(solution)/shard_map/ppermute | solution.py:414
  8.7 0.0 collective-permute-done.1.partner_ref
  8.7 1.3 %collective-permute-start.3 = (bf16[128,512]{1,0:T(8,128)(2,1)S(1)}, bf16[128,512]{1,0:T(8,128)(2,1)S(1)}, u32[]{:S(2)}, u32[]{:S(2)}) collective-permute-start(bf16[128,512]{1,0:T(8,128)(2,1)S(1)} %broadcast_select_fusion), channel_id=1, source_target_pairs={{0,24},{1,8},{16,1},{17,25},{36,60},{37,44},{52,37},{53,61},{72,64... | collective-permute-start | bytes 393224 | tf_op jit(solution)/shard_map/ppermute | solution.py:417
  10.0 1.3 %collective-permute-start.4 = (bf16[128,512]{1,0:T(8,128)(2,1)S(1)}, bf16[128,512]{1,0:T(8,128)(2,1)S(1)}, u32[]{:S(2)}, u32[]{:S(2)}) collective-permute-start(bf16[128,512]{1,0:T(8,128)(2,1)S(1)} %broadcast_select_fusion), channel_id=1, source_target_pairs={{0,4},{1,2},{16,21},{17,19},{36,32},{37,38},{52,49},{53,55},{72,76... | collective-permute-start | bytes 393224 | tf_op jit(solution)/shard_map/ppermute | solution.py:418
  11.3 1.8 %survey.1 = (s32[128,256]{1,0:T(8,128)S(1)}, s32[16,128]{1,0:T(8,128)S(1)}, bf16[256,768]{1,0:T(8,128)(2,1)S(1)}, s32[8,512]{1,0:T(8,128)S(1)}) custom-call(s32[2]{0:T(128)S(1)} %pad_add_fusion.scalars, s32[2,128,128]{2,1,0:T(8,128)} %pair_ref.3, s32[2,128,128]{2,1,0:T(8,128)S(1)} %collective-permute-done.other_ref, ...), custom_call_target="tpu_custom_call" | custom-call | flops 402653184 | bytes 2097152 | tf_op jit(solution)/shard_map/survey/pallas_call | solution.py:288
  13.2 0.0 collective-permute-done.2
  13.2 0.0 collective-permute-done.3
  13.2 0.7 %collective-permute-start.5 = (bf16[128,512]{1,0:T(8,128)(2,1)S(1)}, bf16[128,512]{1,0:T(8,128)(2,1)S(1)}, u32[]{:S(2)}, u32[]{:S(2)}) collective-permute-start(bf16[128,512]{1,0:T(8,128)(2,1)S(1)} %add_select_fusion.after_ref.held_ref), channel_id=1, source_target_pairs={{8,12},{16,20},{24,28},{25,29},{1,5},{9,13},{44,40},{52,48},{60,56... | collective-permute-start | bytes 393224 | tf_op jit(solution)/shard_map/ppermute | solution.py:421
  13.9 0.7 %collective-permute-start.6 = (bf16[128,512]{1,0:T(8,128)(2,1)S(1)}, bf16[128,512]{1,0:T(8,128)(2,1)S(1)}, u32[]{:S(2)}, u32[]{:S(2)}) collective-permute-start(bf16[128,512]{1,0:T(8,128)(2,1)S(1)} %add_select_fusion.after_ref.held_ref), channel_id=1, source_target_pairs={{8,10},{16,18},{24,26},{25,27},{1,3},{9,11},{44,46},{52,54},{60,62... | collective-permute-start | bytes 393224 | tf_op jit(solution)/shard_map/ppermute | solution.py:421
  14.6 1.3 %collective-permute-start.7 = (bf16[128,512]{1,0:T(8,128)(2,1)S(1)}, bf16[128,512]{1,0:T(8,128)(2,1)S(1)}, u32[]{:S(2)}, u32[]{:S(2)}) collective-permute-start(bf16[128,512]{1,0:T(8,128)(2,1)S(1)} %add_select_fusion.after_ref.held_ref), channel_id=1, source_target_pairs={{0,6},{8,14},{16,22},{24,30},{17,23},{25,31},{1,7},{9,15},{36,34},... | collective-permute-start | bytes 393224 | tf_op jit(solution)/shard_map/ppermute | solution.py:421
  15.9 0.0 copy-done
  15.9 0.0 copy-done.1
  15.9 0.0 copy-start.2
  15.9 4.0 %prepare.1 = (bf16[8,1152,256]{2,1,0:T(8,128)(2,1)S(1)}, bf16[512,256]{1,0:T(8,128)(2,1)S(1)}, bf16[512,128]{1,0:T(8,128)(2,1)S(1)}) custom-call(s32[2]{0:T(128)S(1)} %pad_add_fusion.scalars, s32[16,128]{1,0:T(8,128)S(1)} %get-tuple-element.20.low_ref, s32[8,128]{1,0:T(8,128)S(1)} %bitcast.8, s32[2,128,128]{2,1,0:T(8,128)S(1)} %copy-done, ...), custom_call_target="tpu_custom_call" | custom-call | flops 1000000000 | bytes 1048576 | tf_op jit(solution)/shard_map/prepare/pallas_call | solution.py:348
  19.9 0.0 collective-permute-done.4.r0
  20.0 0.0 collective-permute-done.5.r1
  20.0 0.0 collective-permute-done.6.r2
  20.0 0.0 collective-permute-done.7.r3
  20.0 0.0 copy-done.2
  20.0 7.0 %correlate.1.mine_ref = bf16[128,512]{1,0:T(8,128)(2,1)S(1)} custom-call(s32[16,128]{1,0:T(8,128)S(1)} %get-tuple-element.20.low_ref, bf16[128,512]{1,0:T(8,128)(2,1)S(1)} %add_select_fusion.after_ref.held_ref, bf16[128,512]{1,0:T(8,128)(2,1)S(1)} %collective-permute-done.4.r0, bf16[128,512]{1,0:T(8,128)(2,1)S(1)} %collective-permute-done.5.r1, ...), custom_call_target="tpu_custom_call" | custom-call | flops 3623878656 | bytes 6291456 | tf_op jit(solution)/shard_map/correlate/pallas_call | solution.py:218
  27.0 1.8 %collective-permute-start.8 = (bf16[128,512]{1,0:T(8,128)(2,1)S(1)}, bf16[128,512]{1,0:T(8,128)(2,1)S(1)}, u32[]{:S(2)}, u32[]{:S(2)}) collective-permute-start(bf16[128,512]{1,0:T(8,128)(2,1)S(1)} %correlate.1.mine_ref), channel_id=1, source_target_pairs={{0,1},{1,0},{2,3},{3,2},{4,5},{5,4},{6,7},{7,6},{8,9},{9,8},{10,11... | collective-permute-start | bytes 393224 | tf_op jit(solution)/shard_map/ppermute | solution.py:427
  28.8 1.0 %collective-permute-done.8.other_ref = bf16[128,512]{1,0:T(8,128)(2,1)S(1)} collective-permute-done((bf16[128,512]{1,0:T(8,128)(2,1)S(1)}, bf16[128,512]{1,0:T(8,128)(2,1)S(1)}, u32[]{:S(2)}, u32[]{:S(2)}) %collective-permute-start.8) | collective-permute-done | bytes 131104 | tf_op jit(solution)/shard_map/ppermute | solution.py:427
  29.8 0.3 arrange.1
  30.1 23.8 %all_to_all.11 = bf16[64,8,640]{2,1,0:T(8,128)(2,1)S(1)} all-to-all(bf16[64,8,640]{2,1,0:T(8,128)(2,1)S(1)} %bitcast.6), channel_id=1, replica_groups={{0,2,4,6,8,10,12,14,16,18,20,22,24,26,28,30,32,34,36,38,40,42,44,46,48,..., dimensions={0} | all-to-all | bytes 1310720 | tf_op jit(solution)/shard_map/all_to_all | solution.py:430
  53.8 0.8 %finish.1 = f32[8,512]{1,0:T(8,128)} custom-call(bf16[512,640]{1,0:T(8,128)(2,1)S(1)} %bitcast.7), custom_call_target="tpu_custom_call" | custom-call | tf_op jit(solution)/shard_map/finish/pallas_call | solution.py:389
  (3 shorter events, 0.1 us)
Async XLA Ops:
  0.0 2.2 %collective-permute-start = (s32[2,128,128]{2,1,0:T(8,128)}, s32[2,128,128]{2,1,0:T(8,128)S(1)}, u32[]{:S(2)}, u32[]{:S(2)}) collective-permute-start(s32[2,128,128]{2,1,0:T(8,128)} %pair_ref.3), channel_id=1, source_target_pairs={{0,1},{1,0},{2,3},{3,2},{4,5},{5,4},{6,7},{7,6},{8,9},{9,8},{10,11... | collective-permute-start | bytes 393224 | tf_op jit(solution)/shard_map/ppermute | solution.py:411
  2.2 6.5 %collective-permute-start.1 = (bf16[128,512]{1,0:T(8,128)(2,1)S(1)}, bf16[128,512]{1,0:T(8,128)(2,1)S(1)}, u32[]{:S(2)}, u32[]{:S(2)}) collective-permute-start(bf16[128,512]{1,0:T(8,128)(2,1)S(1)} %get-tuple-element.18.mine_ref), channel_id=1, source_target_pairs={{0,1},{1,0},{2,3},{3,2},{4,5},{5,4},{6,7},{7,6},{8,9},{9,8},{10,11... | collective-permute-start | bytes 393224 | tf_op jit(solution)/shard_map/ppermute | solution.py:415
  2.7 13.1 %copy-start = (s32[2,128,128]{2,1,0:T(8,128)S(1)}, s32[2,128,128]{2,1,0:T(8,128)}, u32[]{:S(2)}) copy-start(s32[2,128,128]{2,1,0:T(8,128)} %pair_ref.3) | copy-start | bytes 393220
  2.8 13.2 %copy-start.1 = (s32[1024]{0:T(1024)S(1)}, s32[1024]{0:T(1024)}, u32[]{:S(2)}) copy-start(s32[1024]{0:T(1024)} %param.11) | copy-start | bytes 12292
  2.8 10.4 %collective-permute-start.2 = (bf16[128,512]{1,0:T(8,128)(2,1)S(1)}, bf16[128,512]{1,0:T(8,128)(2,1)S(1)}, u32[]{:S(2)}, u32[]{:S(2)}) collective-permute-start(bf16[128,512]{1,0:T(8,128)(2,1)S(1)} %get-tuple-element.18.mine_ref), channel_id=1, source_target_pairs={{0,16},{16,9},{36,52},{52,45},{72,88},{88,81},{108,124},{124,117}} | collective-permute-start | bytes 393224 | tf_op jit(solution)/shard_map/ppermute | solution.py:414
  8.7 4.5 %collective-permute-start.3 = (bf16[128,512]{1,0:T(8,128)(2,1)S(1)}, bf16[128,512]{1,0:T(8,128)(2,1)S(1)}, u32[]{:S(2)}, u32[]{:S(2)}) collective-permute-start(bf16[128,512]{1,0:T(8,128)(2,1)S(1)} %broadcast_select_fusion), channel_id=1, source_target_pairs={{0,24},{1,8},{16,1},{17,25},{36,60},{37,44},{52,37},{53,61},{72,64... | collective-permute-start | bytes 393224 | tf_op jit(solution)/shard_map/ppermute | solution.py:417
  10.0 9.9 %collective-permute-start.4 = (bf16[128,512]{1,0:T(8,128)(2,1)S(1)}, bf16[128,512]{1,0:T(8,128)(2,1)S(1)}, u32[]{:S(2)}, u32[]{:S(2)}) collective-permute-start(bf16[128,512]{1,0:T(8,128)(2,1)S(1)} %broadcast_select_fusion), channel_id=1, source_target_pairs={{0,4},{1,2},{16,21},{17,19},{36,32},{37,38},{52,49},{53,55},{72,76... | collective-permute-start | bytes 393224 | tf_op jit(solution)/shard_map/ppermute | solution.py:418
  13.2 6.7 %collective-permute-start.5 = (bf16[128,512]{1,0:T(8,128)(2,1)S(1)}, bf16[128,512]{1,0:T(8,128)(2,1)S(1)}, u32[]{:S(2)}, u32[]{:S(2)}) collective-permute-start(bf16[128,512]{1,0:T(8,128)(2,1)S(1)} %add_select_fusion.after_ref.held_ref), channel_id=1, source_target_pairs={{8,12},{16,20},{24,28},{25,29},{1,5},{9,13},{44,40},{52,48},{60,56... | collective-permute-start | bytes 393224 | tf_op jit(solution)/shard_map/ppermute | solution.py:421
  13.9 6.1 %collective-permute-start.6 = (bf16[128,512]{1,0:T(8,128)(2,1)S(1)}, bf16[128,512]{1,0:T(8,128)(2,1)S(1)}, u32[]{:S(2)}, u32[]{:S(2)}) collective-permute-start(bf16[128,512]{1,0:T(8,128)(2,1)S(1)} %add_select_fusion.after_ref.held_ref), channel_id=1, source_target_pairs={{8,10},{16,18},{24,26},{25,27},{1,3},{9,11},{44,46},{52,54},{60,62... | collective-permute-start | bytes 393224 | tf_op jit(solution)/shard_map/ppermute | solution.py:421
  14.6 5.4 %collective-permute-start.7 = (bf16[128,512]{1,0:T(8,128)(2,1)S(1)}, bf16[128,512]{1,0:T(8,128)(2,1)S(1)}, u32[]{:S(2)}, u32[]{:S(2)}) collective-permute-start(bf16[128,512]{1,0:T(8,128)(2,1)S(1)} %add_select_fusion.after_ref.held_ref), channel_id=1, source_target_pairs={{0,6},{8,14},{16,22},{24,30},{17,23},{25,31},{1,7},{9,15},{36,34},... | collective-permute-start | bytes 393224 | tf_op jit(solution)/shard_map/ppermute | solution.py:421
  15.9 4.1 %copy-start.2 = (bf16[2,768,512]{2,1,0:T(8,128)(2,1)S(1)}, bf16[2,768,512]{2,1,0:T(8,128)(2,1)}, u32[]{:S(2)}) copy-start(bf16[2,768,512]{2,1,0:T(8,128)(2,1)} %constant.71.clone.back_ref) | copy-start | bytes 4718596
  27.0 2.8 %collective-permute-start.8 = (bf16[128,512]{1,0:T(8,128)(2,1)S(1)}, bf16[128,512]{1,0:T(8,128)(2,1)S(1)}, u32[]{:S(2)}, u32[]{:S(2)}) collective-permute-start(bf16[128,512]{1,0:T(8,128)(2,1)S(1)} %correlate.1.mine_ref), channel_id=1, source_target_pairs={{0,1},{1,0},{2,3},{3,2},{4,5},{5,4},{6,7},{7,6},{8,9},{9,8},{10,11... | collective-permute-start | bytes 393224 | tf_op jit(solution)/shard_map/ppermute | solution.py:427

commit v4 on v3

--- a/solution.py
+++ b/solution.py
@@ -54,20 +54,20 @@
 
 
 def plans():
-    up, across, along = [[], []], [], []
+    first, side, along = [[], []], [], [[], [], []]
     for s, k, y, z in owners():
-        up[k].append((device(s, z, y, 0), device(s, z + 2, y, k)))
-        up[1 - k].append((device(s, z, y, 0), device(s, z - 1, y, k)))
-        up[1].append((device(s, z, y, 1), device(s, z + 1, y, k)))
-        across.append((device(s, z, y, 0), device(s, z, y + 2, k)))
-        across.append((device(s, z, y, 1), device(s, z, y + 1, k)))
-    for d in (2, 1, 3):
-        plan = []
-        for s, k, y, z in owners():
-            for zz in range(0 if d == 3 else 1, RING):
-                plan.append((device(s, z + zz, y, k), device(s, z + zz, y + d, k)))
-        along.append(plan)
-    return up, across, along
+
+        def chip(own, across, core, s=s, k=k, y=y, z=z):
+            return device(s, z + (across if k == 0 else own), y + (own if k == 0 else across), core)
+
+        first[0].append((chip(0, 0, 0), chip(-1, 0, k)))
+        first[1].append((chip(0, 0, 0), chip(2, 0, k)))
+        first[1].append((chip(0, 0, 1), chip(1, 0, k)))
+        side.append((chip(0, 0, 0), chip(0, 2, k)))
+        side.append((chip(0, 0, 1), chip(0, 1, k)))
+        for plan, d in zip(along, (2, 1, 3)):
+            plan.extend((chip(i, 0, k), chip(i, d, k)) for i in range(0 if d == 3 else 1, RING))
+    return first, side, along
 
 
 def in_hbm(value):
@@ -143,7 +143,7 @@
 
 
 def correlate_kernel(
-    low_ref, held_ref, r0, r1, r2, r3, w_ref, fc_ref, bins_ref, hot_ref, back_ref, out_ref,
+    low_ref, held_ref, r0, r1, r2, r3, w_ref, fc_ref, bins_ref, hot_ref, pieces_ref, back_ref, out_ref,
     fs, total, wide,
 ):
     block = held_ref[...] + ((r0[...] + r1[...]) + (r2[...] + r3[...]))
@@ -211,14 +211,15 @@
             + jnp.dot(low, back_ref[0], preferred_element_type=F32)
             + jnp.dot(high, back_ref[1], preferred_element_type=F32)
         )
-        out_ref[start : start + 128, :] = value.astype(BF)
-
-
-def correlate(lows, held, parts, w, fc, bins, hot, back):
+        out_ref[start : start + 128, :LAGS] = value.astype(BF)
+    out_ref[:, LAGS:] = pieces_ref[...]
+
+
+def correlate(lows, held, parts, w, fc, bins, hot, pieces, back):
     return pl.pallas_call(
         correlate_kernel,
-        out_shape=jax.ShapeDtypeStruct((WIN, LAGS), BF),
-        in_specs=[pl.BlockSpec(memory_space=pltpu.SMEM)] + vmem(10),
+        out_shape=jax.ShapeDtypeStruct((WIN, LAGS + 128), BF),
+        in_specs=[pl.BlockSpec(memory_space=pltpu.SMEM)] + vmem(11),
         out_specs=pl.BlockSpec(memory_space=pltpu.VMEM),
         scratch_shapes=[
             pltpu.VMEM((CH, PERIOD), F32),
@@ -230,11 +231,12 @@
             flops=2 * 128 * SPAN * 256 * PERIOD, bytes_accessed=6 * 1024 * 1024, transcendentals=0
         ),
         name="correlate",
-    )(lows, held, *parts, w, fc, bins, hot, back)
+    )(lows, held, *parts, w, fc, bins, hot, pieces, back)
 
 
 def survey_kernel(
-    scalars, pair_ref, other_ref, mine_ref, partner_ref, w_ref, bins_ref, table_ref, fc_ref, flag_ref, raw, sem
+    scalars, pair_ref, other_ref, mine_ref, partner_ref, w_ref, bins_ref, table_ref, fc_ref, flag_ref, pieces_ref,
+    raw, words, sem,
 ):
     core = scalars[0]
     copy = pltpu.make_async_copy(pair_ref.at[core], raw, sem)
@@ -258,6 +260,10 @@
     low = jnp.minimum(low * fits, WIN)
     table_ref[0:n_groups, :] = jnp.broadcast_to(low, (n_groups, 128))
     table_ref[n_groups:, :] = jnp.broadcast_to(fits, (8, 128))
+    counts = tally_of(rel, words)
+    lane = lax.broadcasted_iota(jnp.int32, (WIN, 128), 1) - 2 * core
+    pieces = jnp.where(lane == 0, counts - counts % 256, 0) + jnp.where(lane == 1, counts % 256, 0)
+    pieces_ref[...] = pieces.astype(F32).astype(BF)
 
 def tally_of(rel, words):
     place = rel % 32
@@ -292,11 +298,13 @@
             jax.ShapeDtypeStruct((CH // GROUP + 8, 128), jnp.int32),
             pltpu.VMEM((2 * CH, PERIOD), BF),
             pltpu.VMEM((8, SAMPLES), jnp.int32),
+            pltpu.VMEM((WIN, 128), BF),
         ],
         in_specs=[pl.BlockSpec(memory_space=pltpu.SMEM), far] + vmem(4),
-        out_specs=[whole] * 4,
+        out_specs=[whole] * 5,
         scratch_shapes=[
             pltpu.VMEM((CH, CH), jnp.int32),
+            pltpu.VMEM((32 * 8, CH), jnp.int32),
             pltpu.SemaphoreType.DMA,
         ],
         compiler_params=pltpu.CompilerParams(vmem_limit_bytes=LIMIT),
@@ -308,28 +316,21 @@
 
 
 def prepare_kernel(
-    scalars, low_ref, order_ref, pair_ref, other_ref, bins_ref, after_ref, hot_ref, pick_ref, tally_ref,
-    ranks, words,
+    scalars, low_ref, order_ref, pair_ref, other_ref, bins_ref, after_ref, hot_ref, pick_ref,
+    ranks,
 ):
     core = scalars[0]
     columns = lax.broadcasted_iota(jnp.int32, (512, WIN), 1)
-    lane = lax.broadcasted_iota(jnp.int32, (WIN, 128), 1)
     turned = jnp.concatenate([order_ref[...], jnp.zeros((120, 128), jnp.int32)], axis=0).T
     ranks[...] = turned.reshape(8, 2, 8, 128)
     half = ranks[:, core].reshape(64, 128)
     order = jnp.concatenate([half[:, a : a + 1] for a in range(8)], axis=0)
-    tally = jnp.zeros((512, 128), F32)
     for i in range(2):
         step = core if i == 0 else 1 - core
         bins = jnp.concatenate([pair_ref[step], other_ref[step]], axis=1)
         lowest = jnp.min(jnp.min(bins, axis=0, keepdims=True), axis=1, keepdims=True)
-        counts = tally_of(bins - lowest, words)
         pick = jnp.where(order - lowest == columns, 1.0, 0.0).astype(BF)
         pick_ref[:, i * WIN : (i + 1) * WIN] = pick
-        parts = jnp.where(lane == 2 * i, counts - counts % 256, 0)
-        parts = parts + jnp.where(lane == 2 * i + 1, counts % 256, 0)
-        tally = tally + jnp.dot(pick, parts.astype(F32).astype(BF), preferred_element_type=F32)
-    tally_ref[...] = tally.astype(BF)
 
     offsets = lax.broadcasted_iota(jnp.int32, (SPAN, 2 * CH), 0)
 
@@ -350,33 +351,30 @@
         out_shape=[
             pltpu.VMEM((CH // GROUP, GROUP * SPAN, 2 * CH), BF),
             pltpu.VMEM((512, 2 * WIN), BF),
-            pltpu.VMEM((512, 128), BF),
         ],
         in_specs=[pl.BlockSpec(memory_space=pltpu.SMEM)] * 2 + vmem(4) + [pl.BlockSpec(memory_space=pl.ANY)],
-        out_specs=vmem(3),
-        scratch_shapes=[pltpu.VMEM((8, 2, 8, 128), jnp.int32), pltpu.VMEM((32 * 8, CH), jnp.int32)],
+        out_specs=vmem(2),
+        scratch_shapes=[pltpu.VMEM((8, 2, 8, 128), jnp.int32)],
         compiler_params=pltpu.CompilerParams(vmem_limit_bytes=LIMIT),
         cost_estimate=pl.CostEstimate(flops=10**9, bytes_accessed=2**20, transcendentals=0),
         name="prepare",
     )(scalars, lows, order, pair, other, bins, after)
 
 
-def arrange_kernel(pick_ref, tally_ref, mine_ref, other_ref, out_ref):
+def arrange_kernel(pick_ref, mine_ref, other_ref, out_ref):
     window = jnp.concatenate([mine_ref[...], other_ref[...]], axis=0)
-    result = jnp.dot(pick_ref[...], window, preferred_element_type=F32)
-    out_ref[:, :LAGS] = result.astype(BF)
-    out_ref[:, LAGS:] = tally_ref[...]
-
-
-def arrange(pick, tally, mine, other):
+    out_ref[...] = jnp.dot(pick_ref[...], window, preferred_element_type=F32).astype(BF)
+
+
+def arrange(pick, mine, other):
     return pl.pallas_call(
         arrange_kernel,
         out_shape=jax.ShapeDtypeStruct((512, LAGS + 128), BF),
-        in_specs=vmem(4),
+        in_specs=vmem(3),
         out_specs=pl.BlockSpec(memory_space=pltpu.VMEM),
         compiler_params=pltpu.CompilerParams(vmem_limit_bytes=LIMIT),
         name="arrange",
-    )(pick, tally, mine, other)
+    )(pick, mine, other)
 
 
 def finish_kernel(parts_ref, out_ref):
@@ -407,25 +405,25 @@
     owner = jnp.logical_and(y == 2 * (src % 2), z == 2 * core + src // 2)
     scalars = jnp.stack([core, owner.astype(jnp.int32)])
 
-    up, across, along = plans()
+    first, side, along = plans()
     other_pair = lax.ppermute(pair_bin, "rcv", swap)
     filtered, w = prefilter(traces, band_group, filters, w)
     filtered, other_pair = lax.optimization_barrier((filtered, other_pair))
-    got = lax.ppermute(filtered, both, up[0])
+    got = lax.ppermute(filtered, both, first[0])
     partner = lax.ppermute(filtered, "rcv", swap)
     seed = jnp.where(core == 0, filtered, partner)
-    got = got + lax.ppermute(seed, both, up[1])
-    parts = [lax.ppermute(seed, both, across)]
-    bins, table, fc, flag = survey(scalars, pair_bin, other_pair, filtered, partner, w)
+    got = got + lax.ppermute(seed, both, first[1])
+    parts = [lax.ppermute(seed, both, side)]
+    bins, table, fc, flag, pieces = survey(scalars, pair_bin, other_pair, filtered, partner, w)
     held = jnp.where(flag[0:1] == 1, seed, got)
     parts = parts + [lax.ppermute(held, both, plan) for plan in along]
-    hot, pick, tally = prepare(
+    hot, pick = prepare(
         scalars, table, bin_order.reshape(8, 128), pair_bin, other_pair, bins, held
     )
 
-    window = correlate(table, held, parts, w, fc, bins, hot, back)
+    window = correlate(table, held, parts, w, fc, bins, hot, pieces, back)
     other_window = lax.ppermute(window, "rcv", swap)
-    payload = arrange(pick, tally, window, other_window)
+    payload = arrange(pick, window, other_window)
     groups = [[2 * i + c for i in range(64)] for c in range(2)]
     arrived = lax.all_to_all(payload, both, 0, 0, tiled=True, axis_index_groups=groups)
     return finish(arrived)

time: 54.9 us -> 53.6 us (0.976)
  Pallas kernels: 16 us -> 14.6 us
  starting transfers between devices: 13.5 us -> 12.2 us
  waiting for transfers between devices: 1.01 us -> 1.79 us
  blocking collectives: 23.8 us -> 24.4 us
    pallas_call x1, Pallas kernels: 4.02 us -> 2.04 us  [prepare(): pl.pallas_call(prepare_kernel, out_shape=[pltpu.VMEM((CH // GROUP, GROUP...]
    ppermute x1, starting transfers between devices: 1.78 us -> 0.09 us  [shards(): other_window = lax.ppermute(window, 'rcv', swap)]
    pallas_call x1, Pallas kernels: 1.81 us -> 2.62 us  [survey(): pl.pallas_call(survey_kernel, out_shape=[pltpu.VMEM((CH, 2 * CH), jnp.int...]
    all_to_all x1, blocking collectives: 23.8 us -> 24.4 us  [shards(): lax.all_to_all(payload, both, 0, 0, tiled=True, axis_index_groups=groups)]
  transfers between devices with their start and end apart: 9 -> 9, of which waited for: 1 -> 2; matrix products, arithmetic and copies ran while one was open for 0% -> 0% of each run, Pallas kernels for 15% -> 13%
where the time goes in v4:
time: 53.6 us; the launch traced here: 53.3 us
  blocking collectives  24.4 us (46%)
  Pallas kernels  14.6 us (27%)
  starting transfers between devices  12.2 us (23%)
  waiting for transfers between devices  1.79 us (3%)
    all_to_all x1, blocking collectives, shards(): lax.all_to_all(payload, both, 0, 0, tiled=True, axis_index_groups=groups)  24.4 us
    pallas_call x1, Pallas kernels, correlate(): pl.pallas_call(correlate_kernel, out_shape=jax.ShapeDtypeStruct((WIN, LAG...  6.68 us
    ppermute x1, starting transfers between devices, shards(): got = lax.ppermute(filtered, both, first[0])  5 us
    ppermute x3, starting transfers between devices, shards(): parts = parts + [lax.ppermute(held, both, plan) for plan in along]  2.64 us
    pallas_call x1, Pallas kernels, survey(): pl.pallas_call(survey_kernel, out_shape=[pltpu.VMEM((CH, 2 * CH), jnp.int...  2.62 us
    ppermute x1, starting transfers between devices, shards(): parts = [lax.ppermute(seed, both, side)]  2.59 us
    pallas_call x1, Pallas kernels, prefilter(): pl.pallas_call(prefilter_kernel, out_shape=[pltpu.VMEM((CH, SAMPLES), BF)...  2.14 us
    pallas_call x1, Pallas kernels, prepare(): pl.pallas_call(prepare_kernel, out_shape=[pltpu.VMEM((CH // GROUP, GROUP...  2.04 us
  transfers between devices with their start and end apart: 9, of which 2 were waited for; matrix products, arithmetic and copies ran while one was open for 0% of the time, Pallas kernels for 13%

profile of v4, /device:TPU:0, one launch (start us, length us, event | category | flops | bytes accessed | tf_op | source)
XLA Modules:
  0.0 53.3 jit_solution(1726390549716942735)
XLA Ops:
  0.0 0.0 collective-permute-start
  0.0 2.1 %prefilter.1 = (bf16[128,512]{1,0:T(8,128)(2,1)S(1)}, bf16[2,512,768]{2,1,0:T(8,128)(2,1)S(1)}) custom-call(bf16[128,512]{1,0:T(8,128)(2,1)} %traces_hbm.1, s32[1,128]{1,0:T(1,128)} %bitcast.9, f32[24,32]{1,0:T(8,128)} %filters_hbm.1, bf16[2,512,768]{2,1,0:T(8,128)(2,1)} %constant.70.clone.w_ref), custom_call_target="tpu_custom_call" | custom-call | tf_op jit(solution)/shard_map/prefilter/pallas_call | solution.py:128
  2.2 0.0 collective-permute-done.other_ref
  2.2 0.6 %collective-permute-start.1 = (bf16[128,512]{1,0:T(8,128)(2,1)S(1)}, bf16[128,512]{1,0:T(8,128)(2,1)S(1)}, u32[]{:S(2)}, u32[]{:S(2)}) collective-permute-start(bf16[128,512]{1,0:T(8,128)(2,1)S(1)} %get-tuple-element.18.mine_ref), channel_id=1, source_target_pairs={{0,1},{1,0},{2,3},{3,2},{4,5},{5,4},{6,7},{7,6},{8,9},{9,8},{10,11... | collective-permute-start | bytes 393224 | tf_op jit(solution)/shard_map/ppermute | solution.py:413
  2.7 0.0 copy-start
  2.8 0.0 copy-start.1
  2.8 0.1 pad_add_fusion.scalars
  2.8 5.0 %collective-permute-start.2 = (bf16[128,512]{1,0:T(8,128)(2,1)S(1)}, bf16[128,512]{1,0:T(8,128)(2,1)S(1)}, u32[]{:S(2)}, u32[]{:S(2)}) collective-permute-start(bf16[128,512]{1,0:T(8,128)(2,1)S(1)} %get-tuple-element.18.mine_ref), channel_id=1, source_target_pairs={{0,6},{16,9},{36,34},{52,45},{72,78},{88,81},{108,106},{124,117}} | collective-permute-start | bytes 393224 | tf_op jit(solution)/shard_map/ppermute | solution.py:412
  7.8 0.0 collective-permute-done.1.partner_ref
  7.9 1.3 %collective-permute-start.3 = (bf16[128,512]{1,0:T(8,128)(2,1)S(1)}, bf16[128,512]{1,0:T(8,128)(2,1)S(1)}, u32[]{:S(2)}, u32[]{:S(2)}) collective-permute-start(bf16[128,512]{1,0:T(8,128)(2,1)S(1)} %broadcast_select_fusion), channel_id=1, source_target_pairs={{0,4},{1,2},{16,1},{17,25},{36,32},{37,38},{52,37},{53,61},{72,76}... | collective-permute-start | bytes 393224 | tf_op jit(solution)/shard_map/ppermute | solution.py:415
  9.2 2.6 %collective-permute-start.4 = (bf16[128,512]{1,0:T(8,128)(2,1)S(1)}, bf16[128,512]{1,0:T(8,128)(2,1)S(1)}, u32[]{:S(2)}, u32[]{:S(2)}) collective-permute-start(bf16[128,512]{1,0:T(8,128)(2,1)S(1)} %broadcast_select_fusion), channel_id=1, source_target_pairs={{0,16},{1,8},{16,21},{17,19},{36,52},{37,44},{52,49},{53,55},{72,8... | collective-permute-start | bytes 393224 | tf_op jit(solution)/shard_map/ppermute | solution.py:416
  11.8 2.6 %survey.1 = (s32[128,256]{1,0:T(8,128)S(1)}, s32[16,128]{1,0:T(8,128)S(1)}, bf16[256,768]{1,0:T(8,128)(2,1)S(1)}, s32[8,512]{1,0:T(8,128)S(1)}, bf16[128,128]{1,0:T(8,128)(2,1)S(1)}) custom-call(s32[2]{0:T(128)S(1)} %pad_add_fusion.scalars, s32[2,128,128]{2,1,0:T(8,128)} %pair_ref.3, s32[2,128,128]{2,1,0:T(8,128)S(1)} %collective-permute-done.other_ref, ...), custom_call_target="tpu_custom_call" | custom-call | flops 402653184 | bytes 2097152 | tf_op jit(solution)/shard_map/survey/pallas_call | solution.py:294
  14.4 0.0 collective-permute-done.2
  14.4 0.0 collective-permute-done.3
  14.5 0.7 %collective-permute-start.5 = (bf16[128,512]{1,0:T(8,128)(2,1)S(1)}, bf16[128,512]{1,0:T(8,128)(2,1)S(1)}, u32[]{:S(2)}, u32[]{:S(2)}) collective-permute-start(bf16[128,512]{1,0:T(8,128)(2,1)S(1)} %add_select_fusion.after_ref.held_ref), channel_id=1, source_target_pairs={{2,18},{4,20},{6,22},{25,29},{1,5},{9,13},{38,54},{32,48},{34,50},... | collective-permute-start | bytes 393224 | tf_op jit(solution)/shard_map/ppermute | solution.py:419
  15.1 0.7 %collective-permute-start.6 = (bf16[128,512]{1,0:T(8,128)(2,1)S(1)}, bf16[128,512]{1,0:T(8,128)(2,1)S(1)}, u32[]{:S(2)}, u32[]{:S(2)}) collective-permute-start(bf16[128,512]{1,0:T(8,128)(2,1)S(1)} %add_select_fusion.after_ref.held_ref), channel_id=1, source_target_pairs={{2,10},{4,12},{6,14},{25,27},{1,3},{9,11},{38,46},{32,40},{34,42},... | collective-permute-start | bytes 393224 | tf_op jit(solution)/shard_map/ppermute | solution.py:419
  15.8 1.3 %collective-permute-start.7 = (bf16[128,512]{1,0:T(8,128)(2,1)S(1)}, bf16[128,512]{1,0:T(8,128)(2,1)S(1)}, u32[]{:S(2)}, u32[]{:S(2)}) collective-permute-start(bf16[128,512]{1,0:T(8,128)(2,1)S(1)} %add_select_fusion.after_ref.held_ref), channel_id=1, source_target_pairs={{0,24},{2,26},{4,28},{6,30},{17,23},{25,31},{1,7},{9,15},{36,60},{... | collective-permute-start | bytes 393224 | tf_op jit(solution)/shard_map/ppermute | solution.py:419
  17.1 0.0 copy-done
  17.1 0.0 copy-done.1
  17.1 0.0 copy-start.2
  17.2 2.0 %prepare.1 = (bf16[8,1152,256]{2,1,0:T(8,128)(2,1)S(1)}, bf16[512,256]{1,0:T(8,128)(2,1)S(1)}) custom-call(s32[2]{0:T(128)S(1)} %pad_add_fusion.scalars, s32[16,128]{1,0:T(8,128)S(1)} %get-tuple-element.20.low_ref, s32[8,128]{1,0:T(8,128)S(1)} %bitcast.8, s32[2,128,128]{2,1,0:T(8,128)S(1)} %copy-done, s32[2,128,128]{2,1,0:T(8,128)S(1)} %collective-permute-done.other_ref, ...), custom_call_target="tpu_custom_call" | custom-call | flops 1000000000 | bytes 1048576 | tf_op jit(solution)/shard_map/prepare/pallas_call | solution.py:349
  19.2 0.0 collective-permute-done.4.r0
  19.2 0.0 collective-permute-done.5.r1
  19.2 0.0 collective-permute-done.6.r2
  19.2 0.4 collective-permute-done.7.r3
  19.6 0.0 copy-done.2
  19.6 6.7 %correlate.1.mine_ref = bf16[128,640]{1,0:T(8,128)(2,1)S(1)} custom-call(s32[16,128]{1,0:T(8,128)S(1)} %get-tuple-element.20.low_ref, bf16[128,512]{1,0:T(8,128)(2,1)S(1)} %add_select_fusion.after_ref.held_ref, bf16[128,512]{1,0:T(8,128)(2,1)S(1)} %collective-permute-done.4.r0, bf16[128,512]{1,0:T(8,128)(2,1)S(1)} %collective-permute-done.5.r1, ...), custom_call_target="tpu_custom_call" | custom-call | flops 3623878656 | bytes 6291456 | tf_op jit(solution)/shard_map/correlate/pallas_call | solution.py:219
  26.3 0.1 collective-permute-start.8
  26.4 1.4 %collective-permute-done.8.other_ref = bf16[128,640]{1,0:T(8,128)(2,1)S(1)} collective-permute-done((bf16[128,640]{1,0:T(8,128)(2,1)S(1)}, bf16[128,640]{1,0:T(8,128)(2,1)S(1)}, u32[]{:S(2)}, u32[]{:S(2)}) %collective-permute-start.8) | collective-permute-done | bytes 163872 | tf_op jit(solution)/shard_map/ppermute | solution.py:425
  27.8 0.4 arrange.1
  28.2 24.4 %all_to_all.11 = bf16[64,8,640]{2,1,0:T(8,128)(2,1)S(1)} all-to-all(bf16[64,8,640]{2,1,0:T(8,128)(2,1)S(1)} %bitcast.6), channel_id=1, replica_groups={{0,2,4,6,8,10,12,14,16,18,20,22,24,26,28,30,32,34,36,38,40,42,44,46,48,..., dimensions={0} | all-to-all | bytes 1310720 | tf_op jit(solution)/shard_map/all_to_all | solution.py:428
  52.5 0.8 %finish.1 = f32[8,512]{1,0:T(8,128)} custom-call(bf16[512,640]{1,0:T(8,128)(2,1)S(1)} %bitcast.7), custom_call_target="tpu_custom_call" | custom-call | tf_op jit(solution)/shard_map/finish/pallas_call | solution.py:387
  (3 shorter events, 0.1 us)
Async XLA Ops:
  0.0 2.2 %collective-permute-start = (s32[2,128,128]{2,1,0:T(8,128)}, s32[2,128,128]{2,1,0:T(8,128)S(1)}, u32[]{:S(2)}, u32[]{:S(2)}) collective-permute-start(s32[2,128,128]{2,1,0:T(8,128)} %pair_ref.3), channel_id=1, source_target_pairs={{0,1},{1,0},{2,3},{3,2},{4,5},{5,4},{6,7},{7,6},{8,9},{9,8},{10,11... | collective-permute-start | bytes 393224 | tf_op jit(solution)/shard_map/ppermute | solution.py:409
  2.2 5.7 %collective-permute-start.1 = (bf16[128,512]{1,0:T(8,128)(2,1)S(1)}, bf16[128,512]{1,0:T(8,128)(2,1)S(1)}, u32[]{:S(2)}, u32[]{:S(2)}) collective-permute-start(bf16[128,512]{1,0:T(8,128)(2,1)S(1)} %get-tuple-element.18.mine_ref), channel_id=1, source_target_pairs={{0,1},{1,0},{2,3},{3,2},{4,5},{5,4},{6,7},{7,6},{8,9},{9,8},{10,11... | collective-permute-start | bytes 393224 | tf_op jit(solution)/shard_map/ppermute | solution.py:413
  2.7 14.4 %copy-start = (s32[2,128,128]{2,1,0:T(8,128)S(1)}, s32[2,128,128]{2,1,0:T(8,128)}, u32[]{:S(2)}) copy-start(s32[2,128,128]{2,1,0:T(8,128)} %pair_ref.3) | copy-start | bytes 393220
  2.8 14.4 %copy-start.1 = (s32[1024]{0:T(1024)S(1)}, s32[1024]{0:T(1024)}, u32[]{:S(2)}) copy-start(s32[1024]{0:T(1024)} %param.11) | copy-start | bytes 12292
  2.8 11.6 %collective-permute-start.2 = (bf16[128,512]{1,0:T(8,128)(2,1)S(1)}, bf16[128,512]{1,0:T(8,128)(2,1)S(1)}, u32[]{:S(2)}, u32[]{:S(2)}) collective-permute-start(bf16[128,512]{1,0:T(8,128)(2,1)S(1)} %get-tuple-element.18.mine_ref), channel_id=1, source_target_pairs={{0,6},{16,9},{36,34},{52,45},{72,78},{88,81},{108,106},{124,117}} | collective-permute-start | bytes 393224 | tf_op jit(solution)/shard_map/ppermute | solution.py:412
  7.9 6.6 %collective-permute-start.3 = (bf16[128,512]{1,0:T(8,128)(2,1)S(1)}, bf16[128,512]{1,0:T(8,128)(2,1)S(1)}, u32[]{:S(2)}, u32[]{:S(2)}) collective-permute-start(bf16[128,512]{1,0:T(8,128)(2,1)S(1)} %broadcast_select_fusion), channel_id=1, source_target_pairs={{0,4},{1,2},{16,1},{17,25},{36,32},{37,38},{52,37},{53,61},{72,76}... | collective-permute-start | bytes 393224 | tf_op jit(solution)/shard_map/ppermute | solution.py:415
  9.2 10.0 %collective-permute-start.4 = (bf16[128,512]{1,0:T(8,128)(2,1)S(1)}, bf16[128,512]{1,0:T(8,128)(2,1)S(1)}, u32[]{:S(2)}, u32[]{:S(2)}) collective-permute-start(bf16[128,512]{1,0:T(8,128)(2,1)S(1)} %broadcast_select_fusion), channel_id=1, source_target_pairs={{0,16},{1,8},{16,21},{17,19},{36,52},{37,44},{52,49},{53,55},{72,8... | collective-permute-start | bytes 393224 | tf_op jit(solution)/shard_map/ppermute | solution.py:416
  14.5 4.7 %collective-permute-start.5 = (bf16[128,512]{1,0:T(8,128)(2,1)S(1)}, bf16[128,512]{1,0:T(8,128)(2,1)S(1)}, u32[]{:S(2)}, u32[]{:S(2)}) collective-permute-start(bf16[128,512]{1,0:T(8,128)(2,1)S(1)} %add_select_fusion.after_ref.held_ref), channel_id=1, source_target_pairs={{2,18},{4,20},{6,22},{25,29},{1,5},{9,13},{38,54},{32,48},{34,50},... | collective-permute-start | bytes 393224 | tf_op jit(solution)/shard_map/ppermute | solution.py:419
  15.1 4.1 %collective-permute-start.6 = (bf16[128,512]{1,0:T(8,128)(2,1)S(1)}, bf16[128,512]{1,0:T(8,128)(2,1)S(1)}, u32[]{:S(2)}, u32[]{:S(2)}) collective-permute-start(bf16[128,512]{1,0:T(8,128)(2,1)S(1)} %add_select_fusion.after_ref.held_ref), channel_id=1, source_target_pairs={{2,10},{4,12},{6,14},{25,27},{1,3},{9,11},{38,46},{32,40},{34,42},... | collective-permute-start | bytes 393224 | tf_op jit(solution)/shard_map/ppermute | solution.py:419
  15.8 3.8 %collective-permute-start.7 = (bf16[128,512]{1,0:T(8,128)(2,1)S(1)}, bf16[128,512]{1,0:T(8,128)(2,1)S(1)}, u32[]{:S(2)}, u32[]{:S(2)}) collective-permute-start(bf16[128,512]{1,0:T(8,128)(2,1)S(1)} %add_select_fusion.after_ref.held_ref), channel_id=1, source_target_pairs={{0,24},{2,26},{4,28},{6,30},{17,23},{25,31},{1,7},{9,15},{36,60},{... | collective-permute-start | bytes 393224 | tf_op jit(solution)/shard_map/ppermute | solution.py:419
  17.1 2.5 %copy-start.2 = (bf16[2,768,512]{2,1,0:T(8,128)(2,1)S(1)}, bf16[2,768,512]{2,1,0:T(8,128)(2,1)}, u32[]{:S(2)}) copy-start(bf16[2,768,512]{2,1,0:T(8,128)(2,1)} %constant.71.clone.back_ref) | copy-start | bytes 4718596
  26.3 1.5 %collective-permute-start.8 = (bf16[128,640]{1,0:T(8,128)(2,1)S(1)}, bf16[128,640]{1,0:T(8,128)(2,1)S(1)}, u32[]{:S(2)}, u32[]{:S(2)}) collective-permute-start(bf16[128,640]{1,0:T(8,128)(2,1)S(1)} %correlate.1.mine_ref), channel_id=1, source_target_pairs={{0,1},{1,0},{2,3},{3,2},{4,5},{5,4},{6,7},{7,6},{8,9},{9,8},{10,11... | collective-permute-start | bytes 491528 | tf_op jit(solution)/shard_map/ppermute | solution.py:425

commit v5 on v4

--- a/solution.py
+++ b/solution.py
@@ -185,7 +185,7 @@
                 gather(g, j, SPAN, spread(hot_ref[g], j))
             return carry
 
-        lax.fori_loop(0, n_groups, body, 0, unroll=2)
+        lax.fori_loop(0, n_groups, body, 0, unroll=4)
 
     @pl.when(jnp.logical_not(fits))
     def _():

time: 53.6 us -> 53.5 us (level)
  no operation moved by 1% of the time
where the time goes in v5:
time: 53.5 us; the launch traced here: 53.2 us
  blocking collectives  24.4 us (46%)
  Pallas kernels  14.5 us (27%)
  starting transfers between devices  12.2 us (23%)
  waiting for transfers between devices  1.79 us (3%)
    all_to_all x1, blocking collectives, shards(): lax.all_to_all(payload, both, 0, 0, tiled=True, axis_index_groups=groups)  24.4 us
    pallas_call x1, Pallas kernels, correlate(): pl.pallas_call(correlate_kernel, out_shape=jax.ShapeDtypeStruct((WIN, LAG...  6.54 us
    ppermute x1, starting transfers between devices, shards(): got = lax.ppermute(filtered, both, first[0])  5 us
    ppermute x3, starting transfers between devices, shards(): parts = parts + [lax.ppermute(held, both, plan) for plan in along]  2.64 us
    pallas_call x1, Pallas kernels, survey(): pl.pallas_call(survey_kernel, out_shape=[pltpu.VMEM((CH, 2 * CH), jnp.int...  2.62 us
    ppermute x1, starting transfers between devices, shards(): parts = [lax.ppermute(seed, both, side)]  2.59 us
    pallas_call x1, Pallas kernels, prefilter(): pl.pallas_call(prefilter_kernel, out_shape=[pltpu.VMEM((CH, SAMPLES), BF)...  2.14 us
    pallas_call x1, Pallas kernels, prepare(): pl.pallas_call(prepare_kernel, out_shape=[pltpu.VMEM((CH // GROUP, GROUP...  2.04 us
  transfers between devices with their start and end apart: 9, of which 2 were waited for; matrix products, arithmetic and copies ran while one was open for 0% of the time, Pallas kernels for 13%

profile of v5, /device:TPU:0, one launch (start us, length us, event | category | flops | bytes accessed | tf_op | source)
XLA Modules:
  0.0 53.2 jit_solution(17238415418512961752)
XLA Ops:
  0.0 0.0 collective-permute-start
  0.0 2.1 %prefilter.1 = (bf16[128,512]{1,0:T(8,128)(2,1)S(1)}, bf16[2,512,768]{2,1,0:T(8,128)(2,1)S(1)}) custom-call(bf16[128,512]{1,0:T(8,128)(2,1)} %traces_hbm.1, s32[1,128]{1,0:T(1,128)} %bitcast.9, f32[24,32]{1,0:T(8,128)} %filters_hbm.1, bf16[2,512,768]{2,1,0:T(8,128)(2,1)} %constant.70.clone.w_ref), custom_call_target="tpu_custom_call" | custom-call | tf_op jit(solution)/shard_map/prefilter/pallas_call | solution.py:128
  2.2 0.0 collective-permute-done.other_ref
  2.2 0.6 %collective-permute-start.1 = (bf16[128,512]{1,0:T(8,128)(2,1)S(1)}, bf16[128,512]{1,0:T(8,128)(2,1)S(1)}, u32[]{:S(2)}, u32[]{:S(2)}) collective-permute-start(bf16[128,512]{1,0:T(8,128)(2,1)S(1)} %get-tuple-element.18.mine_ref), channel_id=1, source_target_pairs={{0,1},{1,0},{2,3},{3,2},{4,5},{5,4},{6,7},{7,6},{8,9},{9,8},{10,11... | collective-permute-start | bytes 393224 | tf_op jit(solution)/shard_map/ppermute | solution.py:413
  2.7 0.0 copy-start
  2.8 0.0 copy-start.1
  2.8 0.1 pad_add_fusion.scalars
  2.8 5.0 %collective-permute-start.2 = (bf16[128,512]{1,0:T(8,128)(2,1)S(1)}, bf16[128,512]{1,0:T(8,128)(2,1)S(1)}, u32[]{:S(2)}, u32[]{:S(2)}) collective-permute-start(bf16[128,512]{1,0:T(8,128)(2,1)S(1)} %get-tuple-element.18.mine_ref), channel_id=1, source_target_pairs={{0,6},{16,9},{36,34},{52,45},{72,78},{88,81},{108,106},{124,117}} | collective-permute-start | bytes 393224 | tf_op jit(solution)/shard_map/ppermute | solution.py:412
  7.8 0.0 collective-permute-done.1.partner_ref
  7.9 1.3 %collective-permute-start.3 = (bf16[128,512]{1,0:T(8,128)(2,1)S(1)}, bf16[128,512]{1,0:T(8,128)(2,1)S(1)}, u32[]{:S(2)}, u32[]{:S(2)}) collective-permute-start(bf16[128,512]{1,0:T(8,128)(2,1)S(1)} %broadcast_select_fusion), channel_id=1, source_target_pairs={{0,4},{1,2},{16,1},{17,25},{36,32},{37,38},{52,37},{53,61},{72,76}... | collective-permute-start | bytes 393224 | tf_op jit(solution)/shard_map/ppermute | solution.py:415
  9.2 2.6 %collective-permute-start.4 = (bf16[128,512]{1,0:T(8,128)(2,1)S(1)}, bf16[128,512]{1,0:T(8,128)(2,1)S(1)}, u32[]{:S(2)}, u32[]{:S(2)}) collective-permute-start(bf16[128,512]{1,0:T(8,128)(2,1)S(1)} %broadcast_select_fusion), channel_id=1, source_target_pairs={{0,16},{1,8},{16,21},{17,19},{36,52},{37,44},{52,49},{53,55},{72,8... | collective-permute-start | bytes 393224 | tf_op jit(solution)/shard_map/ppermute | solution.py:416
  11.8 2.6 %survey.1 = (s32[128,256]{1,0:T(8,128)S(1)}, s32[16,128]{1,0:T(8,128)S(1)}, bf16[256,768]{1,0:T(8,128)(2,1)S(1)}, s32[8,512]{1,0:T(8,128)S(1)}, bf16[128,128]{1,0:T(8,128)(2,1)S(1)}) custom-call(s32[2]{0:T(128)S(1)} %pad_add_fusion.scalars, s32[2,128,128]{2,1,0:T(8,128)} %pair_ref.3, s32[2,128,128]{2,1,0:T(8,128)S(1)} %collective-permute-done.other_ref, ...), custom_call_target="tpu_custom_call" | custom-call | flops 402653184 | bytes 2097152 | tf_op jit(solution)/shard_map/survey/pallas_call | solution.py:294
  14.4 0.0 collective-permute-done.2
  14.4 0.0 collective-permute-done.3
  14.5 0.7 %collective-permute-start.5 = (bf16[128,512]{1,0:T(8,128)(2,1)S(1)}, bf16[128,512]{1,0:T(8,128)(2,1)S(1)}, u32[]{:S(2)}, u32[]{:S(2)}) collective-permute-start(bf16[128,512]{1,0:T(8,128)(2,1)S(1)} %add_select_fusion.after_ref.held_ref), channel_id=1, source_target_pairs={{2,18},{4,20},{6,22},{25,29},{1,5},{9,13},{38,54},{32,48},{34,50},... | collective-permute-start | bytes 393224 | tf_op jit(solution)/shard_map/ppermute | solution.py:419
  15.1 0.7 %collective-permute-start.6 = (bf16[128,512]{1,0:T(8,128)(2,1)S(1)}, bf16[128,512]{1,0:T(8,128)(2,1)S(1)}, u32[]{:S(2)}, u32[]{:S(2)}) collective-permute-start(bf16[128,512]{1,0:T(8,128)(2,1)S(1)} %add_select_fusion.after_ref.held_ref), channel_id=1, source_target_pairs={{2,10},{4,12},{6,14},{25,27},{1,3},{9,11},{38,46},{32,40},{34,42},... | collective-permute-start | bytes 393224 | tf_op jit(solution)/shard_map/ppermute | solution.py:419
  15.8 1.3 %collective-permute-start.7 = (bf16[128,512]{1,0:T(8,128)(2,1)S(1)}, bf16[128,512]{1,0:T(8,128)(2,1)S(1)}, u32[]{:S(2)}, u32[]{:S(2)}) collective-permute-start(bf16[128,512]{1,0:T(8,128)(2,1)S(1)} %add_select_fusion.after_ref.held_ref), channel_id=1, source_target_pairs={{0,24},{2,26},{4,28},{6,30},{17,23},{25,31},{1,7},{9,15},{36,60},{... | collective-permute-start | bytes 393224 | tf_op jit(solution)/shard_map/ppermute | solution.py:419
  17.1 0.0 copy-done
  17.1 0.0 copy-done.1
  17.1 0.0 copy-start.2
  17.2 2.0 %prepare.1 = (bf16[8,1152,256]{2,1,0:T(8,128)(2,1)S(1)}, bf16[512,256]{1,0:T(8,128)(2,1)S(1)}) custom-call(s32[2]{0:T(128)S(1)} %pad_add_fusion.scalars, s32[16,128]{1,0:T(8,128)S(1)} %get-tuple-element.20.low_ref, s32[8,128]{1,0:T(8,128)S(1)} %bitcast.8, s32[2,128,128]{2,1,0:T(8,128)S(1)} %copy-done, s32[2,128,128]{2,1,0:T(8,128)S(1)} %collective-permute-done.other_ref, ...), custom_call_target="tpu_custom_call" | custom-call | flops 1000000000 | bytes 1048576 | tf_op jit(solution)/shard_map/prepare/pallas_call | solution.py:349
  19.2 0.0 collective-permute-done.4.r0
  19.2 0.0 collective-permute-done.5.r1
  19.2 0.0 collective-permute-done.6.r2
  19.2 0.4 collective-permute-done.7.r3
  19.6 0.0 copy-done.2
  19.6 6.5 %correlate.1.mine_ref = bf16[128,640]{1,0:T(8,128)(2,1)S(1)} custom-call(s32[16,128]{1,0:T(8,128)S(1)} %get-tuple-element.20.low_ref, bf16[128,512]{1,0:T(8,128)(2,1)S(1)} %add_select_fusion.after_ref.held_ref, bf16[128,512]{1,0:T(8,128)(2,1)S(1)} %collective-permute-done.4.r0, bf16[128,512]{1,0:T(8,128)(2,1)S(1)} %collective-permute-done.5.r1, ...), custom_call_target="tpu_custom_call" | custom-call | flops 3623878656 | bytes 6291456 | tf_op jit(solution)/shard_map/correlate/pallas_call | solution.py:219
  26.2 0.1 collective-permute-start.8
  26.3 1.4 %collective-permute-done.8.other_ref = bf16[128,640]{1,0:T(8,128)(2,1)S(1)} collective-permute-done((bf16[128,640]{1,0:T(8,128)(2,1)S(1)}, bf16[128,640]{1,0:T(8,128)(2,1)S(1)}, u32[]{:S(2)}, u32[]{:S(2)}) %collective-permute-start.8) | collective-permute-done | bytes 163872 | tf_op jit(solution)/shard_map/ppermute | solution.py:425
  27.7 0.4 arrange.1
  28.0 24.4 %all_to_all.11 = bf16[64,8,640]{2,1,0:T(8,128)(2,1)S(1)} all-to-all(bf16[64,8,640]{2,1,0:T(8,128)(2,1)S(1)} %bitcast.6), channel_id=1, replica_groups={{0,2,4,6,8,10,12,14,16,18,20,22,24,26,28,30,32,34,36,38,40,42,44,46,48,..., dimensions={0} | all-to-all | bytes 1310720 | tf_op jit(solution)/shard_map/all_to_all | solution.py:428
  52.4 0.8 %finish.1 = f32[8,512]{1,0:T(8,128)} custom-call(bf16[512,640]{1,0:T(8,128)(2,1)S(1)} %bitcast.7), custom_call_target="tpu_custom_call" | custom-call | tf_op jit(solution)/shard_map/finish/pallas_call | solution.py:387
  (3 shorter events, 0.1 us)
Async XLA Ops:
  0.0 2.2 %collective-permute-start = (s32[2,128,128]{2,1,0:T(8,128)}, s32[2,128,128]{2,1,0:T(8,128)S(1)}, u32[]{:S(2)}, u32[]{:S(2)}) collective-permute-start(s32[2,128,128]{2,1,0:T(8,128)} %pair_ref.3), channel_id=1, source_target_pairs={{0,1},{1,0},{2,3},{3,2},{4,5},{5,4},{6,7},{7,6},{8,9},{9,8},{10,11... | collective-permute-start | bytes 393224 | tf_op jit(solution)/shard_map/ppermute | solution.py:409
  2.2 5.7 %collective-permute-start.1 = (bf16[128,512]{1,0:T(8,128)(2,1)S(1)}, bf16[128,512]{1,0:T(8,128)(2,1)S(1)}, u32[]{:S(2)}, u32[]{:S(2)}) collective-permute-start(bf16[128,512]{1,0:T(8,128)(2,1)S(1)} %get-tuple-element.18.mine_ref), channel_id=1, source_target_pairs={{0,1},{1,0},{2,3},{3,2},{4,5},{5,4},{6,7},{7,6},{8,9},{9,8},{10,11... | collective-permute-start | bytes 393224 | tf_op jit(solution)/shard_map/ppermute | solution.py:413
  2.7 14.4 %copy-start = (s32[2,128,128]{2,1,0:T(8,128)S(1)}, s32[2,128,128]{2,1,0:T(8,128)}, u32[]{:S(2)}) copy-start(s32[2,128,128]{2,1,0:T(8,128)} %pair_ref.3) | copy-start | bytes 393220
  2.8 14.4 %copy-start.1 = (s32[1024]{0:T(1024)S(1)}, s32[1024]{0:T(1024)}, u32[]{:S(2)}) copy-start(s32[1024]{0:T(1024)} %param.11) | copy-start | bytes 12292
  2.8 11.6 %collective-permute-start.2 = (bf16[128,512]{1,0:T(8,128)(2,1)S(1)}, bf16[128,512]{1,0:T(8,128)(2,1)S(1)}, u32[]{:S(2)}, u32[]{:S(2)}) collective-permute-start(bf16[128,512]{1,0:T(8,128)(2,1)S(1)} %get-tuple-element.18.mine_ref), channel_id=1, source_target_pairs={{0,6},{16,9},{36,34},{52,45},{72,78},{88,81},{108,106},{124,117}} | collective-permute-start | bytes 393224 | tf_op jit(solution)/shard_map/ppermute | solution.py:412
  7.9 6.6 %collective-permute-start.3 = (bf16[128,512]{1,0:T(8,128)(2,1)S(1)}, bf16[128,512]{1,0:T(8,128)(2,1)S(1)}, u32[]{:S(2)}, u32[]{:S(2)}) collective-permute-start(bf16[128,512]{1,0:T(8,128)(2,1)S(1)} %broadcast_select_fusion), channel_id=1, source_target_pairs={{0,4},{1,2},{16,1},{17,25},{36,32},{37,38},{52,37},{53,61},{72,76}... | collective-permute-start | bytes 393224 | tf_op jit(solution)/shard_map/ppermute | solution.py:415
  9.2 10.0 %collective-permute-start.4 = (bf16[128,512]{1,0:T(8,128)(2,1)S(1)}, bf16[128,512]{1,0:T(8,128)(2,1)S(1)}, u32[]{:S(2)}, u32[]{:S(2)}) collective-permute-start(bf16[128,512]{1,0:T(8,128)(2,1)S(1)} %broadcast_select_fusion), channel_id=1, source_target_pairs={{0,16},{1,8},{16,21},{17,19},{36,52},{37,44},{52,49},{53,55},{72,8... | collective-permute-start | bytes 393224 | tf_op jit(solution)/shard_map/ppermute | solution.py:416
  14.5 4.7 %collective-permute-start.5 = (bf16[128,512]{1,0:T(8,128)(2,1)S(1)}, bf16[128,512]{1,0:T(8,128)(2,1)S(1)}, u32[]{:S(2)}, u32[]{:S(2)}) collective-permute-start(bf16[128,512]{1,0:T(8,128)(2,1)S(1)} %add_select_fusion.after_ref.held_ref), channel_id=1, source_target_pairs={{2,18},{4,20},{6,22},{25,29},{1,5},{9,13},{38,54},{32,48},{34,50},... | collective-permute-start | bytes 393224 | tf_op jit(solution)/shard_map/ppermute | solution.py:419
  15.1 4.1 %collective-permute-start.6 = (bf16[128,512]{1,0:T(8,128)(2,1)S(1)}, bf16[128,512]{1,0:T(8,128)(2,1)S(1)}, u32[]{:S(2)}, u32[]{:S(2)}) collective-permute-start(bf16[128,512]{1,0:T(8,128)(2,1)S(1)} %add_select_fusion.after_ref.held_ref), channel_id=1, source_target_pairs={{2,10},{4,12},{6,14},{25,27},{1,3},{9,11},{38,46},{32,40},{34,42},... | collective-permute-start | bytes 393224 | tf_op jit(solution)/shard_map/ppermute | solution.py:419
  15.8 3.8 %collective-permute-start.7 = (bf16[128,512]{1,0:T(8,128)(2,1)S(1)}, bf16[128,512]{1,0:T(8,128)(2,1)S(1)}, u32[]{:S(2)}, u32[]{:S(2)}) collective-permute-start(bf16[128,512]{1,0:T(8,128)(2,1)S(1)} %add_select_fusion.after_ref.held_ref), channel_id=1, source_target_pairs={{0,24},{2,26},{4,28},{6,30},{17,23},{25,31},{1,7},{9,15},{36,60},{... | collective-permute-start | bytes 393224 | tf_op jit(solution)/shard_map/ppermute | solution.py:419
  17.1 2.5 %copy-start.2 = (bf16[2,768,512]{2,1,0:T(8,128)(2,1)S(1)}, bf16[2,768,512]{2,1,0:T(8,128)(2,1)}, u32[]{:S(2)}) copy-start(bf16[2,768,512]{2,1,0:T(8,128)(2,1)} %constant.71.clone.back_ref) | copy-start | bytes 4718596
  26.2 1.5 %collective-permute-start.8 = (bf16[128,640]{1,0:T(8,128)(2,1)S(1)}, bf16[128,640]{1,0:T(8,128)(2,1)S(1)}, u32[]{:S(2)}, u32[]{:S(2)}) collective-permute-start(bf16[128,640]{1,0:T(8,128)(2,1)S(1)} %correlate.1.mine_ref), channel_id=1, source_target_pairs={{0,1},{1,0},{2,3},{3,2},{4,5},{5,4},{6,7},{7,6},{8,9},{9,8},{10,11... | collective-permute-start | bytes 491528 | tf_op jit(solution)/shard_map/ppermute | solution.py:425

commit v6 on v5

--- a/solution.py
+++ b/solution.py
@@ -65,7 +65,7 @@
         first[1].append((chip(0, 0, 1), chip(1, 0, k)))
         side.append((chip(0, 0, 0), chip(0, 2, k)))
         side.append((chip(0, 0, 1), chip(0, 1, k)))
-        for plan, d in zip(along, (2, 1, 3)):
+        for plan, d in zip(along, (2, 1, 3) if k == 0 else (2, 3, 1)):
             plan.extend((chip(i, 0, k), chip(i, d, k)) for i in range(0 if d == 3 else 1, RING))
     return first, side, along
 

time: 53.5 us -> 53.5 us (level)
  no operation moved by 1% of the time
where the time goes in v6:
time: 53.5 us; the launch traced here: 53.2 us
  blocking collectives  24.4 us (46%)
  Pallas kernels  14.5 us (27%)
  starting transfers between devices  12.2 us (23%)
  waiting for transfers between devices  1.79 us (3%)
    all_to_all x1, blocking collectives, shards(): lax.all_to_all(payload, both, 0, 0, tiled=True, axis_index_groups=groups)  24.4 us
    pallas_call x1, Pallas kernels, correlate(): pl.pallas_call(correlate_kernel, out_shape=jax.ShapeDtypeStruct((WIN, LAG...  6.54 us
    ppermute x1, starting transfers between devices, shards(): got = lax.ppermute(filtered, both, first[0])  5 us
    ppermute x3, starting transfers between devices, shards(): parts = parts + [lax.ppermute(held, both, plan) for plan in along]  2.64 us
    pallas_call x1, Pallas kernels, survey(): pl.pallas_call(survey_kernel, out_shape=[pltpu.VMEM((CH, 2 * CH), jnp.int...  2.62 us
    ppermute x1, starting transfers between devices, shards(): parts = [lax.ppermute(seed, both, side)]  2.59 us
    pallas_call x1, Pallas kernels, prefilter(): pl.pallas_call(prefilter_kernel, out_shape=[pltpu.VMEM((CH, SAMPLES), BF)...  2.14 us
    pallas_call x1, Pallas kernels, prepare(): pl.pallas_call(prepare_kernel, out_shape=[pltpu.VMEM((CH // GROUP, GROUP...  2.04 us
  transfers between devices with their start and end apart: 9, of which 2 were waited for; matrix products, arithmetic and copies ran while one was open for 0% of the time, Pallas kernels for 13%

profile of v6, /device:TPU:0, one launch (start us, length us, event | category | flops | bytes accessed | tf_op | source)
XLA Modules:
  0.0 53.2 jit_solution(10018549500643333906)
XLA Ops:
  0.0 0.0 collective-permute-start
  0.0 2.1 %prefilter.1 = (bf16[128,512]{1,0:T(8,128)(2,1)S(1)}, bf16[2,512,768]{2,1,0:T(8,128)(2,1)S(1)}) custom-call(bf16[128,512]{1,0:T(8,128)(2,1)} %traces_hbm.1, s32[1,128]{1,0:T(1,128)} %bitcast.9, f32[24,32]{1,0:T(8,128)} %filters_hbm.1, bf16[2,512,768]{2,1,0:T(8,128)(2,1)} %constant.70.clone.w_ref), custom_call_target="tpu_custom_call" | custom-call | tf_op jit(solution)/shard_map/prefilter/pallas_call | solution.py:128
  2.2 0.0 collective-permute-done.other_ref
  2.2 0.6 %collective-permute-start.1 = (bf16[128,512]{1,0:T(8,128)(2,1)S(1)}, bf16[128,512]{1,0:T(8,128)(2,1)S(1)}, u32[]{:S(2)}, u32[]{:S(2)}) collective-permute-start(bf16[128,512]{1,0:T(8,128)(2,1)S(1)} %get-tuple-element.18.mine_ref), channel_id=1, source_target_pairs={{0,1},{1,0},{2,3},{3,2},{4,5},{5,4},{6,7},{7,6},{8,9},{9,8},{10,11... | collective-permute-start | bytes 393224 | tf_op jit(solution)/shard_map/ppermute | solution.py:413
  2.7 0.0 copy-start
  2.8 0.0 copy-start.1
  2.8 0.1 pad_add_fusion.scalars
  2.8 5.0 %collective-permute-start.2 = (bf16[128,512]{1,0:T(8,128)(2,1)S(1)}, bf16[128,512]{1,0:T(8,128)(2,1)S(1)}, u32[]{:S(2)}, u32[]{:S(2)}) collective-permute-start(bf16[128,512]{1,0:T(8,128)(2,1)S(1)} %get-tuple-element.18.mine_ref), channel_id=1, source_target_pairs={{0,6},{16,9},{36,34},{52,45},{72,78},{88,81},{108,106},{124,117}} | collective-permute-start | bytes 393224 | tf_op jit(solution)/shard_map/ppermute | solution.py:412
  7.8 0.0 collective-permute-done.1.partner_ref
  7.9 1.3 %collective-permute-start.3 = (bf16[128,512]{1,0:T(8,128)(2,1)S(1)}, bf16[128,512]{1,0:T(8,128)(2,1)S(1)}, u32[]{:S(2)}, u32[]{:S(2)}) collective-permute-start(bf16[128,512]{1,0:T(8,128)(2,1)S(1)} %broadcast_select_fusion), channel_id=1, source_target_pairs={{0,4},{1,2},{16,1},{17,25},{36,32},{37,38},{52,37},{53,61},{72,76}... | collective-permute-start | bytes 393224 | tf_op jit(solution)/shard_map/ppermute | solution.py:415
  9.2 2.6 %collective-permute-start.4 = (bf16[128,512]{1,0:T(8,128)(2,1)S(1)}, bf16[128,512]{1,0:T(8,128)(2,1)S(1)}, u32[]{:S(2)}, u32[]{:S(2)}) collective-permute-start(bf16[128,512]{1,0:T(8,128)(2,1)S(1)} %broadcast_select_fusion), channel_id=1, source_target_pairs={{0,16},{1,8},{16,21},{17,19},{36,52},{37,44},{52,49},{53,55},{72,8... | collective-permute-start | bytes 393224 | tf_op jit(solution)/shard_map/ppermute | solution.py:416
  11.8 2.6 %survey.1 = (s32[128,256]{1,0:T(8,128)S(1)}, s32[16,128]{1,0:T(8,128)S(1)}, bf16[256,768]{1,0:T(8,128)(2,1)S(1)}, s32[8,512]{1,0:T(8,128)S(1)}, bf16[128,128]{1,0:T(8,128)(2,1)S(1)}) custom-call(s32[2]{0:T(128)S(1)} %pad_add_fusion.scalars, s32[2,128,128]{2,1,0:T(8,128)} %pair_ref.3, s32[2,128,128]{2,1,0:T(8,128)S(1)} %collective-permute-done.other_ref, ...), custom_call_target="tpu_custom_call" | custom-call | flops 402653184 | bytes 2097152 | tf_op jit(solution)/shard_map/survey/pallas_call | solution.py:294
  14.4 0.0 collective-permute-done.2
  14.4 0.0 collective-permute-done.3
  14.5 0.7 %collective-permute-start.5 = (bf16[128,512]{1,0:T(8,128)(2,1)S(1)}, bf16[128,512]{1,0:T(8,128)(2,1)S(1)}, u32[]{:S(2)}, u32[]{:S(2)}) collective-permute-start(bf16[128,512]{1,0:T(8,128)(2,1)S(1)} %add_select_fusion.after_ref.held_ref), channel_id=1, source_target_pairs={{2,18},{4,20},{6,22},{25,29},{1,5},{9,13},{38,54},{32,48},{34,50},... | collective-permute-start | bytes 393224 | tf_op jit(solution)/shard_map/ppermute | solution.py:419
  15.1 0.7 %collective-permute-start.6 = (bf16[128,512]{1,0:T(8,128)(2,1)S(1)}, bf16[128,512]{1,0:T(8,128)(2,1)S(1)}, u32[]{:S(2)}, u32[]{:S(2)}) collective-permute-start(bf16[128,512]{1,0:T(8,128)(2,1)S(1)} %add_select_fusion.after_ref.held_ref), channel_id=1, source_target_pairs={{2,10},{4,12},{6,14},{17,23},{25,31},{1,7},{9,15},{38,46},{32,40},... | collective-permute-start | bytes 393224 | tf_op jit(solution)/shard_map/ppermute | solution.py:419
  15.8 1.3 %collective-permute-start.7 = (bf16[128,512]{1,0:T(8,128)(2,1)S(1)}, bf16[128,512]{1,0:T(8,128)(2,1)S(1)}, u32[]{:S(2)}, u32[]{:S(2)}) collective-permute-start(bf16[128,512]{1,0:T(8,128)(2,1)S(1)} %add_select_fusion.after_ref.held_ref), channel_id=1, source_target_pairs={{0,24},{2,26},{4,28},{6,30},{25,27},{1,3},{9,11},{36,60},{38,62},{... | collective-permute-start | bytes 393224 | tf_op jit(solution)/shard_map/ppermute | solution.py:419
  17.1 0.0 copy-done
  17.1 0.0 copy-done.1
  17.1 0.0 copy-start.2
  17.2 2.0 %prepare.1 = (bf16[8,1152,256]{2,1,0:T(8,128)(2,1)S(1)}, bf16[512,256]{1,0:T(8,128)(2,1)S(1)}) custom-call(s32[2]{0:T(128)S(1)} %pad_add_fusion.scalars, s32[16,128]{1,0:T(8,128)S(1)} %get-tuple-element.20.low_ref, s32[8,128]{1,0:T(8,128)S(1)} %bitcast.8, s32[2,128,128]{2,1,0:T(8,128)S(1)} %copy-done, s32[2,128,128]{2,1,0:T(8,128)S(1)} %collective-permute-done.other_ref, ...), custom_call_target="tpu_custom_call" | custom-call | flops 1000000000 | bytes 1048576 | tf_op jit(solution)/shard_map/prepare/pallas_call | solution.py:349
  19.2 0.0 collective-permute-done.4.r0
  19.2 0.0 collective-permute-done.5.r1
  19.2 0.0 collective-permute-done.6.r2
  19.2 0.4 collective-permute-done.7.r3
  19.6 0.0 copy-done.2
  19.6 6.5 %correlate.1.mine_ref = bf16[128,640]{1,0:T(8,128)(2,1)S(1)} custom-call(s32[16,128]{1,0:T(8,128)S(1)} %get-tuple-element.20.low_ref, bf16[128,512]{1,0:T(8,128)(2,1)S(1)} %add_select_fusion.after_ref.held_ref, bf16[128,512]{1,0:T(8,128)(2,1)S(1)} %collective-permute-done.4.r0, bf16[128,512]{1,0:T(8,128)(2,1)S(1)} %collective-permute-done.5.r1, ...), custom_call_target="tpu_custom_call" | custom-call | flops 3623878656 | bytes 6291456 | tf_op jit(solution)/shard_map/correlate/pallas_call | solution.py:219
  26.2 0.1 collective-permute-start.8
  26.3 1.4 %collective-permute-done.8.other_ref = bf16[128,640]{1,0:T(8,128)(2,1)S(1)} collective-permute-done((bf16[128,640]{1,0:T(8,128)(2,1)S(1)}, bf16[128,640]{1,0:T(8,128)(2,1)S(1)}, u32[]{:S(2)}, u32[]{:S(2)}) %collective-permute-start.8) | collective-permute-done | bytes 163872 | tf_op jit(solution)/shard_map/ppermute | solution.py:425
  27.7 0.4 arrange.1
  28.0 24.4 %all_to_all.11 = bf16[64,8,640]{2,1,0:T(8,128)(2,1)S(1)} all-to-all(bf16[64,8,640]{2,1,0:T(8,128)(2,1)S(1)} %bitcast.6), channel_id=1, replica_groups={{0,2,4,6,8,10,12,14,16,18,20,22,24,26,28,30,32,34,36,38,40,42,44,46,48,..., dimensions={0} | all-to-all | bytes 1310720 | tf_op jit(solution)/shard_map/all_to_all | solution.py:428
  52.4 0.8 %finish.1 = f32[8,512]{1,0:T(8,128)} custom-call(bf16[512,640]{1,0:T(8,128)(2,1)S(1)} %bitcast.7), custom_call_target="tpu_custom_call" | custom-call | tf_op jit(solution)/shard_map/finish/pallas_call | solution.py:387
  (3 shorter events, 0.1 us)
Async XLA Ops:
  0.0 2.2 %collective-permute-start = (s32[2,128,128]{2,1,0:T(8,128)}, s32[2,128,128]{2,1,0:T(8,128)S(1)}, u32[]{:S(2)}, u32[]{:S(2)}) collective-permute-start(s32[2,128,128]{2,1,0:T(8,128)} %pair_ref.3), channel_id=1, source_target_pairs={{0,1},{1,0},{2,3},{3,2},{4,5},{5,4},{6,7},{7,6},{8,9},{9,8},{10,11... | collective-permute-start | bytes 393224 | tf_op jit(solution)/shard_map/ppermute | solution.py:409
  2.2 5.7 %collective-permute-start.1 = (bf16[128,512]{1,0:T(8,128)(2,1)S(1)}, bf16[128,512]{1,0:T(8,128)(2,1)S(1)}, u32[]{:S(2)}, u32[]{:S(2)}) collective-permute-start(bf16[128,512]{1,0:T(8,128)(2,1)S(1)} %get-tuple-element.18.mine_ref), channel_id=1, source_target_pairs={{0,1},{1,0},{2,3},{3,2},{4,5},{5,4},{6,7},{7,6},{8,9},{9,8},{10,11... | collective-permute-start | bytes 393224 | tf_op jit(solution)/shard_map/ppermute | solution.py:413
  2.7 14.4 %copy-start = (s32[2,128,128]{2,1,0:T(8,128)S(1)}, s32[2,128,128]{2,1,0:T(8,128)}, u32[]{:S(2)}) copy-start(s32[2,128,128]{2,1,0:T(8,128)} %pair_ref.3) | copy-start | bytes 393220
  2.8 14.4 %copy-start.1 = (s32[1024]{0:T(1024)S(1)}, s32[1024]{0:T(1024)}, u32[]{:S(2)}) copy-start(s32[1024]{0:T(1024)} %param.11) | copy-start | bytes 12292
  2.8 11.6 %collective-permute-start.2 = (bf16[128,512]{1,0:T(8,128)(2,1)S(1)}, bf16[128,512]{1,0:T(8,128)(2,1)S(1)}, u32[]{:S(2)}, u32[]{:S(2)}) collective-permute-start(bf16[128,512]{1,0:T(8,128)(2,1)S(1)} %get-tuple-element.18.mine_ref), channel_id=1, source_target_pairs={{0,6},{16,9},{36,34},{52,45},{72,78},{88,81},{108,106},{124,117}} | collective-permute-start | bytes 393224 | tf_op jit(solution)/shard_map/ppermute | solution.py:412
  7.9 6.6 %collective-permute-start.3 = (bf16[128,512]{1,0:T(8,128)(2,1)S(1)}, bf16[128,512]{1,0:T(8,128)(2,1)S(1)}, u32[]{:S(2)}, u32[]{:S(2)}) collective-permute-start(bf16[128,512]{1,0:T(8,128)(2,1)S(1)} %broadcast_select_fusion), channel_id=1, source_target_pairs={{0,4},{1,2},{16,1},{17,25},{36,32},{37,38},{52,37},{53,61},{72,76}... | collective-permute-start | bytes 393224 | tf_op jit(solution)/shard_map/ppermute | solution.py:415
  9.2 10.0 %collective-permute-start.4 = (bf16[128,512]{1,0:T(8,128)(2,1)S(1)}, bf16[128,512]{1,0:T(8,128)(2,1)S(1)}, u32[]{:S(2)}, u32[]{:S(2)}) collective-permute-start(bf16[128,512]{1,0:T(8,128)(2,1)S(1)} %broadcast_select_fusion), channel_id=1, source_target_pairs={{0,16},{1,8},{16,21},{17,19},{36,52},{37,44},{52,49},{53,55},{72,8... | collective-permute-start | bytes 393224 | tf_op jit(solution)/shard_map/ppermute | solution.py:416
  14.5 4.7 %collective-permute-start.5 = (bf16[128,512]{1,0:T(8,128)(2,1)S(1)}, bf16[128,512]{1,0:T(8,128)(2,1)S(1)}, u32[]{:S(2)}, u32[]{:S(2)}) collective-permute-start(bf16[128,512]{1,0:T(8,128)(2,1)S(1)} %add_select_fusion.after_ref.held_ref), channel_id=1, source_target_pairs={{2,18},{4,20},{6,22},{25,29},{1,5},{9,13},{38,54},{32,48},{34,50},... | collective-permute-start | bytes 393224 | tf_op jit(solution)/shard_map/ppermute | solution.py:419
  15.1 4.1 %collective-permute-start.6 = (bf16[128,512]{1,0:T(8,128)(2,1)S(1)}, bf16[128,512]{1,0:T(8,128)(2,1)S(1)}, u32[]{:S(2)}, u32[]{:S(2)}) collective-permute-start(bf16[128,512]{1,0:T(8,128)(2,1)S(1)} %add_select_fusion.after_ref.held_ref), channel_id=1, source_target_pairs={{2,10},{4,12},{6,14},{17,23},{25,31},{1,7},{9,15},{38,46},{32,40},... | collective-permute-start | bytes 393224 | tf_op jit(solution)/shard_map/ppermute | solution.py:419
  15.8 3.8 %collective-permute-start.7 = (bf16[128,512]{1,0:T(8,128)(2,1)S(1)}, bf16[128,512]{1,0:T(8,128)(2,1)S(1)}, u32[]{:S(2)}, u32[]{:S(2)}) collective-permute-start(bf16[128,512]{1,0:T(8,128)(2,1)S(1)} %add_select_fusion.after_ref.held_ref), channel_id=1, source_target_pairs={{0,24},{2,26},{4,28},{6,30},{25,27},{1,3},{9,11},{36,60},{38,62},{... | collective-permute-start | bytes 393224 | tf_op jit(solution)/shard_map/ppermute | solution.py:419
  17.1 2.5 %copy-start.2 = (bf16[2,768,512]{2,1,0:T(8,128)(2,1)S(1)}, bf16[2,768,512]{2,1,0:T(8,128)(2,1)}, u32[]{:S(2)}) copy-start(bf16[2,768,512]{2,1,0:T(8,128)(2,1)} %constant.71.clone.back_ref) | copy-start | bytes 4718596
  26.2 1.5 %collective-permute-start.8 = (bf16[128,640]{1,0:T(8,128)(2,1)S(1)}, bf16[128,640]{1,0:T(8,128)(2,1)S(1)}, u32[]{:S(2)}, u32[]{:S(2)}) collective-permute-start(bf16[128,640]{1,0:T(8,128)(2,1)S(1)} %correlate.1.mine_ref), channel_id=1, source_target_pairs={{0,1},{1,0},{2,3},{3,2},{4,5},{5,4},{6,7},{7,6},{8,9},{9,8},{10,11... | collective-permute-start | bytes 491528 | tf_op jit(solution)/shard_map/ppermute | solution.py:425
